TPU v7x, 256 devices: a whole 4x4x8 slice. The times are simulated.
256 devices in a mesh: res: 32 (over y, x, z_hi), frame: 8 (over z_lo, core).
Axes of the slice: x: 4, y: 4, z: 8 (z_hi: 2, z_lo: 4; z = z_hi * 4 + z_lo), core: 2. Of those that a mesh axis runs over, the one named last changes fastest.
Arguments:
- activations: bfloat16 [16, 4096, 768], P('frame', 'res'), may hold values from -6 to 6
- contacts: int32 [32, 5], replicated, may hold values from 0 to 1, as said below
- frame_index: int32 [16], replicated, may hold values from 0 to 45, as said below
- spatial_qkv: bfloat16 [768, 2304], replicated, may hold values from -8 to 8
- spatial_out: bfloat16 [768, 768], replicated, may hold values from -0.21875 to 0.21875
- time_qkv: bfloat16 [768, 2304], replicated, may hold values from -8 to 8
- time_out: bfloat16 [768, 768], replicated, may hold values from -0.21875 to 0.21875
Outputs:
- layer_out: bfloat16 [16, 4096, 768], P('frame', 'res')
Inputs may be any that keep to these rules, and one draw needn't show every extreme that they name: contacts[b, 2] = 1 for every block; contacts are symmetric, contacts[b, 2 + d] = contacts[b + d, 2 - d]; flags that name a block outside 0 to 31 are 0. Strictly increasing, frame_index[0] = 0, frame_index[15] = 45.
All inputs are finite; a program needn't handle non-finite values.
Results may differ from a plain program's by a relative error of at most 0.025.
Values may be sent and summed in bfloat16 or wider, within the bound.
No kernel may reach another device: no remote copies, remote signals or barrier semaphores. Data moves between devices by JAX's collectives and lax.ppermute only.
A program may use at most 128 MiB of HBM per device.

v0:
```python
import jax
import jax.numpy as jnp
from jax import lax
from jax.sharding import PartitionSpec as P

HEAD = 64
HALO = 2


def shifted(block, axis, distance):
    devices = range(lax.axis_size(axis))
    route = [(i - distance, i) for i in devices if i - distance in devices]
    return lax.ppermute(block, axis, route)


def normalize(values_in):
    widened = values_in.astype(jnp.float32)
    mean_square = jnp.mean(widened * widened, axis=-1, keepdims=True)
    return (widened * lax.rsqrt(mean_square + 1e-06)).astype(jnp.bfloat16)


def rotate(entries, positions):
    half_size = HEAD // 2
    frequency = 10000.0 ** (-jnp.arange(half_size, dtype=jnp.float32) / half_size)
    angles = positions.astype(jnp.float32)[:, None] * frequency[None, :]
    cosine = jnp.cos(angles)[:, None, None, :]
    sine = jnp.sin(angles)[:, None, None, :]
    first = entries[..., :half_size]
    second = entries[..., half_size:]
    return jnp.concatenate(
        [first * cosine - second * sine, first * sine + second * cosine], axis=-1
    )


def softmax_weights(scores):
    top = jnp.max(scores, axis=-1, keepdims=True)
    expo = jnp.exp(scores - top)
    return (expo / jnp.sum(expo, axis=-1, keepdims=True)).astype(jnp.bfloat16)


def time_attend(query, keys, values):
    score_scale = HEAD ** (-0.5)
    scores = (
        jnp.einsum("frhd,grhd->rhfg", query, keys, preferred_element_type=jnp.float32) * score_scale
    )
    weights = softmax_weights(scores)
    return jnp.einsum(
        "rhfg,grhd->frhd", weights, values, preferred_element_type=jnp.float32
    ).astype(jnp.bfloat16)


def tile_scores(query, keys):
    return jnp.einsum(
        "frhd,fshd->fhrs", query, keys, preferred_element_type=jnp.float32
    ) * HEAD ** (-0.5)


def tile_values(weights, values):
    return jnp.einsum("fhrs,fshd->frhd", weights, values, preferred_element_type=jnp.float32)


def shards(activations, contacts, frame_index, spatial_qkv, spatial_out, time_qkv, time_out):
    frames_dev, block_rows, model_width = activations.shape
    head_count = model_width // HEAD
    flat = activations.reshape(frames_dev * block_rows, model_width)
    normed = normalize(flat)
    projected = jnp.dot(normed, spatial_qkv, preferred_element_type=jnp.float32).astype(
        jnp.bfloat16
    )
    projected = projected.reshape(frames_dev, block_rows, 3, head_count, HEAD)
    query = projected[:, :, 0]
    keys = projected[:, :, 1]
    values = projected[:, :, 2]
    contact_row = lax.dynamic_slice_in_dim(contacts, lax.axis_index("res"), 1, 0)[0]
    tile_list = []
    for offset in range(-HALO, HALO + 1):
        if offset == 0:
            tile_list.append((keys, values))
        else:
            tile_list.append(shifted((keys, values), "res", -offset))
    score_list = []
    for column in range(2 * HALO + 1):
        near_keys = tile_list[column][0]
        if column == HALO:
            score_list.append(tile_scores(query, near_keys))
        else:
            score_list.append(
                jnp.where(contact_row[column] > 0, tile_scores(query, near_keys), -1e30)
            )
    weights = softmax_weights(jnp.concatenate(score_list, axis=-1))
    value_shape = (frames_dev, block_rows, head_count, HEAD)
    spatial_sum = jnp.zeros(value_shape, jnp.float32)
    for column in range(2 * HALO + 1):
        part_weights = weights[..., column * block_rows : (column + 1) * block_rows]
        near_values = tile_list[column][1]
        spatial_sum = spatial_sum + tile_values(part_weights, near_values)
    spatial_mix = spatial_sum.astype(jnp.bfloat16).reshape(frames_dev * block_rows, model_width)
    hidden = (
        flat.astype(jnp.float32)
        + jnp.dot(spatial_mix, spatial_out, preferred_element_type=jnp.float32)
    ).astype(jnp.bfloat16)
    renormed = normalize(hidden)
    time_projected = jnp.dot(renormed, time_qkv, preferred_element_type=jnp.float32).astype(
        jnp.bfloat16
    )
    time_projected = time_projected.reshape(frames_dev, block_rows, 3, head_count, HEAD)
    first_frame = lax.axis_index("frame") * frames_dev
    positions = lax.dynamic_slice_in_dim(frame_index, first_frame, frames_dev, 0)
    time_query = rotate(time_projected[:, :, 0].astype(jnp.float32), positions).astype(jnp.bfloat16)
    time_keys = rotate(time_projected[:, :, 1].astype(jnp.float32), positions).astype(jnp.bfloat16)
    time_values = time_projected[:, :, 2]
    all_keys, all_values = (
        lax.all_gather(time_keys, "frame", axis=0, tiled=True),
        lax.all_gather(time_values, "frame", axis=0, tiled=True),
    )
    time_mix = time_attend(time_query, all_keys, all_values)
    time_mix = time_mix.reshape(frames_dev * block_rows, model_width)
    layer_out = hidden.astype(jnp.float32) + jnp.dot(
        time_mix, time_out, preferred_element_type=jnp.float32
    )
    return layer_out.astype(jnp.bfloat16).reshape(frames_dev, block_rows, model_width)


def solution(mesh):
    placed = (P("frame", "res", None), P(), P(), P(), P(), P(), P())
    return jax.shard_map(
        shards, mesh=mesh, in_specs=placed, out_specs=P("frame", "res", None), check_vma=False
    )
```

profile of v0, /device:TPU:1, one launch (start us, length us, event | category | flops | bytes accessed | tf_op | source)
XLA Modules:
  0.0 235.5 jit_solution(11103141464811378505)
XLA Ops:
  6.5 1.3 multiply_reduce_fusion.1
  7.9 1.1 fusion.30
  9.0 2.1 convolution_convert_fusion.1
  11.1 1.6 copy.34
  12.7 0.3 reshape.131
  13.1 1.5 fusion.44
  14.5 0.1 copy.96
  14.6 4.7 %collective-permute-start.1 = (bf16[2,128,12,64]{1,3,2,0:T(8,128)(2,1)S(1)}, bf16[2,128,12,64]{1,3,2,0:T(8,128)(2,1)}, u32[]{:S(2)}, u32[]{:S(2)}) collective-permute-start(bf16[2,128,12,64]{1,3,2,0:T(8,128)(2,1)S(1)} %bitcast.92), channel_id=1, source_target_pairs={{0,16},{8,24},{16,32},{24,40},{32,48},{40,56},{48,64},{56,72},{64,... | collective-permute-start | bytes 1179656 | tf_op jit(solution)/shard_map/ppermute | solution.py:13
  19.3 9.5 %collective-permute-start.2 = (bf16[2,128,12,64]{1,3,2,0:T(8,128)(2,1)S(1)}, bf16[2,128,12,64]{1,3,2,0:T(8,128)(2,1)}, u32[]{:S(2)}, u32[]{:S(2)}) collective-permute-start(bf16[2,128,12,64]{1,3,2,0:T(8,128)(2,1)S(1)} %bitcast.93), channel_id=1, source_target_pairs={{0,8},{8,16},{16,24},{24,32},{32,40},{40,48},{48,56},{56,64},{64,7... | collective-permute-start | bytes 1179656 | tf_op jit(solution)/shard_map/ppermute | solution.py:13
  28.9 1.3 collective-permute-start.3
  30.2 1.3 collective-permute-start.4
  31.5 0.8 copy.97
  32.3 7.9 %collective-permute-start.5 = (bf16[2,128,12,64]{1,3,2,0:T(8,128)(2,1)}, bf16[2,128,12,64]{1,3,2,0:T(8,128)(2,1)S(1)}, u32[]{:S(2)}, u32[]{:S(2)}) collective-permute-start(bf16[2,128,12,64]{1,3,2,0:T(8,128)(2,1)} %bitcast.89), channel_id=1, source_target_pairs={{0,8},{8,16},{16,24},{24,32},{32,40},{40,48},{48,56},{56,64},{64,7... | collective-permute-start | bytes 1179656 | tf_op jit(solution)/shard_map/ppermute | solution.py:13
  40.3 0.1 constant_dynamic-slice_fusion
  40.3 0.1 dynamic-slice_convert_fusion
  40.4 0.1 multiply_cosine_fusion
  40.5 0.6 fusion.45
  43.6 4.0 %collective-permute-start = (bf16[2,128,12,64]{1,3,2,0:T(8,128)(2,1)}, bf16[2,128,12,64]{1,3,2,0:T(8,128)(2,1)S(1)}, u32[]{:S(2)}, u32[]{:S(2)}) collective-permute-start(bf16[2,128,12,64]{1,3,2,0:T(8,128)(2,1)} %bitcast.89), channel_id=1, source_target_pairs={{0,16},{8,24},{16,32},{24,40},{32,48},{40,56},{48,64},{56,72},{64,... | collective-permute-start | bytes 1179656 | tf_op jit(solution)/shard_map/ppermute | solution.py:13
  47.6 1.5 fusion.39
  49.1 1.3 collective-permute-start.7
  50.4 1.5 fusion.38
  51.8 0.4 fusion.40
  52.3 0.6 collective-permute-done.3
  52.9 1.3 collective-permute-start.6
  54.2 0.5 fusion.41
  54.6 0.5 fusion.42
  55.1 1.1 fusion.1
  56.2 1.4 divide_convert_fusion
  57.6 0.3 fusion.22
  57.9 0.3 fusion.24
  58.3 1.2 collective-permute-done.7
  59.4 0.3 fusion.19
  59.8 0.3 fusion.13
  60.1 0.0 copy-start.2
  60.1 0.0 copy-start.8
  60.2 19.0 %collective-permute-done.6 = bf16[2,128,12,64]{1,3,2,0:T(8,128)(2,1)S(1)} collective-permute-done((bf16[2,128,12,64]{1,3,2,0:T(8,128)(2,1)}, bf16[2,128,12,64]{1,3,2,0:T(8,128)(2,1)S(1)}, u32[]{:S(2)}, u32[]{:S(2)}) %collective-permute-start.6) | collective-permute-done | bytes 393248 | tf_op jit(solution)/shard_map/ppermute | solution.py:13
  79.2 0.3 fusion.18
  79.5 0.0 copy-start.7
  79.5 0.4 copy.43
  80.0 0.6 multiply_reduce_fusion
  80.6 0.9 copy-done.5
  81.5 0.0 copy-done.7
  81.5 1.1 convolution_convert_fusion
  82.7 0.8 copy.44
  83.5 0.3 reshape.133
  83.8 1.5 fusion.43
  85.3 1.9 copy.60
  87.2 1.9 copy.61
  89.0 2.4 %bitcast_convert_fusion = (f32[2,128,12,64]{3,0,2,1:T(2,128)S(1)}, f32[2,128,12,64]{3,0,2,1:T(2,128)S(1)}) fusion(bf16[2,128,1,12,64]{4,0,3,1,2:T(2,128)(2,1)} %copy.61, bf16[2,128,1,12,64]{4,0,3,1,2:T(2,128)(2,1)} %copy.60), kind=kLoop, calls=%fused_computation.46 | loop fusion | flops 393216 | bytes 2359296 | tf_op jit(solution)/shard_map/convert_element_type | solution.py:110
  91.5 5.0 %subtract_convert_fusion.1 = (bf16[2,128,12,32]{3,0,2,1:T(2,128)(2,1)}, bf16[2,128,12,32]{3,0,2,1:T(2,128)(2,1)}, bf16[2,128,12,32]{3,0,2,1:T(2,128)(2,1)S(1)}, bf16[2,128,12,32]{3,0,2,1:T(2,128)(2,1)S(1)}) fusion(f32[2,128,12,64]{3,0,2,1:T(2,128)S(1)} %get-tuple-element.38, f32[2,32]{1,0:T(2,128)S(1)} %get-tuple-element.32, ...), kind=kLoop, calls=%fused_computation.12 | loop fusion | flops 1572864 | bytes 2359808 | tf_op jit(solution)/shard_map/convert.5
  96.5 2.1 pad_maximum_fusion
  98.6 1.7 copy.49
  100.3 0.0 all-gather.4.cloned.1.call-update
  100.4 0.0 all-gather.6.cloned.1.call-start
  100.4 0.8 copy.45
  101.2 0.0 all-gather.6.cloned.1.call-update
  101.3 60.5 %all-gather.4.cloned.1.call-done = bf16[16,128,12,64]{1,3,2,0:T(8,128)(2,1)} async-done(((bf16[2,128,12,64]{1,3,2,0:T(8,128)(2,1)}), bf16[16,128,12,64]{1,3,2,0:T(8,128)(2,1)}) %all-gather.4.cloned.1.call-update) | async-done | bytes 3145744 | tf_op jit(solution)/shard_map/all_gather | solution.py:113
  161.7 10.3 %copy.50 = bf16[16,128,12,64]{3,0,2,1:T(8,128)(2,1)} copy(bf16[16,128,12,64]{1,3,2,0:T(8,128)(2,1)} %all-gather.4.cloned.1.call-done) | data formatting | bytes 6291456 | tf_op jit(solution)/shard_map/all_gather | solution.py:113
  172.0 8.7 %fusion.46 = (f32[128,12,2]{2,1,0:T(8,128)}, f32[128,12,2,16]{3,2,1,0:T(2,128)S(1)}) fusion(bf16[16,128,12,64]{3,0,2,1:T(8,128)(2,1)} %copy.50, bf16[2,128,12,32]{3,0,2,1:T(2,128)(2,1)S(1)} %copy-done.4, bf16[2,128,12,32]{3,0,2,1:T(2,128)(2,1)S(1)} %copy-done.3), kind=kOutput, calls=%fused_computation.84 | convolution fusion | flops 7225359 | bytes 3747840 | tf_op jit(solution)/shard_map/sub | solution.py:37
  180.7 26.6 %all-gather.6.cloned.1.call-done = bf16[16,128,1,12,64]{1,4,3,2,0:T(8,128)(2,1)} async-done(((bf16[2,128,1,12,64]{1,4,3,2,0:T(8,128)(2,1)}), bf16[16,128,1,12,64]{1,4,3,2,0:T(8,128)(2,1)}) %all-gather.6.cloned.1.call-update) | async-done | bytes 3145744 | tf_op jit(solution)/shard_map/all_gather | solution.py:114
  207.3 10.3 %copy.46 = bf16[16,128,1,12,64]{4,0,3,1,2:T(8,128)(2,1)} copy(bf16[16,128,1,12,64]{1,4,3,2,0:T(8,128)(2,1)} %all-gather.6.cloned.1.call-done) | data formatting | bytes 6291456 | tf_op jit(solution)/shard_map/all_gather | solution.py:114
  217.5 5.1 %fusion.9 = bf16[2,128,12,64]{3,0,2,1:T(2,128)(2,1)} fusion(bf16[16,128,1,12,64]{4,0,3,1,2:T(8,128)(2,1)} %copy.46, f32[128,12,2,16]{3,2,1,0:T(2,128)S(1)} %get-tuple-element.36, f32[128,12,2]{2,1,0:T(8,128)S(1)} %copy-done.10), kind=kOutput, calls=%fused_computation.22 | convolution fusion | flops 6586368 | bytes 3747840 | tf_op jit(solution)/shard_map/rhfg,grhd->frhd/dot_general | solution.py:47
  222.6 3.2 %copy.51 = bf16[2,128,12,64]{1,0,3,2:T(2,128)(2,1)} copy(bf16[2,128,12,64]{3,0,2,1:T(2,128)(2,1)} %fusion.9) | data formatting | bytes 786432 | tf_op jit(solution)/shard_map/convert_element_type | solution.py:49
  225.8 2.9 %fusion.16 = bf16[256,768]{1,0:T(8,128)(2,1)} fusion(f32[256,768]{1,0:T(8,128)} %copy-done.5, bf16[768,768]{1,0:T(8,128)(2,1)} %param.13, bf16[96,8,2,128]{3,2,1,0:T(2,128)(2,1)} %bitcast.91), kind=kOutput, calls=%fused_computation.31 | convolution fusion | flops 302383104 | bytes 2752512 | tf_op jit(solution)/shard_map/dot_general | solution.py:118
  (27 shorter events, 0.1 us)
Async XLA Ops:
  6.5 2.5 %copy-start = (bf16[768,2304]{1,0:T(8,128)(2,1)S(1)}, bf16[768,2304]{1,0:T(8,128)(2,1)}, u32[]{:S(2)}) copy-start(bf16[768,2304]{1,0:T(8,128)(2,1)} %param.10) | copy-start | bytes 10616836
  6.5 155.2 %all-gather.4.cloned.1.call-start = ((), (), s32[]{:S(2)}) async-start(), calls=%async_computation | async-start | bytes 3538944 | tf_op jit(solution)/shard_map/all_gather | solution.py:113
  13.0 27.2 %copy-start.6 = (s32[32,5]{0,1:T(8,128)S(1)}, s32[32,5]{0,1:T(8,128)}, u32[]{:S(2)}) copy-start(s32[32,5]{0,1:T(8,128)} %param.8) | copy-start | bytes 1924
  13.0 27.3 %copy-start.9 = (s32[16]{0:T(128)S(1)}, s32[16]{0:T(128)}, u32[]{:S(2)}) copy-start(s32[16]{0:T(128)} %param.9) | copy-start | bytes 196
  14.6 29.0 %collective-permute-start.1 = (bf16[2,128,12,64]{1,3,2,0:T(8,128)(2,1)S(1)}, bf16[2,128,12,64]{1,3,2,0:T(8,128)(2,1)}, u32[]{:S(2)}, u32[]{:S(2)}) collective-permute-start(bf16[2,128,12,64]{1,3,2,0:T(8,128)(2,1)S(1)} %bitcast.92), channel_id=1, source_target_pairs={{0,16},{8,24},{16,32},{24,40},{32,48},{40,56},{48,64},{56,72},{64,... | collective-permute-start | bytes 1179656 | tf_op jit(solution)/shard_map/ppermute | solution.py:13
  19.3 29.7 %collective-permute-start.2 = (bf16[2,128,12,64]{1,3,2,0:T(8,128)(2,1)S(1)}, bf16[2,128,12,64]{1,3,2,0:T(8,128)(2,1)}, u32[]{:S(2)}, u32[]{:S(2)}) collective-permute-start(bf16[2,128,12,64]{1,3,2,0:T(8,128)(2,1)S(1)} %bitcast.93), channel_id=1, source_target_pairs={{0,8},{8,16},{16,24},{24,32},{32,40},{40,48},{48,56},{56,64},{64,7... | collective-permute-start | bytes 1179656 | tf_op jit(solution)/shard_map/ppermute | solution.py:13
  28.9 24.0 %collective-permute-start.3 = (bf16[2,128,12,64]{1,3,2,0:T(8,128)(2,1)S(1)}, bf16[2,128,12,64]{1,3,2,0:T(8,128)(2,1)S(1)}, u32[]{:S(2)}, u32[]{:S(2)}) collective-permute-start(bf16[2,128,12,64]{1,3,2,0:T(8,128)(2,1)S(1)} %bitcast.94), channel_id=1, source_target_pairs={{8,0},{16,8},{24,16},{32,24},{40,32},{48,40},{56,48},{64,56},{72,6... | collective-permute-start | bytes 1179656 | tf_op jit(solution)/shard_map/ppermute | solution.py:13
  30.2 24.4 %collective-permute-start.4 = (bf16[2,128,12,64]{1,3,2,0:T(8,128)(2,1)S(1)}, bf16[2,128,12,64]{1,3,2,0:T(8,128)(2,1)S(1)}, u32[]{:S(2)}, u32[]{:S(2)}) collective-permute-start(bf16[2,128,12,64]{1,3,2,0:T(8,128)(2,1)S(1)} %bitcast.95), channel_id=1, source_target_pairs={{16,0},{24,8},{32,16},{40,24},{48,32},{56,40},{64,48},{72,56},{80,... | collective-permute-start | bytes 1179656 | tf_op jit(solution)/shard_map/ppermute | solution.py:13
  32.3 25.6 %collective-permute-start.5 = (bf16[2,128,12,64]{1,3,2,0:T(8,128)(2,1)}, bf16[2,128,12,64]{1,3,2,0:T(8,128)(2,1)S(1)}, u32[]{:S(2)}, u32[]{:S(2)}) collective-permute-start(bf16[2,128,12,64]{1,3,2,0:T(8,128)(2,1)} %bitcast.89), channel_id=1, source_target_pairs={{0,8},{8,16},{16,24},{24,32},{32,40},{40,48},{48,56},{56,64},{64,7... | collective-permute-start | bytes 1179656 | tf_op jit(solution)/shard_map/ppermute | solution.py:13
  43.6 16.2 %collective-permute-start = (bf16[2,128,12,64]{1,3,2,0:T(8,128)(2,1)}, bf16[2,128,12,64]{1,3,2,0:T(8,128)(2,1)S(1)}, u32[]{:S(2)}, u32[]{:S(2)}) collective-permute-start(bf16[2,128,12,64]{1,3,2,0:T(8,128)(2,1)} %bitcast.89), channel_id=1, source_target_pairs={{0,16},{8,24},{16,32},{24,40},{32,48},{40,56},{48,64},{56,72},{64,... | collective-permute-start | bytes 1179656 | tf_op jit(solution)/shard_map/ppermute | solution.py:13
  49.1 10.4 %collective-permute-start.7 = (bf16[2,128,12,64]{1,3,2,0:T(8,128)(2,1)}, bf16[2,128,12,64]{1,3,2,0:T(8,128)(2,1)S(1)}, u32[]{:S(2)}, u32[]{:S(2)}) collective-permute-start(bf16[2,128,12,64]{1,3,2,0:T(8,128)(2,1)} %bitcast.89), channel_id=1, source_target_pairs={{16,0},{24,8},{32,16},{40,24},{48,32},{56,40},{64,48},{72,56},{80,... | collective-permute-start | bytes 1179656 | tf_op jit(solution)/shard_map/ppermute | solution.py:13
  52.9 26.3 %collective-permute-start.6 = (bf16[2,128,12,64]{1,3,2,0:T(8,128)(2,1)}, bf16[2,128,12,64]{1,3,2,0:T(8,128)(2,1)S(1)}, u32[]{:S(2)}, u32[]{:S(2)}) collective-permute-start(bf16[2,128,12,64]{1,3,2,0:T(8,128)(2,1)} %bitcast.89), channel_id=1, source_target_pairs={{8,0},{16,8},{24,16},{32,24},{40,32},{48,40},{56,48},{64,56},{72,6... | collective-permute-start | bytes 1179656 | tf_op jit(solution)/shard_map/ppermute | solution.py:13
  60.1 19.8 %copy-start.2 = (bf16[2,128,768]{2,1,0:T(8,128)(2,1)S(1)}, bf16[2,128,768]{2,1,0:T(8,128)(2,1)}, u32[]{:S(2)}) copy-start(bf16[2,128,768]{2,1,0:T(8,128)(2,1)} %param.7) | copy-start | bytes 1179652
  60.1 19.8 %copy-start.8 = (bf16[768,768]{1,0:T(8,128)(2,1)S(1)}, bf16[768,768]{1,0:T(8,128)(2,1)}, u32[]{:S(2)}) copy-start(bf16[768,768]{1,0:T(8,128)(2,1)} %param.11) | copy-start | bytes 3538948
  79.5 2.0 copy-start.7
  80.5 0.9 copy-start.5
  100.4 106.9 %all-gather.6.cloned.1.call-start = ((), (), s32[]{:S(2)}) async-start(), calls=%async_computation.1 | async-start | bytes 3538944 | tf_op jit(solution)/shard_map/all_gather | solution.py:114
  101.3 70.7 %copy-start.3 = (bf16[2,128,12,32]{3,0,2,1:T(2,128)(2,1)S(1)}, bf16[2,128,12,32]{3,0,2,1:T(2,128)(2,1)}, u32[]{:S(2)}) copy-start(bf16[2,128,12,32]{3,0,2,1:T(2,128)(2,1)} %get-tuple-element.5) | copy-start | bytes 589828
  101.3 70.7 %copy-start.4 = (bf16[2,128,12,32]{3,0,2,1:T(2,128)(2,1)S(1)}, bf16[2,128,12,32]{3,0,2,1:T(2,128)(2,1)}, u32[]{:S(2)}) copy-start(bf16[2,128,12,32]{3,0,2,1:T(2,128)(2,1)} %get-tuple-element.6) | copy-start | bytes 589828
  180.7 36.8 %copy-start.10 = (f32[128,12,2]{2,1,0:T(8,128)S(1)}, f32[128,12,2]{2,1,0:T(8,128)}, u32[]{:S(2)}) copy-start(f32[128,12,2]{2,1,0:T(8,128)} %get-tuple-element.35) | copy-start | bytes 36868
  222.6 6.1 %copy-start.1 = (bf16[768,2304]{1,0:T(8,128)(2,1)S(1)}, bf16[768,2304]{1,0:T(8,128)(2,1)}, u32[]{:S(2)}) copy-start(bf16[768,2304]{1,0:T(8,128)(2,1)} %param.10) | copy-start | bytes 10616836
Sparse Core Ops, SparseCore 0:
  100.5 61.2 all-gather.3
  163.5 43.6 all-gather.5
where the time goes:
time: 238 us; the launch traced here: 236 us
  waiting for transfers between devices  108 us (45%)
  local copies, waits for them, and re-layouts  39 us (16%)
  starting transfers between devices  31.3 us (13%)
  matrix products  26.5 us (11%)
  between operations  16.3 us (7%)
  other arithmetic  14.7 us (6%)
    all_gather x1, waiting for transfers between devices, shards(): lax.all_gather(time_keys, 'frame', axis=0, tiled=True)  60.5 us
    ppermute x8, starting transfers between devices, shifted(): return lax.ppermute(block, axis, route)  31.3 us
    all_gather x1, waiting for transfers between devices, shards(): lax.all_gather(time_values, 'frame', axis=0, tiled=True)  26.6 us
    ppermute x8, waiting for transfers between devices, shifted(): return lax.ppermute(block, axis, route)  20.8 us
    all_gather x1, local copies, waits for them, and re-layouts, shards(): lax.all_gather(time_keys, 'frame', axis=0, tiled=True)  10.3 us
    all_gather x1, local copies, waits for them, and re-layouts, shards(): lax.all_gather(time_values, 'frame', axis=0, tiled=True)  10.3 us
    sub x1, matrix products, softmax_weights(): expo = jnp.exp(scores - top)  8.7 us
    unnamed x26, local copies, waits for them, and re-layouts  5.69 us
  transfers between devices with their start and end apart: 10, of which 5 were waited for; matrix products, arithmetic and copies ran while one was open for 13% of the time, Pallas kernels for 0%

commit v1 on v0

v1 whole, which is shorter than its diff:
```python
import functools

import jax
import jax.numpy as jnp
from jax import lax
from jax.experimental import pallas as pl
from jax.experimental.pallas import tpu as pltpu
from jax.sharding import Mesh
from jax.sharding import PartitionSpec as P

HEAD = 64
HALO = 2
PAIR = 2 * HEAD
EXCLUDED = -1e30
LOG2E = 1.4426950408889634
COLUMN = ("half", "chip", "core")


def unit_rows(rows):
    widened = rows.astype(jnp.float32)
    mean_square = jnp.mean(widened * widened, axis=-1, keepdims=True)
    return (widened * lax.rsqrt(mean_square + 1e-06)).astype(jnp.bfloat16)


def dot(left, right):
    return jnp.dot(left, right, preferred_element_type=jnp.float32)


def dot_rows(left, right):
    return lax.dot_general(
        left, right, (((1,), (1,)), ((), ())), preferred_element_type=jnp.float32
    )


def pair_attend(query, keys, values, biases):
    lane = lax.broadcasted_iota(jnp.int32, query.shape, 1)
    parts = []
    for head in range(2):
        inside = (lane >= HEAD) if head else (lane < HEAD)
        own = jnp.where(inside, query, jnp.zeros_like(query))
        scores = dot_rows(own, keys) + biases
        top = jnp.max(scores, axis=-1, keepdims=True)
        expo = jnp.exp2(scores - top)
        total = jnp.sum(expo, axis=-1, keepdims=True)
        parts.append(dot(expo.astype(jnp.bfloat16), values) / total)
    return jnp.where(lane < HEAD, parts[0], parts[1]).astype(jnp.bfloat16)


def spatial_kernel(
    half_ref, bias_ref, kept_ref, other_ref, qkv_ref, out_w_ref, hidden_ref, query, keys, values, mix, base
):
    half = half_ref[0]
    width = query.shape[1]
    block = kept_ref.shape[1]
    for tiles, parity in ((kept_ref, half), (other_ref, 1 - half)):
        for step in range(3):
            tile = tiles[step]
            normed = unit_rows(tile)
            at = pl.ds(pl.multiple_of((2 * step + parity) * block, block), block)
            projected = dot(normed, qkv_ref[:, width:]).astype(jnp.bfloat16)
            keys[at, :] = projected[:, :width]
            values[at, :] = projected[:, width:]
            if step == 1:
                here = pl.ds(pl.multiple_of(parity * block, block), block)
                query[here, :] = (dot(normed, qkv_ref[:, :width]) * (LOG2E / 8.0)).astype(jnp.bfloat16)
                base[here, :] = tile
    biases = jnp.concatenate(
        [jnp.broadcast_to(bias_ref[y : y + 1, :], (block, bias_ref.shape[1])) for y in range(2)], axis=0
    )
    for pair in range(width // PAIR):
        at = slice(pair * PAIR, (pair + 1) * PAIR)
        mix[:, at] = pair_attend(query[:, at], keys[:, at], values[:, at], biases)
    hidden = base[...].astype(jnp.float32) + dot(mix[...], out_w_ref[...])
    hidden_ref[...] = hidden.astype(jnp.bfloat16)


def time_kernel(hidden_ref, cos_ref, sin_ref, qkv_ref, out_w_ref, layer_ref, query, keys, values, mix):
    rows, width = hidden_ref.shape
    frames = cos_ref.shape[0]
    group = rows // frames
    normed = unit_rows(hidden_ref[...])
    cosine = jnp.concatenate(
        [jnp.broadcast_to(cos_ref[f : f + 1, :], (group, PAIR)) for f in range(frames)], axis=0
    )
    sine = jnp.concatenate(
        [jnp.broadcast_to(sin_ref[f : f + 1, :], (group, PAIR)) for f in range(frames)], axis=0
    )
    lane = lax.broadcasted_iota(jnp.int32, (rows, PAIR), 1)
    first = (lane % HEAD) < HEAD // 2

    def rotate(entries):
        entries = entries.astype(jnp.bfloat16).astype(jnp.float32)
        swapped = jnp.where(
            first, pltpu.roll(entries, PAIR - HEAD // 2, 1), pltpu.roll(entries, HEAD // 2, 1)
        )
        return entries * cosine + swapped * sine

    projected = dot(normed, qkv_ref[:, : 2 * width])
    for pair in range(width // PAIR):
        at = slice(pair * PAIR, (pair + 1) * PAIR)
        query[:, at] = (rotate(projected[:, at]) * (LOG2E / 8.0)).astype(jnp.bfloat16)
        keys[:, at] = rotate(projected[:, width + pair * PAIR : width + (pair + 1) * PAIR]).astype(jnp.bfloat16)
    values[...] = dot(normed, qkv_ref[:, 2 * width :]).astype(jnp.bfloat16)
    row = lax.broadcasted_iota(jnp.int32, (rows, rows), 0)
    column = lax.broadcasted_iota(jnp.int32, (rows, rows), 1)
    biases = jnp.where(row % group == column % group, 0.0, EXCLUDED)
    for pair in range(width // PAIR):
        at = slice(pair * PAIR, (pair + 1) * PAIR)
        mix[:, at] = pair_attend(query[:, at], keys[:, at], values[:, at], biases)
    layer = (hidden_ref[...].astype(jnp.float32) + dot(mix[...], out_w_ref[...])).astype(jnp.bfloat16)
    per_half = frames // 2
    for j in range(frames):
        frame = 2 * (j % per_half) + j // per_half
        layer_ref[frame * group : (frame + 1) * group, :] = layer[j * group : (j + 1) * group, :]


def shards(activations, contacts, frame_index, spatial_qkv, spatial_out, time_qkv, time_out):
    frames_dev, block, width = activations.shape
    pairs = lax.axis_size("pair")
    pair = lax.axis_index("pair")
    half = lax.axis_index("half")
    kept = lax.dynamic_index_in_dim(activations, half, 0, keepdims=False)
    given = lax.dynamic_index_in_dim(activations, 1 - half, 0, keepdims=False)
    other = lax.ppermute(given, "half", [(0, 1), (1, 0)])

    def from_neighbours(tile):
        before = lax.ppermute(tile, "pair", [(i, (i + 1) % pairs) for i in range(pairs)])
        after = lax.ppermute(tile, "pair", [((i + 1) % pairs, i) for i in range(pairs)])
        return jnp.stack([before, tile, after])

    kept_tiles = from_neighbours(kept)
    other_tiles = from_neighbours(other)
    flags = lax.dynamic_slice_in_dim(contacts, 2 * pair, 2, 0)
    spread = jnp.stack([jnp.pad(flags[0], (0, 1)), jnp.pad(flags[1], (1, 0))])
    biases = jnp.repeat(jnp.where(spread > 0, 0.0, EXCLUDED).astype(jnp.float32), block, axis=1)
    vmem = pl.BlockSpec(memory_space=pltpu.VMEM)
    rows = 2 * block
    hidden = pl.pallas_call(
        spatial_kernel,
        out_shape=jax.ShapeDtypeStruct((rows, width), jnp.bfloat16),
        in_specs=[pl.BlockSpec(memory_space=pltpu.SMEM)] + [vmem] * 5,
        out_specs=vmem,
        scratch_shapes=[
            pltpu.VMEM((rows, width), jnp.bfloat16),
            pltpu.VMEM((6 * block, width), jnp.bfloat16),
            pltpu.VMEM((6 * block, width), jnp.bfloat16),
            pltpu.VMEM((rows, width), jnp.bfloat16),
            pltpu.VMEM((rows, width), jnp.bfloat16),
        ],
        compiler_params=pltpu.CompilerParams(vmem_limit_bytes=40 * 1024 * 1024),
        name="spatial",
    )(half.astype(jnp.int32).reshape(1), biases, kept_tiles, other_tiles, spatial_qkv, spatial_out)

    members = 2 * lax.axis_size("chip") * lax.axis_size("core")
    group = rows // members
    hidden = lax.all_to_all(hidden.reshape(members, group, width), COLUMN, 0, 0, tiled=True)

    half_size = HEAD // 2
    frequency = 10000.0 ** (-jnp.arange(half_size, dtype=jnp.float32) / half_size)
    order = frame_index.reshape(members // 2, 2).T.reshape(members)
    angles = order.astype(jnp.float32)[:, None] * frequency[None, :]
    cosine, sine = jnp.cos(angles), jnp.sin(angles)
    cosine = jnp.concatenate([cosine] * 4, axis=1)
    sine = jnp.concatenate([-sine, sine] * 2, axis=1)
    layer = pl.pallas_call(
        time_kernel,
        out_shape=jax.ShapeDtypeStruct((rows, width), jnp.bfloat16),
        in_specs=[vmem] * 5,
        out_specs=vmem,
        scratch_shapes=[pltpu.VMEM((rows, width), jnp.bfloat16)] * 4,
        compiler_params=pltpu.CompilerParams(vmem_limit_bytes=40 * 1024 * 1024),
        name="temporal",
    )(hidden.reshape(rows, width), cosine, sine, time_qkv, time_out)
    return lax.all_to_all(
        layer.reshape(members, group, width), ("chip", "core"), 0, 1, tiled=True
    )


def solution(mesh):
    res, frame = mesh.devices.shape
    fine = Mesh(mesh.devices.reshape(res // 2, 2, frame // 2, 2), ("pair", "half", "chip", "core"))
    placed = (P(("chip", "core"), ("pair", "half"), None), P(), P(), P(), P(), P(), P())
    return jax.shard_map(
        shards, mesh=fine, in_specs=placed, out_specs=placed[0], check_vma=False
    )
```

time: 238 us -> 88.3 us (0.37)
  waiting for transfers between devices: 108 us -> 19.9 us
  local copies, waits for them, and re-layouts: 39 us -> 8.46 us
  matrix products: 26.5 us -> 0 us
  between operations: 16.3 us -> 0.1 us
  blocking collectives: 0 us -> 14.2 us
  other arithmetic: 14.7 us -> 0.97 us
  Pallas kernels: 0 us -> 12.7 us
    all_gather x2 -> x0, waiting for transfers between devices: 87 us -> none  [the longest x1 60.5 us: shards(): lax.all_gather(time_keys, 'frame', axis=0, tiled=True)]
    all_gather x2 -> x0, local copies, waits for them, and re-layouts: 20.5 us -> none  [the longest x1 10.3 us: shards(): lax.all_gather(time_keys, 'frame', axis=0, tiled=True)]
    dot_general x15 -> x0, matrix products: 17.8 us -> none  [the longest x1 5.1 us: time_attend(): jnp.einsum('rhfg,grhd->frhd', weights, values, preferred_element_type=jnp...]
    ppermute x8 -> x5, waiting for transfers between devices: 20.8 us -> 6.28 us  [the longest x1 3.39 us: shards(): other = lax.ppermute(given, 'half', [(0, 1), (1, 0)])]
    all_to_all x0 -> x1, blocking collectives: none -> 14.2 us  [shards(): lax.all_to_all(layer.reshape(members, group, width), ('chip', 'core'), 0,...]
    all_to_all x0 -> x1, starting transfers between devices: none -> 14 us  [shards(): lax.all_to_all(hidden.reshape(members, group, width), COLUMN, 0, 0, tiled...]
    ppermute x8 -> x5, starting transfers between devices: 31.3 us -> 17.6 us  [the longest x2 8.59 us: from_neighbours(): lax.ppermute(tile, 'pair', [((i + 1) % pairs, i) for i in range(pairs)])]
    all_to_all x0 -> x1, waiting for transfers between devices: none -> 13.6 us  [shards(): lax.all_to_all(hidden.reshape(members, group, width), COLUMN, 0, 0, tiled...]
  transfers between devices with their start and end apart: 10 -> 6, of which waited for: 5 -> 3; matrix products, arithmetic and copies ran while one was open for 13% -> 2% of each run, Pallas kernels for 0% -> 0%
where the time goes in v1:
time: 88.3 us; the launch traced here: 87.9 us
  starting transfers between devices  31.6 us (36%)
  waiting for transfers between devices  19.9 us (23%)
  blocking collectives  14.2 us (16%)
  Pallas kernels  12.7 us (14%)
  local copies, waits for them, and re-layouts  8.46 us (10%)
  other arithmetic  0.97 us (1%)
    all_to_all x1, blocking collectives, shards(): lax.all_to_all(layer.reshape(members, group, width), ('chip', 'core'), 0,...  14.2 us
    all_to_all x1, starting transfers between devices, shards(): lax.all_to_all(hidden.reshape(members, group, width), COLUMN, 0, 0, tiled...  14 us
    all_to_all x1, waiting for transfers between devices, shards(): lax.all_to_all(hidden.reshape(members, group, width), COLUMN, 0, 0, tiled...  13.6 us
    ppermute x2, starting transfers between devices, from_neighbours(): lax.ppermute(tile, 'pair', [((i + 1) % pairs, i) for i in range(pairs)])  8.59 us
    pallas_call x1, Pallas kernels, shards(): pl.pallas_call(spatial_kernel, out_shape=jax.ShapeDtypeStruct((rows, widt...  7.71 us
    ppermute x1, starting transfers between devices, shards(): other = lax.ppermute(given, 'half', [(0, 1), (1, 0)])  6.91 us
    unnamed x18, local copies, waits for them, and re-layouts  6.06 us
    pallas_call x1, Pallas kernels, shards(): pl.pallas_call(time_kernel, out_shape=jax.ShapeDtypeStruct((rows, width),...  5 us
  transfers between devices with their start and end apart: 6, of which 3 were waited for; matrix products, arithmetic and copies ran while one was open for 2% of the time, Pallas kernels for 0%

profile of v1, /device:TPU:1, one launch (start us, length us, event | category | flops | bytes accessed | tf_op | source)
XLA Modules:
  0.0 87.9 jit_solution(11473060660255980122)
XLA Ops:
  0.0 0.0 copy-start
  0.0 1.1 %dynamic-slice_bitcast_fusion = (bf16[128,768]{1,0:T(8,128)(2,1)S(1)}, bf16[1,128,768]{2,1,0:T(8,128)(2,1)S(1)}) fusion(bf16[2,128,768]{2,1,0:T(8,128)(2,1)} %param.7, s32[]{:T(128)S(6)} %select_n.17, s32[]{:T(128)S(6)} %select_n.16), kind=kLoop, calls=%fused_computation.2 | loop fusion | bytes 786440 | tf_op jit(solution)/shard_map/jit(dynamic_index_in_dim)/squeeze | solution.py:123
  1.1 2.1 %collective-permute-start = (bf16[128,768]{1,0:T(8,128)(2,1)S(1)}, bf16[128,768]{1,0:T(8,128)(2,1)S(1)}, u32[]{:S(2)}, u32[]{:S(2)}) collective-permute-start(bf16[128,768]{1,0:T(8,128)(2,1)S(1)} %bitcast.30), channel_id=1, source_target_pairs={{0,16},{16,32},{32,48},{48,64},{64,80},{80,96},{96,112},{112,128},... | collective-permute-start | bytes 589832 | tf_op jit(solution)/shard_map/ppermute | solution.py:127
  3.2 3.8 %collective-permute-start.1 = (bf16[128,768]{1,0:T(8,128)(2,1)S(1)}, bf16[128,768]{1,0:T(8,128)(2,1)S(1)}, u32[]{:S(2)}, u32[]{:S(2)}) collective-permute-start(bf16[128,768]{1,0:T(8,128)(2,1)S(1)} %bitcast.31), channel_id=1, source_target_pairs={{16,0},{32,16},{48,32},{64,48},{80,64},{96,80},{112,96},{128,112},... | collective-permute-start | bytes 589832 | tf_op jit(solution)/shard_map/ppermute | solution.py:128
  7.0 6.9 %collective-permute-start.2 = (bf16[128,768]{1,0:T(8,128)(2,1)S(1)}, bf16[128,768]{1,0:T(8,128)(2,1)S(1)}, u32[]{:S(2)}, u32[]{:S(2)}) collective-permute-start(bf16[128,768]{1,0:T(8,128)(2,1)S(1)} %get-tuple-element.7), channel_id=1, source_target_pairs={{0,8},{8,0},{1,9},{9,1},{2,10},{10,2},{3,11},{11,3},{4,12},{12,4},... | collective-permute-start | bytes 589832 | tf_op jit(solution)/shard_map/ppermute | solution.py:124
  13.9 0.0 copy-done
  13.9 0.1 constant_dynamic-slice_fusion.1
  14.0 0.2 slice_reduce_fusion.1
  14.2 0.1 pad_bitcast_fusion
  14.2 3.4 %collective-permute-done.2 = bf16[128,768]{1,0:T(8,128)(2,1)S(1)} collective-permute-done((bf16[128,768]{1,0:T(8,128)(2,1)S(1)}, bf16[128,768]{1,0:T(8,128)(2,1)S(1)}, u32[]{:S(2)}, u32[]{:S(2)}) %collective-permute-start.2) | collective-permute-done | bytes 196640 | tf_op jit(solution)/shard_map/ppermute | solution.py:124
  17.6 0.0 collective-permute-start.3
  17.6 4.8 %collective-permute-start.4 = (bf16[128,768]{1,0:T(8,128)(2,1)S(1)}, bf16[128,768]{1,0:T(8,128)(2,1)S(1)}, u32[]{:S(2)}, u32[]{:S(2)}) collective-permute-start(bf16[128,768]{1,0:T(8,128)(2,1)S(1)} %collective-permute-done.2), channel_id=1, source_target_pairs={{16,0},{32,16},{48,32},{64,48},{80,64},{96,80},{112,96},{128,112},... | collective-permute-start | bytes 589832 | tf_op jit(solution)/shard_map/ppermute | solution.py:128
  22.4 0.1 broadcast_bitcast_fusion
  22.5 0.0 collective-permute-done
  22.5 0.0 collective-permute-done.1
  22.5 0.1 pad_maximum_fusion.kept_ref
  22.6 2.9 %collective-permute-done.3 = bf16[128,768]{1,0:T(8,128)(2,1)S(1)} collective-permute-done((bf16[128,768]{1,0:T(8,128)(2,1)S(1)}, bf16[128,768]{1,0:T(8,128)(2,1)S(1)}, u32[]{:S(2)}, u32[]{:S(2)}) %collective-permute-start.3) | collective-permute-done | bytes 196640 | tf_op jit(solution)/shard_map/ppermute | solution.py:127
  25.5 0.0 collective-permute-done.4
  25.5 0.1 pad_maximum_fusion.1.other_ref
  25.5 0.0 copy-start.1
  25.6 2.0 %copy-done.1 = bf16[768,2304]{1,0:T(8,128)(2,1)S(1)} copy-done((bf16[768,2304]{1,0:T(8,128)(2,1)S(1)}, bf16[768,2304]{1,0:T(8,128)(2,1)}, u32[]{:S(2)}) %copy-start.1) | copy-done | bytes 3538968
  27.6 0.0 copy-start.4
  27.6 1.3 %copy-done.4 = bf16[768,768]{1,0:T(8,128)(2,1)S(1)} copy-done((bf16[768,768]{1,0:T(8,128)(2,1)S(1)}, bf16[768,768]{1,0:T(8,128)(2,1)}, u32[]{:S(2)}) %copy-start.4) | copy-done | bytes 1179672
  28.8 0.0 copy-start.7
  28.8 0.0 copy-start.2
  28.8 7.7 %spatial.1 = bf16[256,768]{1,0:T(8,128)(2,1)S(1)} custom-call(s32[1]{0:T(128)} %bitcast.half_ref, f32[2,768]{1,0:T(2,128)S(1)} %bitcast.28, bf16[3,128,768]{2,1,0:T(8,128)(2,1)S(1)} %pad_maximum_fusion.kept_ref, bf16[3,128,768]{2,1,0:T(8,128)(2,1)S(1)} %pad_maximum_fusion.1.other_ref, bf16[768,2304]{1,0:T(8,128)(2,1)S(1)} %copy-done.1, ...), custom_call_target="tpu_custom_call" | custom-call | tf_op jit(solution)/shard_map/spatial/pallas_call | solution.py:138
  36.6 0.0 copy-start.3
  36.6 0.7 copy-done.3
  37.3 14.0 %all-to-all-start = ((bf16[16,16,768]{2,1,0:T(8,128)(2,1)}), bf16[16,16,768]{2,1,0:T(8,128)(2,1)}, u32[]{:S(2)}, u32[]{:S(2)}) async-start(bf16[16,16,768]{2,1,0:T(8,128)(2,1)} %bitcast.26), calls=%async_computation | async-start | bytes 786432 | tf_op jit(solution)/shard_map/all_to_all | solution.py:156
  51.3 0.0 copy-done.7
  51.3 0.1 convert_element_type.17
  51.4 0.1 copy.10
  51.5 0.1 convert_element_type.19
  51.5 0.1 fusion
  51.7 0.7 pad_maximum_fusion.2
  52.4 13.6 %all-to-all-done = bf16[16,16,768]{2,1,0:T(8,128)(2,1)} async-done(((bf16[16,16,768]{2,1,0:T(8,128)(2,1)}), bf16[16,16,768]{2,1,0:T(8,128)(2,1)}, u32[]{:S(2)}, u32[]{:S(2)}) %all-to-all-start) | async-done | bytes 393248 | tf_op jit(solution)/shard_map/all_to_all | solution.py:156
  65.9 0.0 copy-done.2
  65.9 0.0 copy-start.5
  65.9 1.3 %copy-done.5 = bf16[768,768]{1,0:T(8,128)(2,1)S(1)} copy-done((bf16[768,768]{1,0:T(8,128)(2,1)S(1)}, bf16[768,768]{1,0:T(8,128)(2,1)}, u32[]{:S(2)}) %copy-start.5) | copy-done | bytes 1179672
  67.2 0.0 copy-start.6
  67.2 0.7 copy-done.6
  67.9 5.0 %temporal.1 = bf16[256,768]{1,0:T(8,128)(2,1)S(1)} custom-call(bf16[256,768]{1,0:T(8,128)(2,1)} %bitcast.11.hidden_ref, f32[16,128]{1,0:T(8,128)S(1)} %get-tuple-element.14.cos_ref, f32[16,128]{1,0:T(8,128)S(1)} %copy-done.6, bf16[768,2304]{1,0:T(8,128)(2,1)S(1)} %copy-done.2, bf16[768,768]{1,0:T(8,128)(2,1)S(1)} %copy-done.5), custom_call_target="tpu_custom_call" | custom-call | tf_op jit(solution)/shard_map/temporal/pallas_call | solution.py:165
  72.9 14.2 %all_to_all.23 = bf16[16,16,768]{2,1,0:T(8,128)(2,1)S(1)} all-to-all(bf16[16,16,768]{2,1,0:T(8,128)(2,1)S(1)} %bitcast.27), channel_id=1, replica_groups=mesh['pair'=16,'half'=2,'chip'=4,'core'=2] {'chip','core'}, dimensions={0} | all-to-all | bytes 786432 | tf_op jit(solution)/shard_map/all_to_all | solution.py:174
  87.1 0.8 copy.11
  (4 shorter events, 0.0 us)
Async XLA Ops:
  0.0 13.9 %copy-start = (s32[32,5]{0,1:T(8,128)S(1)}, s32[32,5]{0,1:T(8,128)}, u32[]{:S(2)}) copy-start(s32[32,5]{0,1:T(8,128)} %param.8) | copy-start | bytes 1924
  1.1 21.4 %collective-permute-start = (bf16[128,768]{1,0:T(8,128)(2,1)S(1)}, bf16[128,768]{1,0:T(8,128)(2,1)S(1)}, u32[]{:S(2)}, u32[]{:S(2)}) collective-permute-start(bf16[128,768]{1,0:T(8,128)(2,1)S(1)} %bitcast.30), channel_id=1, source_target_pairs={{0,16},{16,32},{32,48},{48,64},{64,80},{80,96},{96,112},{112,128},... | collective-permute-start | bytes 589832 | tf_op jit(solution)/shard_map/ppermute | solution.py:127
  3.2 19.3 %collective-permute-start.1 = (bf16[128,768]{1,0:T(8,128)(2,1)S(1)}, bf16[128,768]{1,0:T(8,128)(2,1)S(1)}, u32[]{:S(2)}, u32[]{:S(2)}) collective-permute-start(bf16[128,768]{1,0:T(8,128)(2,1)S(1)} %bitcast.31), channel_id=1, source_target_pairs={{16,0},{32,16},{48,32},{64,48},{80,64},{96,80},{112,96},{128,112},... | collective-permute-start | bytes 589832 | tf_op jit(solution)/shard_map/ppermute | solution.py:128
  7.0 10.6 %collective-permute-start.2 = (bf16[128,768]{1,0:T(8,128)(2,1)S(1)}, bf16[128,768]{1,0:T(8,128)(2,1)S(1)}, u32[]{:S(2)}, u32[]{:S(2)}) collective-permute-start(bf16[128,768]{1,0:T(8,128)(2,1)S(1)} %get-tuple-element.7), channel_id=1, source_target_pairs={{0,8},{8,0},{1,9},{9,1},{2,10},{10,2},{3,11},{11,3},{4,12},{12,4},... | collective-permute-start | bytes 589832 | tf_op jit(solution)/shard_map/ppermute | solution.py:124
  17.6 7.8 %collective-permute-start.3 = (bf16[128,768]{1,0:T(8,128)(2,1)S(1)}, bf16[128,768]{1,0:T(8,128)(2,1)S(1)}, u32[]{:S(2)}, u32[]{:S(2)}) collective-permute-start(bf16[128,768]{1,0:T(8,128)(2,1)S(1)} %collective-permute-done.2), channel_id=1, source_target_pairs={{0,16},{16,32},{32,48},{48,64},{64,80},{80,96},{96,112},{112,128},... | collective-permute-start | bytes 589832 | tf_op jit(solution)/shard_map/ppermute | solution.py:127
  17.6 7.8 %collective-permute-start.4 = (bf16[128,768]{1,0:T(8,128)(2,1)S(1)}, bf16[128,768]{1,0:T(8,128)(2,1)S(1)}, u32[]{:S(2)}, u32[]{:S(2)}) collective-permute-start(bf16[128,768]{1,0:T(8,128)(2,1)S(1)} %collective-permute-done.2), channel_id=1, source_target_pairs={{16,0},{32,16},{48,32},{64,48},{80,64},{96,80},{112,96},{128,112},... | collective-permute-start | bytes 589832 | tf_op jit(solution)/shard_map/ppermute | solution.py:128
  25.5 2.0 %copy-start.1 = (bf16[768,2304]{1,0:T(8,128)(2,1)S(1)}, bf16[768,2304]{1,0:T(8,128)(2,1)}, u32[]{:S(2)}) copy-start(bf16[768,2304]{1,0:T(8,128)(2,1)} %qkv_ref.2) | copy-start | bytes 10616836
  27.6 1.3 %copy-start.4 = (bf16[768,768]{1,0:T(8,128)(2,1)S(1)}, bf16[768,768]{1,0:T(8,128)(2,1)}, u32[]{:S(2)}) copy-start(bf16[768,768]{1,0:T(8,128)(2,1)} %out_w_ref.2) | copy-start | bytes 3538948
  28.8 22.4 %copy-start.7 = (s32[16]{0:T(128)S(1)}, s32[16]{0:T(128)}, u32[]{:S(2)}) copy-start(s32[16]{0:T(128)} %param.9) | copy-start | bytes 196
  28.8 37.1 %copy-start.2 = (bf16[768,2304]{1,0:T(8,128)(2,1)S(1)}, bf16[768,2304]{1,0:T(8,128)(2,1)}, u32[]{:S(2)}) copy-start(bf16[768,2304]{1,0:T(8,128)(2,1)} %qkv_ref.3) | copy-start | bytes 10616836
  36.6 0.7 copy-start.3
  37.3 28.6 %all-to-all-start = ((bf16[16,16,768]{2,1,0:T(8,128)(2,1)}), bf16[16,16,768]{2,1,0:T(8,128)(2,1)}, u32[]{:S(2)}, u32[]{:S(2)}) async-start(bf16[16,16,768]{2,1,0:T(8,128)(2,1)} %bitcast.26), calls=%async_computation | async-start | bytes 786432 | tf_op jit(solution)/shard_map/all_to_all | solution.py:156
  65.9 1.3 %copy-start.5 = (bf16[768,768]{1,0:T(8,128)(2,1)S(1)}, bf16[768,768]{1,0:T(8,128)(2,1)}, u32[]{:S(2)}) copy-start(bf16[768,768]{1,0:T(8,128)(2,1)} %out_w_ref.3) | copy-start | bytes 3538948
  67.2 0.7 copy-start.6

commit v2 on v1

v2 whole, which is shorter than its diff:
```python
import math

import jax
import jax.numpy as jnp
from jax import lax
from jax.experimental import pallas as pl
from jax.experimental.pallas import tpu as pltpu
from jax.sharding import Mesh
from jax.sharding import PartitionSpec as P

HEAD = 64
PAIR = 2 * HEAD
EXCLUDED = -1e30
LOG2E = 1.4426950408889634
SCALE = LOG2E / 8.0
COLUMN = ("half", "chip", "core")
VMEM = pl.BlockSpec(memory_space=pltpu.VMEM)
SMEM = pl.BlockSpec(memory_space=pltpu.SMEM)
HBM = pl.BlockSpec(memory_space=pltpu.HBM)
LIMIT = pltpu.CompilerParams(vmem_limit_bytes=24 * 1024 * 1024)


def unit_rows(rows):
    widened = rows.astype(jnp.float32)
    mean_square = jnp.mean(widened * widened, axis=-1, keepdims=True)
    return (widened * lax.rsqrt(mean_square + 1e-06)).astype(jnp.bfloat16)


def dot(left, right):
    return jnp.dot(left, right, preferred_element_type=jnp.float32)


def dot_rows(left, right):
    return lax.dot_general(
        left, right, (((1,), (1,)), ((), ())), preferred_element_type=jnp.float32
    )


def lanes_of(query, head):
    lane = lax.broadcasted_iota(jnp.int32, query.shape, 1)
    inside = (lane >= HEAD) if head else (lane < HEAD)
    return jnp.where(inside, query, jnp.zeros_like(query))


def side_by_side(first, second, rows):
    lane = lax.broadcasted_iota(jnp.int32, (rows, PAIR), 1)
    return jnp.where(lane < HEAD, first, second)


def attend(query, keys, values, biases, head, floor=None):
    scores = dot_rows(lanes_of(query, head), keys) + biases
    top = jnp.max(scores, axis=-1, keepdims=True)
    if floor is not None:
        top = jnp.maximum(top, floor)
    expo = jnp.exp2(scores - top)
    total = jnp.sum(expo, axis=-1, keepdims=True)
    return dot(expo.astype(jnp.bfloat16), values), top, total


def two_rows(bias_ref, block):
    return jnp.concatenate(
        [jnp.broadcast_to(bias_ref[y : y + 1, :], (block, bias_ref.shape[1])) for y in range(2)], axis=0
    )


def give_kernel(place_ref, act_ref, given_ref, semaphore):
    move = pltpu.make_async_copy(act_ref.at[1 - place_ref[0]], given_ref, semaphore)
    move.start()
    move.wait()


def contact_biases(place_ref, contacts_ref, early_ref, late_ref):
    half, pair = place_ref[0], place_ref[1]
    block = early_ref.shape[1] // 4
    to_other = 1 - 2 * half
    for row, (parity, moves) in enumerate(
        (
            (half, (0, -2, 2, to_other, to_other - 2, to_other + 2)),
            (1 - half, (-to_other, -to_other - 2, -to_other + 2, 0, -2, 2)),
        )
    ):
        for tile, move in enumerate(moves):
            column = jnp.clip(move + 2, 0, 4)
            flag = jnp.where(column == move + 2, contacts_ref[2 * pair + parity, column], 0)
            ref, at = (early_ref, tile) if tile < 4 else (late_ref, tile - 4)
            ref[row : row + 1, at * block : (at + 1) * block] = jnp.full(
                (1, block), jnp.where(flag > 0, 0.0, EXCLUDED), jnp.float32
            )


def rotation_tables(frame_ref, cos_ref, sin_ref):
    frames, lanes = cos_ref.shape
    row = lax.broadcasted_iota(jnp.int32, (frames, lanes), 0)
    lane = lax.broadcasted_iota(jnp.int32, (frames, lanes), 1)
    position = jnp.zeros((frames, lanes), jnp.int32)
    for j in range(frames):
        frame = 2 * (j % (frames // 2)) + j // (frames // 2)
        position = jnp.where(row == j, frame_ref[frame], position)
    half_size = HEAD // 2
    exponent = (lane % half_size).astype(jnp.float32) * (-math.log(10000.0) / half_size)
    angles = position.astype(jnp.float32) * jnp.exp(exponent)
    cos_ref[...] = jnp.cos(angles)
    sine = jnp.sin(angles)
    sin_ref[...] = jnp.where(lane % HEAD < half_size, -sine, sine)


def first_kernel(
    place_ref, contacts_ref, frame_ref, given_ref, act_ref, qkv_hbm, out_hbm, time_qkv_hbm, time_out_hbm,
    qkv_ref, out_ref, time_qkv_ref, time_out_ref, normed_ref, base_ref, query_ref, keys_ref, values_ref,
    early_ref, late_ref, cos_ref, sin_ref, sent, semaphores,
):
    half = place_ref[0]
    width = base_ref.shape[1]
    own = pltpu.make_async_copy(act_ref.at[half], base_ref, semaphores.at[0])
    own.start()
    loads = []
    for at, (source, target) in enumerate(
        ((qkv_hbm, qkv_ref), (out_hbm, out_ref), (time_qkv_hbm, time_qkv_ref), (time_out_hbm, time_out_ref))
    ):
        loads.append(pltpu.make_async_copy(source, target, semaphores.at[at + 1]))
        loads[-1].start()
    own.wait()
    normed = unit_rows(base_ref[...])
    sent[...] = normed
    store = pltpu.make_async_copy(sent, normed_ref, semaphores.at[5])
    store.start()
    loads[0].wait()
    query_ref[...] = (dot(normed, qkv_ref[:, :width]) * SCALE).astype(jnp.bfloat16)
    keys_ref[...] = dot(normed, qkv_ref[:, width : 2 * width]).astype(jnp.bfloat16)
    values_ref[...] = dot(normed, qkv_ref[:, 2 * width :]).astype(jnp.bfloat16)
    contact_biases(place_ref, contacts_ref, early_ref, late_ref)
    rotation_tables(frame_ref, cos_ref, sin_ref)
    store.wait()
    for load in loads[1:]:
        load.wait()


def early_kernel(
    bias_ref, query_in, keys_in, values_in, before_ref, after_ref, other_ref, qkv_ref,
    query_ref, sums_ref, tops_ref, totals_ref, keys, values,
):
    block, width = other_ref.shape
    query_ref[:block, :] = query_in[...]
    normed = unit_rows(other_ref[...])
    query_ref[block:, :] = (dot(normed, qkv_ref[:, :width]) * SCALE).astype(jnp.bfloat16)
    keys[:block, :] = keys_in[...]
    values[:block, :] = values_in[...]
    tiles = jnp.concatenate([before_ref[...], after_ref[...], normed], axis=0)
    keys[block:, :] = dot(tiles, qkv_ref[:, width : 2 * width]).astype(jnp.bfloat16)
    values[block:, :] = dot(tiles, qkv_ref[:, 2 * width :]).astype(jnp.bfloat16)
    biases = two_rows(bias_ref, block)
    for pair in range(width // PAIR):
        at = slice(pair * PAIR, (pair + 1) * PAIR)
        parts = [attend(query_ref[:, at], keys[:, at], values[:, at], biases, head) for head in range(2)]
        for ref, piece in ((sums_ref, 0), (tops_ref, 1), (totals_ref, 2)):
            ref[:, at] = side_by_side(parts[0][piece], parts[1][piece], 2 * block)


def late_kernel(
    place_ref, bias_ref, query_ref, sums_ref, tops_ref, totals_ref, before_ref, after_ref,
    base_ref, other_ref, qkv_ref, out_ref, hidden_ref, keys, values, mix, hidden, semaphore,
):
    half = place_ref[0]
    block, width = other_ref.shape
    tiles = unit_rows(jnp.concatenate([before_ref[...], after_ref[...]], axis=0))
    keys[...] = dot(tiles, qkv_ref[:, width : 2 * width]).astype(jnp.bfloat16)
    values[...] = dot(tiles, qkv_ref[:, 2 * width :]).astype(jnp.bfloat16)
    biases = two_rows(bias_ref, block)
    for pair in range(width // PAIR):
        at = slice(pair * PAIR, (pair + 1) * PAIR)
        floors = tops_ref[:, at]
        parts = [
            attend(
                query_ref[:, at], keys[:, at], values[:, at], biases, head,
                floors[:, head * HEAD : head * HEAD + 1],
            )
            for head in range(2)
        ]
        late = [side_by_side(parts[0][piece], parts[1][piece], 2 * block) for piece in range(3)]
        share = jnp.exp2(floors - late[1])
        total = totals_ref[:, at] * share + late[2]
        mix[:, at] = ((sums_ref[:, at] * share + late[0]) / total).astype(jnp.bfloat16)
    added = dot(mix[...], out_ref[...])
    here = pl.ds(pl.multiple_of(half * block, block), block)
    there = pl.ds(pl.multiple_of((1 - half) * block, block), block)
    hidden[here, :] = (base_ref[...].astype(jnp.float32) + added[:block]).astype(jnp.bfloat16)
    hidden[there, :] = (other_ref[...].astype(jnp.float32) + added[block:]).astype(jnp.bfloat16)
    store = pltpu.make_async_copy(hidden, hidden_ref, semaphore)
    store.start()
    store.wait()


def time_kernel(
    hidden_ref, cos_ref, sin_ref, qkv_ref, out_w_ref, layer_ref, query, keys, values, mix, layer, semaphore
):
    rows, width = hidden_ref.shape
    frames = cos_ref.shape[0]
    group = rows // frames
    normed = unit_rows(hidden_ref[...])
    cosine = jnp.concatenate(
        [jnp.broadcast_to(cos_ref[f : f + 1, :], (group, PAIR)) for f in range(frames)], axis=0
    )
    sine = jnp.concatenate(
        [jnp.broadcast_to(sin_ref[f : f + 1, :], (group, PAIR)) for f in range(frames)], axis=0
    )
    lane = lax.broadcasted_iota(jnp.int32, (rows, PAIR), 1)
    first = (lane % HEAD) < HEAD // 2

    def rotate(entries):
        entries = entries.astype(jnp.bfloat16).astype(jnp.float32)
        swapped = jnp.where(
            first, pltpu.roll(entries, PAIR - HEAD // 2, 1), pltpu.roll(entries, HEAD // 2, 1)
        )
        return entries * cosine + swapped * sine

    projected = dot(normed, qkv_ref[:, : 2 * width])
    for pair in range(width // PAIR):
        at = slice(pair * PAIR, (pair + 1) * PAIR)
        query[:, at] = (rotate(projected[:, at]) * SCALE).astype(jnp.bfloat16)
        keys[:, at] = rotate(projected[:, width + pair * PAIR : width + (pair + 1) * PAIR]).astype(jnp.bfloat16)
    values[...] = dot(normed, qkv_ref[:, 2 * width :]).astype(jnp.bfloat16)
    row = lax.broadcasted_iota(jnp.int32, (rows, rows), 0)
    column = lax.broadcasted_iota(jnp.int32, (rows, rows), 1)
    biases = jnp.where(row % group == column % group, 0.0, EXCLUDED)
    for pair in range(width // PAIR):
        at = slice(pair * PAIR, (pair + 1) * PAIR)
        parts = [attend(query[:, at], keys[:, at], values[:, at], biases, head) for head in range(2)]
        mix[:, at] = side_by_side(
            parts[0][0] / parts[0][2], parts[1][0] / parts[1][2], rows
        ).astype(jnp.bfloat16)
    added = (hidden_ref[...].astype(jnp.float32) + dot(mix[...], out_w_ref[...])).astype(jnp.bfloat16)
    per_half = frames // 2
    for j in range(frames):
        frame = 2 * (j % per_half) + j // per_half
        layer[frame * group : (frame + 1) * group, :] = added[j * group : (j + 1) * group, :]
    store = pltpu.make_async_copy(layer, layer_ref, semaphore)
    store.start()
    store.wait()


def shards(activations, contacts, frame_index, spatial_qkv, spatial_out, time_qkv, time_out):
    frames_dev, block, width = activations.shape
    pairs = lax.axis_size("pair")
    pair = lax.axis_index("pair")
    half = lax.axis_index("half")
    place = jnp.stack([half, pair]).astype(jnp.int32)
    activations, spatial_qkv, spatial_out, time_qkv, time_out = (
        pltpu.with_memory_space_constraint(x, pltpu.HBM)
        for x in (activations, spatial_qkv, spatial_out, time_qkv, time_out)
    )
    rows = 2 * block
    bf16, f32 = jnp.bfloat16, jnp.float32
    given = pl.pallas_call(
        give_kernel,
        out_shape=pltpu.HBM((block, width), bf16),
        in_specs=[SMEM, HBM],
        out_specs=HBM,
        scratch_shapes=[pltpu.SemaphoreType.DMA],
        name="give",
    )(place, activations)
    other = lax.ppermute(given, "half", [(0, 1), (1, 0)])

    def from_neighbours(tile):
        before = lax.ppermute(tile, "pair", [(i, (i + 1) % pairs) for i in range(pairs)])
        after = lax.ppermute(tile, "pair", [((i + 1) % pairs, i) for i in range(pairs)])
        return before, after

    tile_in_vmem = pltpu.VMEM((block, width), bf16)
    weights = (spatial_qkv, spatial_out, time_qkv, time_out)
    members = 2 * lax.axis_size("chip") * lax.axis_size("core")
    table = pltpu.VMEM((members, PAIR), f32)
    *weights, normed, base, query, keys, values, early_bias, late_bias, cosine, sine = pl.pallas_call(
        first_kernel,
        out_shape=tuple(pltpu.VMEM(w.shape, bf16) for w in weights)
        + (pltpu.HBM((block, width), bf16),)
        + (tile_in_vmem,) * 4
        + (pltpu.VMEM((2, 4 * block), f32), pltpu.VMEM((2, 2 * block), f32), table, table),
        in_specs=[SMEM] * 3 + [HBM] * 6,
        out_specs=(VMEM,) * 4 + (HBM,) + (VMEM,) * 8,
        scratch_shapes=[tile_in_vmem, pltpu.SemaphoreType.DMA((6,))],
        compiler_params=LIMIT,
        cost_estimate=pl.CostEstimate(flops=2 * block * width * 3 * width, bytes_accessed=10_000_000, transcendentals=0),
        name="first",
    )(place, contacts, frame_index, pltpu.with_memory_space_constraint(given, pltpu.HBM), activations, *weights)
    spatial_qkv, spatial_out, time_qkv, time_out = weights
    kept_before, kept_after = from_neighbours(normed)
    other_before, other_after = from_neighbours(other)

    wide = pltpu.VMEM((rows, width), f32)
    query, sums, tops, totals = pl.pallas_call(
        early_kernel,
        out_shape=(pltpu.VMEM((rows, width), bf16), wide, wide, wide),
        in_specs=[VMEM] * 8,
        out_specs=(VMEM,) * 4,
        scratch_shapes=[pltpu.VMEM((4 * block, width), bf16)] * 2,
        compiler_params=LIMIT,
        cost_estimate=pl.CostEstimate(flops=4_000_000_000, bytes_accessed=4_000_000, transcendentals=2_000_000),
        name="early",
    )(early_bias, query, keys, values, kept_before, kept_after, other, spatial_qkv)
    hidden = pl.pallas_call(
        late_kernel,
        out_shape=pltpu.HBM((rows, width), bf16),
        in_specs=[SMEM] + [VMEM] * 11,
        out_specs=HBM,
        scratch_shapes=[pltpu.VMEM((rows, width), bf16)] * 4 + [pltpu.SemaphoreType.DMA],
        compiler_params=LIMIT,
        name="late",
    )(
        place, late_bias, query, sums, tops, totals, other_before, other_after,
        base, other, spatial_qkv, spatial_out,
    )

    group = rows // members
    hidden = lax.all_to_all(hidden.reshape(members, group, width), COLUMN, 0, 0, tiled=True)

    layer = pl.pallas_call(
        time_kernel,
        out_shape=pltpu.HBM((rows, width), bf16),
        in_specs=[VMEM] * 5,
        out_specs=HBM,
        scratch_shapes=[pltpu.VMEM((rows, width), bf16)] * 5 + [pltpu.SemaphoreType.DMA],
        compiler_params=LIMIT,
        name="temporal",
    )(hidden.reshape(rows, width), cosine, sine, time_qkv, time_out)
    return lax.all_to_all(
        layer.reshape(members, group, width), ("chip", "core"), 0, 1, tiled=True
    )


def solution(mesh):
    res, frame = mesh.devices.shape
    fine = Mesh(mesh.devices.reshape(res // 2, 2, frame // 2, 2), ("pair", "half", "chip", "core"))
    placed = (P(("chip", "core"), ("pair", "half"), None), P(), P(), P(), P(), P(), P())
    return jax.shard_map(
        shards, mesh=fine, in_specs=placed, out_specs=placed[0], check_vma=False
    )
```

time: 88.3 us -> 85 us (0.963)
  blocking collectives: 14.2 us -> 34.4 us
  waiting for transfers between devices: 19.9 us -> 0.01 us
  Pallas kernels: 12.7 us -> 29 us
  starting transfers between devices: 31.6 us -> 17.7 us
  local copies, waits for them, and re-layouts: 8.46 us -> 2.85 us
    all_to_all x0 -> x1, blocking collectives: none -> 20 us  [shards(): lax.all_to_all(hidden.reshape(members, group, width), COLUMN, 0, 0, tiled...]
    pallas_call x2 -> x5, Pallas kernels: 12.7 us -> 29 us  [the longest x1 7.73 us: shards(): pl.pallas_call(give_kernel, out_shape=pltpu.HBM((block, width), bf16), in...]
    all_to_all x1 -> x0, starting transfers between devices: 14 us -> none  [shards(): lax.all_to_all(hidden.reshape(members, group, width), COLUMN, 0, 0, tiled...]
    all_to_all x1 -> x0, waiting for transfers between devices: 13.6 us -> none  [shards(): lax.all_to_all(hidden.reshape(members, group, width), COLUMN, 0, 0, tiled...]
    unnamed x18 -> x5, local copies, waits for them, and re-layouts: 6.06 us -> 2.07 us
    ppermute x1, waiting for transfers between devices: 3.39 us -> 0.01 us  [shards(): other = lax.ppermute(given, 'half', [(0, 1), (1, 0)])]
    ppermute x2, waiting for transfers between devices: 2.89 us -> 0.01 us  [from_neighbours(): lax.ppermute(tile, 'pair', [(i, (i + 1) % pairs) for i in range(pairs)])]
    squeeze x1 -> x0, local copies, waits for them, and re-layouts: 1.06 us -> none  [shards(): given = lax.dynamic_index_in_dim(activations, 1 - half, 0, keepdims=False)]
  transfers between devices with their start and end apart: 6 -> 5, of which waited for: 3 -> 0; matrix products, arithmetic and copies ran while one was open for 2% -> 1% of each run, Pallas kernels for 0% -> 12%
where the time goes in v2:
time: 85 us; the launch traced here: 84.7 us
  blocking collectives  34.4 us (40%)
  Pallas kernels  29 us (34%)
  starting transfers between devices  17.7 us (21%)
  local copies, waits for them, and re-layouts  2.85 us (3%)
    all_to_all x1, blocking collectives, shards(): lax.all_to_all(hidden.reshape(members, group, width), COLUMN, 0, 0, tiled...  20 us
    all_to_all x1, blocking collectives, shards(): lax.all_to_all(layer.reshape(members, group, width), ('chip', 'core'), 0,...  14.4 us
    ppermute x2, starting transfers between devices, from_neighbours(): lax.ppermute(tile, 'pair', [((i + 1) % pairs, i) for i in range(pairs)])  8.59 us
    ppermute x1, starting transfers between devices, shards(): other = lax.ppermute(given, 'half', [(0, 1), (1, 0)])  7.83 us
    pallas_call x1, Pallas kernels, shards(): pl.pallas_call(give_kernel, out_shape=pltpu.HBM((block, width), bf16), in...  7.73 us
    pallas_call x1, Pallas kernels, shards(): pl.pallas_call(late_kernel, out_shape=pltpu.HBM((rows, width), bf16), in_...  6.73 us
    pallas_call x1, Pallas kernels, shards(): pl.pallas_call(early_kernel, out_shape=(pltpu.VMEM((rows, width), bf16),...  5.06 us
    pallas_call x1, Pallas kernels, shards(): pl.pallas_call(first_kernel, out_shape=tuple((pltpu.VMEM(w.shape, bf16) f...  4.75 us
  transfers between devices with their start and end apart: 5, of which 0 were waited for; matrix products, arithmetic and copies ran while one was open for 1% of the time, Pallas kernels for 12%

profile of v2, /device:TPU:1, one launch (start us, length us, event | category | flops | bytes accessed | tf_op | source)
XLA Modules:
  0.0 84.7 jit_solution(4530690900769866592)
XLA Ops:
  0.0 0.6 pad_add_fusion.place_ref
  0.6 7.7 %give.1.given_ref = bf16[128,768]{1,0:T(8,128)(2,1)} custom-call(s32[2]{0:T(128)} %pad_add_fusion.place_ref, bf16[2,128,768]{2,1,0:T(8,128)(2,1)} %act_ref.3), custom_call_target="tpu_custom_call" | custom-call | tf_op jit(solution)/shard_map/give/pallas_call | solution.py:253
  8.4 7.8 %collective-permute-start.2 = (bf16[128,768]{1,0:T(8,128)(2,1)}, bf16[128,768]{1,0:T(8,128)(2,1)S(1)}, u32[]{:S(2)}, u32[]{:S(2)}) collective-permute-start(bf16[128,768]{1,0:T(8,128)(2,1)} %give.1.given_ref), channel_id=1, source_target_pairs={{0,8},{8,0},{1,9},{9,1},{2,10},{10,2},{3,11},{11,3},{4,12},{12,4},... | collective-permute-start | bytes 589832 | tf_op jit(solution)/shard_map/ppermute | solution.py:261
  16.2 0.8 copy.8.contacts_ref
  17.0 0.0 copy-start
  17.0 0.7 copy-done
  17.6 0.0 copy-start.1
  17.6 0.7 copy-done.1
  18.3 4.7 %first.1 = (bf16[768,2304]{1,0:T(8,128)(2,1)S(1)}, bf16[768,768]{1,0:T(8,128)(2,1)S(1)}, bf16[768,2304]{1,0:T(8,128)(2,1)S(1)}, bf16[768,768]{1,0:T(8,128)(2,1)S...) custom-call(s32[2]{0:T(128)S(1)} %copy-done, ...), custom_call_target="tpu_custom_call" | custom-call | flops 452984832 | bytes 10000000 | tf_op jit(solution)/shard_map/first/pallas_call | solution.py:272
  23.0 1.3 %collective-permute-start = (bf16[128,768]{1,0:T(8,128)(2,1)}, bf16[128,768]{1,0:T(8,128)(2,1)S(1)}, u32[]{:S(2)}, u32[]{:S(2)}) collective-permute-start(bf16[128,768]{1,0:T(8,128)(2,1)} %get-tuple-element.27), channel_id=1, source_target_pairs={{0,16},{16,32},{32,48},{48,64},{64,80},{80,96},{96,112},{112,128},... | collective-permute-start | bytes 589832 | tf_op jit(solution)/shard_map/ppermute | solution.py:264
  24.3 3.8 %collective-permute-start.1 = (bf16[128,768]{1,0:T(8,128)(2,1)}, bf16[128,768]{1,0:T(8,128)(2,1)S(1)}, u32[]{:S(2)}, u32[]{:S(2)}) collective-permute-start(bf16[128,768]{1,0:T(8,128)(2,1)} %get-tuple-element.27), channel_id=1, source_target_pairs={{16,0},{32,16},{48,32},{64,48},{80,64},{96,80},{112,96},{128,112},... | collective-permute-start | bytes 589832 | tf_op jit(solution)/shard_map/ppermute | solution.py:265
  28.1 0.0 collective-permute-done.2.other_ref
  28.1 0.0 collective-permute-start.3
  28.1 4.8 %collective-permute-start.4 = (bf16[128,768]{1,0:T(8,128)(2,1)S(1)}, bf16[128,768]{1,0:T(8,128)(2,1)S(1)}, u32[]{:S(2)}, u32[]{:S(2)}) collective-permute-start(bf16[128,768]{1,0:T(8,128)(2,1)S(1)} %collective-permute-done.2.other_ref), channel_id=1, source_target_pairs={{16,0},{32,16},{48,32},{64,48},{80,64},{96,80},{112,96},{128,112},... | collective-permute-start | bytes 589832 | tf_op jit(solution)/shard_map/ppermute | solution.py:265
  32.9 0.0 collective-permute-done.before_ref
  32.9 0.0 collective-permute-done.1.after_ref
  32.9 5.1 %early.1 = (bf16[256,768]{1,0:T(8,128)(2,1)S(1)}, f32[256,768]{1,0:T(8,128)S(1)}, f32[256,768]{1,0:T(8,128)S(1)}, f32[256,768]{1,0:T(8,128)S(1)}) custom-call(f32[2,512]{1,0:T(2,128)S(1)} %get-tuple-element.23.bias_ref, bf16[128,768]{1,0:T(8,128)(2,1)S(1)} %get-tuple-element.24.query_in, bf16[128,768]{1,0:T(8,128)(2,1)S(1)} %get-tuple-element.25.keys_in, ...), custom_call_target="tpu_custom_call" | custom-call | flops 4000000000 | bytes 4000000 | tf_op jit(solution)/shard_map/early/pallas_call | solution.py:290
  38.0 0.0 collective-permute-done.3.before_ref
  38.0 0.0 collective-permute-done.4.after_ref
  38.0 6.7 %late.1 = bf16[256,768]{1,0:T(8,128)(2,1)} custom-call(s32[2]{0:T(128)S(1)} %copy-done, f32[2,256]{1,0:T(2,128)S(1)} %get-tuple-element.22.bias_ref, bf16[256,768]{1,0:T(8,128)(2,1)S(1)} %get-tuple-element.29.query_ref, f32[256,768]{1,0:T(8,128)S(1)} %get-tuple-element.30.sums_ref, f32[256,768]{1,0:T(8,128)S(1)} %get-tuple-element.31.tops_ref, ...), custom_call_target="tpu_custom_call" | custom-call | tf_op jit(solution)/shard_map/late/pallas_call | solution.py:300
  44.8 20.0 %all_to_all.23 = bf16[16,16,768]{2,1,0:T(8,128)(2,1)S(1)} all-to-all(bf16[16,16,768]{2,1,0:T(8,128)(2,1)} %bitcast.10), channel_id=1, replica_groups=mesh['pair'=16,'half'=2,'chip'=4,'core'=2] {'half','chip','core'}, dimensions={0} | all-to-all | bytes 786432 | tf_op jit(solution)/shard_map/all_to_all | solution.py:314
  64.7 4.7 %temporal.1 = bf16[256,768]{1,0:T(8,128)(2,1)} custom-call(bf16[256,768]{1,0:T(8,128)(2,1)S(1)} %bitcast.9, f32[16,128]{1,0:T(8,128)S(1)} %get-tuple-element.35.cos_ref, f32[16,128]{1,0:T(8,128)S(1)} %get-tuple-element.36.sin_ref, bf16[768,2304]{1,0:T(8,128)(2,1)S(1)} %get-tuple-element.37.qkv_ref, bf16[768,768]{1,0:T(8,128)(2,1)S(1)} %get-tuple-element.38.out_w_ref), custom_call_target="tpu_custom_call" | custom-call | tf_op jit(solution)/shard_map/temporal/pallas_call | solution.py:316
  69.4 14.4 %all_to_all.24 = bf16[16,16,768]{2,1,0:T(8,128)(2,1)S(1)} all-to-all(bf16[16,16,768]{2,1,0:T(8,128)(2,1)} %bitcast.12), channel_id=1, replica_groups=mesh['pair'=16,'half'=2,'chip'=4,'core'=2] {'chip','core'}, dimensions={0} | all-to-all | bytes 786432 | tf_op jit(solution)/shard_map/all_to_all | solution.py:325
  83.9 0.8 copy.9
Async XLA Ops:
  8.4 19.8 %collective-permute-start.2 = (bf16[128,768]{1,0:T(8,128)(2,1)}, bf16[128,768]{1,0:T(8,128)(2,1)S(1)}, u32[]{:S(2)}, u32[]{:S(2)}) collective-permute-start(bf16[128,768]{1,0:T(8,128)(2,1)} %give.1.given_ref), channel_id=1, source_target_pairs={{0,8},{8,0},{1,9},{9,1},{2,10},{10,2},{3,11},{11,3},{4,12},{12,4},... | collective-permute-start | bytes 589832 | tf_op jit(solution)/shard_map/ppermute | solution.py:261
  17.0 0.7 copy-start
  17.6 0.7 copy-start.1
  23.0 9.9 %collective-permute-start = (bf16[128,768]{1,0:T(8,128)(2,1)}, bf16[128,768]{1,0:T(8,128)(2,1)S(1)}, u32[]{:S(2)}, u32[]{:S(2)}) collective-permute-start(bf16[128,768]{1,0:T(8,128)(2,1)} %get-tuple-element.27), channel_id=1, source_target_pairs={{0,16},{16,32},{32,48},{48,64},{64,80},{80,96},{96,112},{112,128},... | collective-permute-start | bytes 589832 | tf_op jit(solution)/shard_map/ppermute | solution.py:264
  24.3 8.6 %collective-permute-start.1 = (bf16[128,768]{1,0:T(8,128)(2,1)}, bf16[128,768]{1,0:T(8,128)(2,1)S(1)}, u32[]{:S(2)}, u32[]{:S(2)}) collective-permute-start(bf16[128,768]{1,0:T(8,128)(2,1)} %get-tuple-element.27), channel_id=1, source_target_pairs={{16,0},{32,16},{48,32},{64,48},{80,64},{96,80},{112,96},{128,112},... | collective-permute-start | bytes 589832 | tf_op jit(solution)/shard_map/ppermute | solution.py:265
  28.1 9.9 %collective-permute-start.3 = (bf16[128,768]{1,0:T(8,128)(2,1)S(1)}, bf16[128,768]{1,0:T(8,128)(2,1)S(1)}, u32[]{:S(2)}, u32[]{:S(2)}) collective-permute-start(bf16[128,768]{1,0:T(8,128)(2,1)S(1)} %collective-permute-done.2.other_ref), channel_id=1, source_target_pairs={{0,16},{16,32},{32,48},{48,64},{64,80},{80,96},{96,112},{112,128},... | collective-permute-start | bytes 589832 | tf_op jit(solution)/shard_map/ppermute | solution.py:264
  28.1 9.9 %collective-permute-start.4 = (bf16[128,768]{1,0:T(8,128)(2,1)S(1)}, bf16[128,768]{1,0:T(8,128)(2,1)S(1)}, u32[]{:S(2)}, u32[]{:S(2)}) collective-permute-start(bf16[128,768]{1,0:T(8,128)(2,1)S(1)} %collective-permute-done.2.other_ref), channel_id=1, source_target_pairs={{16,0},{32,16},{48,32},{64,48},{80,64},{96,80},{112,96},{128,112},... | collective-permute-start | bytes 589832 | tf_op jit(solution)/shard_map/ppermute | solution.py:265

commit v3 on v2

--- a/solution.py
+++ b/solution.py
@@ -63,14 +63,14 @@
     )
 
 
-def give_kernel(place_ref, act_ref, given_ref, semaphore):
-    move = pltpu.make_async_copy(act_ref.at[1 - place_ref[0]], given_ref, semaphore)
+def give_kernel(act_ref, given_ref, semaphore):
+    move = pltpu.make_async_copy(act_ref.at[1 - lax.axis_index("half")], given_ref, semaphore)
     move.start()
     move.wait()
 
 
-def contact_biases(place_ref, contacts_ref, early_ref, late_ref):
-    half, pair = place_ref[0], place_ref[1]
+def contact_biases(contacts_ref, early_ref, late_ref):
+    half, pair = lax.axis_index("half"), lax.axis_index("pair")
     block = early_ref.shape[1] // 4
     to_other = 1 - 2 * half
     for row, (parity, moves) in enumerate(
@@ -105,11 +105,11 @@
 
 
 def first_kernel(
-    place_ref, contacts_ref, frame_ref, given_ref, act_ref, qkv_hbm, out_hbm, time_qkv_hbm, time_out_hbm,
+    contacts_ref, frame_ref, given_ref, act_ref, qkv_hbm, out_hbm, time_qkv_hbm, time_out_hbm,
     qkv_ref, out_ref, time_qkv_ref, time_out_ref, normed_ref, base_ref, query_ref, keys_ref, values_ref,
-    early_ref, late_ref, cos_ref, sin_ref, sent, semaphores,
+    early_ref, late_ref, cos_ref, sin_ref, semaphores,
 ):
-    half = place_ref[0]
+    half = lax.axis_index("half")
     width = base_ref.shape[1]
     own = pltpu.make_async_copy(act_ref.at[half], base_ref, semaphores.at[0])
     own.start()
@@ -121,16 +121,13 @@
         loads[-1].start()
     own.wait()
     normed = unit_rows(base_ref[...])
-    sent[...] = normed
-    store = pltpu.make_async_copy(sent, normed_ref, semaphores.at[5])
-    store.start()
+    normed_ref[...] = normed
     loads[0].wait()
     query_ref[...] = (dot(normed, qkv_ref[:, :width]) * SCALE).astype(jnp.bfloat16)
     keys_ref[...] = dot(normed, qkv_ref[:, width : 2 * width]).astype(jnp.bfloat16)
     values_ref[...] = dot(normed, qkv_ref[:, 2 * width :]).astype(jnp.bfloat16)
-    contact_biases(place_ref, contacts_ref, early_ref, late_ref)
+    contact_biases(contacts_ref, early_ref, late_ref)
     rotation_tables(frame_ref, cos_ref, sin_ref)
-    store.wait()
     for load in loads[1:]:
         load.wait()
 
@@ -157,10 +154,10 @@
 
 
 def late_kernel(
-    place_ref, bias_ref, query_ref, sums_ref, tops_ref, totals_ref, before_ref, after_ref,
+    bias_ref, query_ref, sums_ref, tops_ref, totals_ref, before_ref, after_ref,
     base_ref, other_ref, qkv_ref, out_ref, hidden_ref, keys, values, mix, hidden, semaphore,
 ):
-    half = place_ref[0]
+    half = lax.axis_index("half")
     block, width = other_ref.shape
     tiles = unit_rows(jnp.concatenate([before_ref[...], after_ref[...]], axis=0))
     keys[...] = dot(tiles, qkv_ref[:, width : 2 * width]).astype(jnp.bfloat16)
@@ -241,9 +238,6 @@
 def shards(activations, contacts, frame_index, spatial_qkv, spatial_out, time_qkv, time_out):
     frames_dev, block, width = activations.shape
     pairs = lax.axis_size("pair")
-    pair = lax.axis_index("pair")
-    half = lax.axis_index("half")
-    place = jnp.stack([half, pair]).astype(jnp.int32)
     activations, spatial_qkv, spatial_out, time_qkv, time_out = (
         pltpu.with_memory_space_constraint(x, pltpu.HBM)
         for x in (activations, spatial_qkv, spatial_out, time_qkv, time_out)
@@ -252,12 +246,12 @@
     bf16, f32 = jnp.bfloat16, jnp.float32
     given = pl.pallas_call(
         give_kernel,
-        out_shape=pltpu.HBM((block, width), bf16),
-        in_specs=[SMEM, HBM],
-        out_specs=HBM,
+        out_shape=pltpu.VMEM((block, width), bf16),
+        in_specs=[HBM],
+        out_specs=VMEM,
         scratch_shapes=[pltpu.SemaphoreType.DMA],
         name="give",
-    )(place, activations)
+    )(activations)
     other = lax.ppermute(given, "half", [(0, 1), (1, 0)])
 
     def from_neighbours(tile):
@@ -272,16 +266,16 @@
     *weights, normed, base, query, keys, values, early_bias, late_bias, cosine, sine = pl.pallas_call(
         first_kernel,
         out_shape=tuple(pltpu.VMEM(w.shape, bf16) for w in weights)
-        + (pltpu.HBM((block, width), bf16),)
+        + (tile_in_vmem,)
         + (tile_in_vmem,) * 4
         + (pltpu.VMEM((2, 4 * block), f32), pltpu.VMEM((2, 2 * block), f32), table, table),
-        in_specs=[SMEM] * 3 + [HBM] * 6,
-        out_specs=(VMEM,) * 4 + (HBM,) + (VMEM,) * 8,
-        scratch_shapes=[tile_in_vmem, pltpu.SemaphoreType.DMA((6,))],
+        in_specs=[SMEM] * 2 + [VMEM] + [HBM] * 5,
+        out_specs=(VMEM,) * 13,
+        scratch_shapes=[pltpu.SemaphoreType.DMA((5,))],
         compiler_params=LIMIT,
         cost_estimate=pl.CostEstimate(flops=2 * block * width * 3 * width, bytes_accessed=10_000_000, transcendentals=0),
         name="first",
-    )(place, contacts, frame_index, pltpu.with_memory_space_constraint(given, pltpu.HBM), activations, *weights)
+    )(contacts, frame_index, given, activations, *weights)
     spatial_qkv, spatial_out, time_qkv, time_out = weights
     kept_before, kept_after = from_neighbours(normed)
     other_before, other_after = from_neighbours(other)
@@ -300,13 +294,13 @@
     hidden = pl.pallas_call(
         late_kernel,
         out_shape=pltpu.HBM((rows, width), bf16),
-        in_specs=[SMEM] + [VMEM] * 11,
+        in_specs=[VMEM] * 11,
         out_specs=HBM,
         scratch_shapes=[pltpu.VMEM((rows, width), bf16)] * 4 + [pltpu.SemaphoreType.DMA],
         compiler_params=LIMIT,
         name="late",
     )(
-        place, late_bias, query, sums, tops, totals, other_before, other_after,
+        late_bias, query, sums, tops, totals, other_before, other_after,
         base, other, spatial_qkv, spatial_out,
     )
 

time: 85 us -> 76.8 us (0.904)
  Pallas kernels: 29 us -> 21.6 us
    pallas_call x1, Pallas kernels: 7.73 us -> 0.93 us  [shards(): pl.pallas_call(give_kernel, out_shape=pltpu.VMEM((block, width), bf16), i...]
    unnamed x5 -> x3, local copies, waits for them, and re-layouts: 2.07 us -> 1.42 us
  transfers between devices with their start and end apart: 5 -> 5, of which waited for: 0 -> 0; matrix products, arithmetic and copies ran while one was open for 1% -> 1% of each run, Pallas kernels for 12% -> 13%
where the time goes in v3:
time: 76.8 us; the launch traced here: 76.5 us
  blocking collectives  34.9 us (45%)
  Pallas kernels  21.6 us (28%)
  starting transfers between devices  17.7 us (23%)
  local copies, waits for them, and re-layouts  2.19 us (3%)
    all_to_all x1, blocking collectives, shards(): lax.all_to_all(hidden.reshape(members, group, width), COLUMN, 0, 0, tiled...  20.5 us
    all_to_all x1, blocking collectives, shards(): lax.all_to_all(layer.reshape(members, group, width), ('chip', 'core'), 0,...  14.4 us
    ppermute x2, starting transfers between devices, from_neighbours(): lax.ppermute(tile, 'pair', [((i + 1) % pairs, i) for i in range(pairs)])  8.59 us
    ppermute x1, starting transfers between devices, shards(): other = lax.ppermute(given, 'half', [(0, 1), (1, 0)])  7.83 us
    pallas_call x1, Pallas kernels, shards(): pl.pallas_call(late_kernel, out_shape=pltpu.HBM((rows, width), bf16), in_...  6.2 us
    pallas_call x1, Pallas kernels, shards(): pl.pallas_call(early_kernel, out_shape=(pltpu.VMEM((rows, width), bf16),...  5.03 us
    pallas_call x1, Pallas kernels, shards(): pl.pallas_call(time_kernel, out_shape=pltpu.HBM((rows, width), bf16), in_...  4.77 us
    pallas_call x1, Pallas kernels, shards(): pl.pallas_call(first_kernel, out_shape=tuple((pltpu.VMEM(w.shape, bf16) f...  4.67 us
  transfers between devices with their start and end apart: 5, of which 0 were waited for; matrix products, arithmetic and copies ran while one was open for 1% of the time, Pallas kernels for 13%

profile of v3, /device:TPU:1, one launch (start us, length us, event | category | flops | bytes accessed | tf_op | source)
XLA Modules:
  0.0 76.5 jit_solution(10286279248719616207)
XLA Ops:
  0.0 0.9 %give.1.given_ref = bf16[128,768]{1,0:T(8,128)(2,1)S(1)} custom-call(bf16[2,128,768]{2,1,0:T(8,128)(2,1)} %act_ref.3), custom_call_target="tpu_custom_call" | custom-call | tf_op jit(solution)/shard_map/give/pallas_call | solution.py:247
  0.9 7.8 %collective-permute-start.2 = (bf16[128,768]{1,0:T(8,128)(2,1)S(1)}, bf16[128,768]{1,0:T(8,128)(2,1)S(1)}, u32[]{:S(2)}, u32[]{:S(2)}) collective-permute-start(bf16[128,768]{1,0:T(8,128)(2,1)S(1)} %give.1.given_ref), channel_id=1, source_target_pairs={{0,8},{8,0},{1,9},{9,1},{2,10},{10,2},{3,11},{11,3},{4,12},{12,4},... | collective-permute-start | bytes 589832 | tf_op jit(solution)/shard_map/ppermute | solution.py:255
  8.8 0.8 %copy.8.contacts_ref = s32[32,5]{1,0:T(8,128)S(1)} copy(s32[32,5]{0,1:T(8,128)} %param.8) | data formatting | bytes 1280 | tf_op args[1]
  9.5 0.0 copy-start
  9.5 0.7 copy-done
  10.2 4.7 %first.1 = (bf16[768,2304]{1,0:T(8,128)(2,1)S(1)}, bf16[768,768]{1,0:T(8,128)(2,1)S(1)}, bf16[768,2304]{1,0:T(8,128)(2,1)S(1)}, bf16[768,768]{1,0:T(8,128)(2,1)S...) custom-call(s32[32,5]{1,0:T(8,128)S(1)} %copy.8.contacts_ref, ...), custom_call_target="tpu_custom_call" | custom-call | flops 452984832 | bytes 10000000 | tf_op jit(solution)/shard_map/first/pallas_call | solution.py:266
  14.9 1.3 %collective-permute-start = (bf16[128,768]{1,0:T(8,128)(2,1)S(1)}, bf16[128,768]{1,0:T(8,128)(2,1)S(1)}, u32[]{:S(2)}, u32[]{:S(2)}) collective-permute-start(bf16[128,768]{1,0:T(8,128)(2,1)S(1)} %get-tuple-element.27), channel_id=1, source_target_pairs={{0,16},{16,32},{32,48},{48,64},{64,80},{80,96},{96,112},{112,128},... | collective-permute-start | bytes 589832 | tf_op jit(solution)/shard_map/ppermute | solution.py:258
  16.2 3.8 %collective-permute-start.1 = (bf16[128,768]{1,0:T(8,128)(2,1)S(1)}, bf16[128,768]{1,0:T(8,128)(2,1)S(1)}, u32[]{:S(2)}, u32[]{:S(2)}) collective-permute-start(bf16[128,768]{1,0:T(8,128)(2,1)S(1)} %get-tuple-element.27), channel_id=1, source_target_pairs={{16,0},{32,16},{48,32},{64,48},{80,64},{96,80},{112,96},{128,112},... | collective-permute-start | bytes 589832 | tf_op jit(solution)/shard_map/ppermute | solution.py:259
  20.0 0.0 collective-permute-done.2.other_ref
  20.0 0.0 collective-permute-start.3
  20.0 4.8 %collective-permute-start.4 = (bf16[128,768]{1,0:T(8,128)(2,1)S(1)}, bf16[128,768]{1,0:T(8,128)(2,1)S(1)}, u32[]{:S(2)}, u32[]{:S(2)}) collective-permute-start(bf16[128,768]{1,0:T(8,128)(2,1)S(1)} %collective-permute-done.2.other_ref), channel_id=1, source_target_pairs={{16,0},{32,16},{48,32},{64,48},{80,64},{96,80},{112,96},{128,112},... | collective-permute-start | bytes 589832 | tf_op jit(solution)/shard_map/ppermute | solution.py:259
  24.8 0.0 collective-permute-done.before_ref
  24.8 0.0 collective-permute-done.1.after_ref
  24.8 5.0 %early.1 = (bf16[256,768]{1,0:T(8,128)(2,1)S(1)}, f32[256,768]{1,0:T(8,128)S(1)}, f32[256,768]{1,0:T(8,128)S(1)}, f32[256,768]{1,0:T(8,128)S(1)}) custom-call(f32[2,512]{1,0:T(2,128)S(1)} %get-tuple-element.23.bias_ref, bf16[128,768]{1,0:T(8,128)(2,1)S(1)} %get-tuple-element.24.query_in, bf16[128,768]{1,0:T(8,128)(2,1)S(1)} %get-tuple-element.25.keys_in, ...), custom_call_target="tpu_custom_call" | custom-call | flops 4000000000 | bytes 4000000 | tf_op jit(solution)/shard_map/early/pallas_call | solution.py:284
  29.8 0.0 collective-permute-done.3.before_ref
  29.8 0.0 collective-permute-done.4.after_ref
  29.8 6.2 %late.1 = bf16[256,768]{1,0:T(8,128)(2,1)} custom-call(f32[2,256]{1,0:T(2,128)S(1)} %get-tuple-element.22.bias_ref, bf16[256,768]{1,0:T(8,128)(2,1)S(1)} %get-tuple-element.29.query_ref, f32[256,768]{1,0:T(8,128)S(1)} %get-tuple-element.30.sums_ref, f32[256,768]{1,0:T(8,128)S(1)} %get-tuple-element.31.tops_ref, f32[256,768]{1,0:T(8,128)S(1)} %get-tuple-element.32.totals_ref, ...), custom_call_target="tpu_custom_call" | custom-call | tf_op jit(solution)/shard_map/late/pallas_call | solution.py:294
  36.0 20.5 %all_to_all.23 = bf16[16,16,768]{2,1,0:T(8,128)(2,1)S(1)} all-to-all(bf16[16,16,768]{2,1,0:T(8,128)(2,1)} %bitcast.8), channel_id=1, replica_groups=mesh['pair'=16,'half'=2,'chip'=4,'core'=2] {'half','chip','core'}, dimensions={0} | all-to-all | bytes 786432 | tf_op jit(solution)/shard_map/all_to_all | solution.py:308
  56.5 4.8 %temporal.1 = bf16[256,768]{1,0:T(8,128)(2,1)} custom-call(bf16[256,768]{1,0:T(8,128)(2,1)S(1)} %bitcast.7, f32[16,128]{1,0:T(8,128)S(1)} %get-tuple-element.35.cos_ref, f32[16,128]{1,0:T(8,128)S(1)} %get-tuple-element.36.sin_ref, bf16[768,2304]{1,0:T(8,128)(2,1)S(1)} %get-tuple-element.37.qkv_ref, bf16[768,768]{1,0:T(8,128)(2,1)S(1)} %get-tuple-element.38.out_w_ref), custom_call_target="tpu_custom_call" | custom-call | tf_op jit(solution)/shard_map/temporal/pallas_call | solution.py:310
  61.3 14.4 %all_to_all.24 = bf16[16,16,768]{2,1,0:T(8,128)(2,1)S(1)} all-to-all(bf16[16,16,768]{2,1,0:T(8,128)(2,1)} %bitcast.10), channel_id=1, replica_groups=mesh['pair'=16,'half'=2,'chip'=4,'core'=2] {'chip','core'}, dimensions={0} | all-to-all | bytes 786432 | tf_op jit(solution)/shard_map/all_to_all | solution.py:319
  75.7 0.8 %copy.9 = bf16[8,2,16,768]{3,2,0,1:T(8,128)(2,1)} copy(bf16[8,2,16,768]{3,2,1,0:T(8,128)(2,1)S(1)} %bitcast.9) | data formatting | bytes 786432 | tf_op jit(solution)/shard_map/all_to_all | solution.py:319
Async XLA Ops:
  0.9 19.0 %collective-permute-start.2 = (bf16[128,768]{1,0:T(8,128)(2,1)S(1)}, bf16[128,768]{1,0:T(8,128)(2,1)S(1)}, u32[]{:S(2)}, u32[]{:S(2)}) collective-permute-start(bf16[128,768]{1,0:T(8,128)(2,1)S(1)} %give.1.given_ref), channel_id=1, source_target_pairs={{0,8},{8,0},{1,9},{9,1},{2,10},{10,2},{3,11},{11,3},{4,12},{12,4},... | collective-permute-start | bytes 589832 | tf_op jit(solution)/shard_map/ppermute | solution.py:255
  9.5 0.7 copy-start
  14.9 9.9 %collective-permute-start = (bf16[128,768]{1,0:T(8,128)(2,1)S(1)}, bf16[128,768]{1,0:T(8,128)(2,1)S(1)}, u32[]{:S(2)}, u32[]{:S(2)}) collective-permute-start(bf16[128,768]{1,0:T(8,128)(2,1)S(1)} %get-tuple-element.27), channel_id=1, source_target_pairs={{0,16},{16,32},{32,48},{48,64},{64,80},{80,96},{96,112},{112,128},... | collective-permute-start | bytes 589832 | tf_op jit(solution)/shard_map/ppermute | solution.py:258
  16.2 8.6 %collective-permute-start.1 = (bf16[128,768]{1,0:T(8,128)(2,1)S(1)}, bf16[128,768]{1,0:T(8,128)(2,1)S(1)}, u32[]{:S(2)}, u32[]{:S(2)}) collective-permute-start(bf16[128,768]{1,0:T(8,128)(2,1)S(1)} %get-tuple-element.27), channel_id=1, source_target_pairs={{16,0},{32,16},{48,32},{64,48},{80,64},{96,80},{112,96},{128,112},... | collective-permute-start | bytes 589832 | tf_op jit(solution)/shard_map/ppermute | solution.py:259
  20.0 9.8 %collective-permute-start.3 = (bf16[128,768]{1,0:T(8,128)(2,1)S(1)}, bf16[128,768]{1,0:T(8,128)(2,1)S(1)}, u32[]{:S(2)}, u32[]{:S(2)}) collective-permute-start(bf16[128,768]{1,0:T(8,128)(2,1)S(1)} %collective-permute-done.2.other_ref), channel_id=1, source_target_pairs={{0,16},{16,32},{32,48},{48,64},{64,80},{80,96},{96,112},{112,128},... | collective-permute-start | bytes 589832 | tf_op jit(solution)/shard_map/ppermute | solution.py:258
  20.0 9.8 %collective-permute-start.4 = (bf16[128,768]{1,0:T(8,128)(2,1)S(1)}, bf16[128,768]{1,0:T(8,128)(2,1)S(1)}, u32[]{:S(2)}, u32[]{:S(2)}) collective-permute-start(bf16[128,768]{1,0:T(8,128)(2,1)S(1)} %collective-permute-done.2.other_ref), channel_id=1, source_target_pairs={{16,0},{32,16},{48,32},{64,48},{80,64},{96,80},{112,96},{128,112},... | collective-permute-start | bytes 589832 | tf_op jit(solution)/shard_map/ppermute | solution.py:259

commit v4 on v3

--- a/solution.py
+++ b/solution.py
@@ -36,31 +36,40 @@
     )
 
 
-def lanes_of(query, head):
-    lane = lax.broadcasted_iota(jnp.int32, query.shape, 1)
-    inside = (lane >= HEAD) if head else (lane < HEAD)
-    return jnp.where(inside, query, jnp.zeros_like(query))
-
-
-def side_by_side(first, second, rows):
+def by_head(pair_query):
+    lane = lax.broadcasted_iota(jnp.int32, pair_query.shape, 1)
+    nothing = jnp.zeros_like(pair_query)
+    return jnp.concatenate(
+        [jnp.where(lane < HEAD, pair_query, nothing), jnp.where(lane < HEAD, nothing, pair_query)], axis=0
+    )
+
+
+def side_by_side(stacked):
+    rows = stacked.shape[0] // 2
     lane = lax.broadcasted_iota(jnp.int32, (rows, PAIR), 1)
-    return jnp.where(lane < HEAD, first, second)
-
-
-def attend(query, keys, values, biases, head, floor=None):
-    scores = dot_rows(lanes_of(query, head), keys) + biases
-    top = jnp.max(scores, axis=-1, keepdims=True)
-    if floor is not None:
-        top = jnp.maximum(top, floor)
-    expo = jnp.exp2(scores - top)
-    total = jnp.sum(expo, axis=-1, keepdims=True)
-    return dot(expo.astype(jnp.bfloat16), values), top, total
+    return jnp.where(lane < HEAD, stacked[:rows, :PAIR], stacked[rows:, :PAIR])
 
 
 def two_rows(bias_ref, block):
-    return jnp.concatenate(
-        [jnp.broadcast_to(bias_ref[y : y + 1, :], (block, bias_ref.shape[1])) for y in range(2)], axis=0
-    )
+    halves = [jnp.broadcast_to(bias_ref[y : y + 1, :], (block, bias_ref.shape[1])) for y in range(2)]
+    return jnp.concatenate(halves * 2, axis=0)
+
+
+def attend(stacked_query, keys, values, pairs, biases, finish, floors=None):
+    width = keys.shape[0]
+
+    def scores_of(pair):
+        return dot_rows(stacked_query[pair], keys[:, pair * PAIR : (pair + 1) * PAIR]) + biases
+
+    scores = scores_of(0)
+    for pair in range(pairs):
+        ahead = scores_of(pair + 1) if pair + 1 < pairs else None
+        top = jnp.broadcast_to(jnp.max(scores, axis=-1, keepdims=True), (scores.shape[0], PAIR))
+        if floors is not None:
+            top = jnp.maximum(top, floors[pair])
+        expo = jnp.exp2(scores - jnp.concatenate([top] * (width // PAIR), axis=1)).astype(jnp.bfloat16)
+        finish(pair, top, dot(expo, values[pair]))
+        scores = ahead
 
 
 def give_kernel(act_ref, given_ref, semaphore):
@@ -137,20 +146,27 @@
     query_ref, sums_ref, tops_ref, totals_ref, keys, values,
 ):
     block, width = other_ref.shape
-    query_ref[:block, :] = query_in[...]
+    pairs = width // PAIR
     normed = unit_rows(other_ref[...])
-    query_ref[block:, :] = (dot(normed, qkv_ref[:, :width]) * SCALE).astype(jnp.bfloat16)
+    query = (dot(normed, qkv_ref[:, :width]) * SCALE).astype(jnp.bfloat16)
     keys[:block, :] = keys_in[...]
-    values[:block, :] = values_in[...]
     tiles = jnp.concatenate([before_ref[...], after_ref[...], normed], axis=0)
     keys[block:, :] = dot(tiles, qkv_ref[:, width : 2 * width]).astype(jnp.bfloat16)
-    values[block:, :] = dot(tiles, qkv_ref[:, 2 * width :]).astype(jnp.bfloat16)
-    biases = two_rows(bias_ref, block)
-    for pair in range(width // PAIR):
+    fresh = dot(tiles, qkv_ref[:, 2 * width :]).astype(jnp.bfloat16)
+    for pair in range(pairs):
         at = slice(pair * PAIR, (pair + 1) * PAIR)
-        parts = [attend(query_ref[:, at], keys[:, at], values[:, at], biases, head) for head in range(2)]
-        for ref, piece in ((sums_ref, 0), (tops_ref, 1), (totals_ref, 2)):
-            ref[:, at] = side_by_side(parts[0][piece], parts[1][piece], 2 * block)
+        values[pair, :block, :PAIR] = values_in[:, at]
+        values[pair, block:, :PAIR] = fresh[:, at]
+        values[pair, :, PAIR:] = jnp.ones((4 * block, PAIR), jnp.bfloat16)
+        query_ref[pair] = by_head(jnp.concatenate([query_in[:, at], query[:, at]], axis=0))
+
+    def finish(pair, top, product):
+        at = slice(pair * PAIR, (pair + 1) * PAIR)
+        tops_ref[pair] = top
+        sums_ref[:, at] = side_by_side(product)
+        totals_ref[:, at] = side_by_side(product[:, PAIR:])
+
+    attend(query_ref, keys, values, pairs, two_rows(bias_ref, block), finish)
 
 
 def late_kernel(
@@ -159,24 +175,21 @@
 ):
     half = lax.axis_index("half")
     block, width = other_ref.shape
+    pairs = width // PAIR
     tiles = unit_rows(jnp.concatenate([before_ref[...], after_ref[...]], axis=0))
     keys[...] = dot(tiles, qkv_ref[:, width : 2 * width]).astype(jnp.bfloat16)
-    values[...] = dot(tiles, qkv_ref[:, 2 * width :]).astype(jnp.bfloat16)
-    biases = two_rows(bias_ref, block)
-    for pair in range(width // PAIR):
+    fresh = dot(tiles, qkv_ref[:, 2 * width :]).astype(jnp.bfloat16)
+    for pair in range(pairs):
+        values[pair, :, :PAIR] = fresh[:, pair * PAIR : (pair + 1) * PAIR]
+        values[pair, :, PAIR:] = jnp.ones((2 * block, PAIR), jnp.bfloat16)
+
+    def finish(pair, top, product):
         at = slice(pair * PAIR, (pair + 1) * PAIR)
-        floors = tops_ref[:, at]
-        parts = [
-            attend(
-                query_ref[:, at], keys[:, at], values[:, at], biases, head,
-                floors[:, head * HEAD : head * HEAD + 1],
-            )
-            for head in range(2)
-        ]
-        late = [side_by_side(parts[0][piece], parts[1][piece], 2 * block) for piece in range(3)]
-        share = jnp.exp2(floors - late[1])
-        total = totals_ref[:, at] * share + late[2]
-        mix[:, at] = ((sums_ref[:, at] * share + late[0]) / total).astype(jnp.bfloat16)
+        share = side_by_side(jnp.exp2(tops_ref[pair] - top))
+        total = totals_ref[:, at] * share + side_by_side(product[:, PAIR:])
+        mix[:, at] = ((sums_ref[:, at] * share + side_by_side(product)) / total).astype(jnp.bfloat16)
+
+    attend(query_ref, keys, values, pairs, two_rows(bias_ref, block), finish, tops_ref)
     added = dot(mix[...], out_ref[...])
     here = pl.ds(pl.multiple_of(half * block, block), block)
     there = pl.ds(pl.multiple_of((1 - half) * block, block), block)
@@ -210,21 +223,23 @@
         )
         return entries * cosine + swapped * sine
 
-    projected = dot(normed, qkv_ref[:, : 2 * width])
-    for pair in range(width // PAIR):
+    pairs = width // PAIR
+    projected = dot(normed, qkv_ref[...])
+    for pair in range(pairs):
         at = slice(pair * PAIR, (pair + 1) * PAIR)
-        query[:, at] = (rotate(projected[:, at]) * SCALE).astype(jnp.bfloat16)
+        query[pair] = by_head((rotate(projected[:, at]) * SCALE).astype(jnp.bfloat16))
         keys[:, at] = rotate(projected[:, width + pair * PAIR : width + (pair + 1) * PAIR]).astype(jnp.bfloat16)
-    values[...] = dot(normed, qkv_ref[:, 2 * width :]).astype(jnp.bfloat16)
-    row = lax.broadcasted_iota(jnp.int32, (rows, rows), 0)
-    column = lax.broadcasted_iota(jnp.int32, (rows, rows), 1)
+        values[pair, :, :PAIR] = projected[:, 2 * width + pair * PAIR : 2 * width + (pair + 1) * PAIR].astype(jnp.bfloat16)
+        values[pair, :, PAIR:] = jnp.ones((rows, PAIR), jnp.bfloat16)
+    row = lax.broadcasted_iota(jnp.int32, (2 * rows, rows), 0)
+    column = lax.broadcasted_iota(jnp.int32, (2 * rows, rows), 1)
     biases = jnp.where(row % group == column % group, 0.0, EXCLUDED)
-    for pair in range(width // PAIR):
-        at = slice(pair * PAIR, (pair + 1) * PAIR)
-        parts = [attend(query[:, at], keys[:, at], values[:, at], biases, head) for head in range(2)]
-        mix[:, at] = side_by_side(
-            parts[0][0] / parts[0][2], parts[1][0] / parts[1][2], rows
-        ).astype(jnp.bfloat16)
+
+    def finish(pair, top, product):
+        mixed = side_by_side(product) / side_by_side(product[:, PAIR:])
+        mix[:, pair * PAIR : (pair + 1) * PAIR] = mixed.astype(jnp.bfloat16)
+
+    attend(query, keys, values, pairs, biases, finish)
     added = (hidden_ref[...].astype(jnp.float32) + dot(mix[...], out_w_ref[...])).astype(jnp.bfloat16)
     per_half = frames // 2
     for j in range(frames):
@@ -281,12 +296,16 @@
     other_before, other_after = from_neighbours(other)
 
     wide = pltpu.VMEM((rows, width), f32)
+    tops_shape = pltpu.VMEM((width // PAIR, 2 * rows, PAIR), f32)
     query, sums, tops, totals = pl.pallas_call(
         early_kernel,
-        out_shape=(pltpu.VMEM((rows, width), bf16), wide, wide, wide),
+        out_shape=(pltpu.VMEM((width // PAIR, 2 * rows, PAIR), bf16), wide, tops_shape, wide),
         in_specs=[VMEM] * 8,
         out_specs=(VMEM,) * 4,
-        scratch_shapes=[pltpu.VMEM((4 * block, width), bf16)] * 2,
+        scratch_shapes=[
+            pltpu.VMEM((4 * block, width), bf16),
+            pltpu.VMEM((width // PAIR, 4 * block, 2 * PAIR), bf16),
+        ],
         compiler_params=LIMIT,
         cost_estimate=pl.CostEstimate(flops=4_000_000_000, bytes_accessed=4_000_000, transcendentals=2_000_000),
         name="early",
@@ -296,7 +315,13 @@
         out_shape=pltpu.HBM((rows, width), bf16),
         in_specs=[VMEM] * 11,
         out_specs=HBM,
-        scratch_shapes=[pltpu.VMEM((rows, width), bf16)] * 4 + [pltpu.SemaphoreType.DMA],
+        scratch_shapes=[
+            pltpu.VMEM((rows, width), bf16),
+            pltpu.VMEM((width // PAIR, rows, 2 * PAIR), bf16),
+            pltpu.VMEM((rows, width), bf16),
+            pltpu.VMEM((rows, width), bf16),
+            pltpu.SemaphoreType.DMA,
+        ],
         compiler_params=LIMIT,
         name="late",
     )(
@@ -312,7 +337,14 @@
         out_shape=pltpu.HBM((rows, width), bf16),
         in_specs=[VMEM] * 5,
         out_specs=HBM,
-        scratch_shapes=[pltpu.VMEM((rows, width), bf16)] * 5 + [pltpu.SemaphoreType.DMA],
+        scratch_shapes=[
+            pltpu.VMEM((width // PAIR, 2 * rows, PAIR), bf16),
+            pltpu.VMEM((rows, width), bf16),
+            pltpu.VMEM((width // PAIR, rows, 2 * PAIR), bf16),
+            pltpu.VMEM((rows, width), bf16),
+            pltpu.VMEM((rows, width), bf16),
+            pltpu.SemaphoreType.DMA,
+        ],
         compiler_params=LIMIT,
         name="temporal",
     )(hidden.reshape(rows, width), cosine, sine, time_qkv, time_out)

time: 76.8 us -> 72.5 us (0.944)
  Pallas kernels: 21.6 us -> 17 us
    pallas_call x1, Pallas kernels: 6.2 us -> 3.29 us  [shards(): pl.pallas_call(late_kernel, out_shape=pltpu.HBM((rows, width), bf16), in_...]
    pallas_call x1, Pallas kernels: 5.03 us -> 3.35 us  [shards(): pl.pallas_call(early_kernel, out_shape=(pltpu.VMEM((width // PAIR, 2 * ro...]
  transfers between devices with their start and end apart: 5 -> 5, of which waited for: 0 -> 1; matrix products, arithmetic and copies ran while one was open for 1% -> 1% of each run, Pallas kernels for 13% -> 11%
where the time goes in v4:
time: 72.5 us; the launch traced here: 72.2 us
  blocking collectives  34.9 us (48%)
  starting transfers between devices  17.7 us (24%)
  Pallas kernels  17 us (23%)
  local copies, waits for them, and re-layouts  2.19 us (3%)
    all_to_all x1, blocking collectives, shards(): lax.all_to_all(hidden.reshape(members, group, width), COLUMN, 0, 0, tiled...  20.5 us
    all_to_all x1, blocking collectives, shards(): lax.all_to_all(layer.reshape(members, group, width), ('chip', 'core'), 0,...  14.4 us
    ppermute x2, starting transfers between devices, from_neighbours(): lax.ppermute(tile, 'pair', [((i + 1) % pairs, i) for i in range(pairs)])  8.59 us
    ppermute x1, starting transfers between devices, shards(): other = lax.ppermute(given, 'half', [(0, 1), (1, 0)])  7.83 us
    pallas_call x1, Pallas kernels, shards(): pl.pallas_call(time_kernel, out_shape=pltpu.HBM((rows, width), bf16), in_...  4.76 us
    pallas_call x1, Pallas kernels, shards(): pl.pallas_call(first_kernel, out_shape=tuple((pltpu.VMEM(w.shape, bf16) f...  4.67 us
    pallas_call x1, Pallas kernels, shards(): pl.pallas_call(early_kernel, out_shape=(pltpu.VMEM((width // PAIR, 2 * ro...  3.35 us
    pallas_call x1, Pallas kernels, shards(): pl.pallas_call(late_kernel, out_shape=pltpu.HBM((rows, width), bf16), in_...  3.29 us
  transfers between devices with their start and end apart: 5, of which 1 were waited for; matrix products, arithmetic and copies ran while one was open for 1% of the time, Pallas kernels for 11%

profile of v4, /device:TPU:1, one launch (start us, length us, event | category | flops | bytes accessed | tf_op | source)
XLA Modules:
  0.0 72.2 jit_solution(16481370420235560189)
XLA Ops:
  0.0 0.9 %give.1.given_ref = bf16[128,768]{1,0:T(8,128)(2,1)S(1)} custom-call(bf16[2,128,768]{2,1,0:T(8,128)(2,1)} %act_ref.3), custom_call_target="tpu_custom_call" | custom-call | tf_op jit(solution)/shard_map/give/pallas_call | solution.py:262
  0.9 7.8 %collective-permute-start.2 = (bf16[128,768]{1,0:T(8,128)(2,1)S(1)}, bf16[128,768]{1,0:T(8,128)(2,1)S(1)}, u32[]{:S(2)}, u32[]{:S(2)}) collective-permute-start(bf16[128,768]{1,0:T(8,128)(2,1)S(1)} %give.1.given_ref), channel_id=1, source_target_pairs={{0,8},{8,0},{1,9},{9,1},{2,10},{10,2},{3,11},{11,3},{4,12},{12,4},... | collective-permute-start | bytes 589832 | tf_op jit(solution)/shard_map/ppermute | solution.py:270
  8.8 0.8 %copy.8.contacts_ref = s32[32,5]{1,0:T(8,128)S(1)} copy(s32[32,5]{0,1:T(8,128)} %param.8) | data formatting | bytes 1280 | tf_op args[1]
  9.5 0.0 copy-start
  9.5 0.7 copy-done
  10.2 4.7 %first.1 = (bf16[768,2304]{1,0:T(8,128)(2,1)S(1)}, bf16[768,768]{1,0:T(8,128)(2,1)S(1)}, bf16[768,2304]{1,0:T(8,128)(2,1)S(1)}, bf16[768,768]{1,0:T(8,128)(2,1)S...) custom-call(s32[32,5]{1,0:T(8,128)S(1)} %copy.8.contacts_ref, ...), custom_call_target="tpu_custom_call" | custom-call | flops 452984832 | bytes 10000000 | tf_op jit(solution)/shard_map/first/pallas_call | solution.py:281
  14.9 1.3 %collective-permute-start = (bf16[128,768]{1,0:T(8,128)(2,1)S(1)}, bf16[128,768]{1,0:T(8,128)(2,1)S(1)}, u32[]{:S(2)}, u32[]{:S(2)}) collective-permute-start(bf16[128,768]{1,0:T(8,128)(2,1)S(1)} %get-tuple-element.27), channel_id=1, source_target_pairs={{0,16},{16,32},{32,48},{48,64},{64,80},{80,96},{96,112},{112,128},... | collective-permute-start | bytes 589832 | tf_op jit(solution)/shard_map/ppermute | solution.py:273
  16.2 3.8 %collective-permute-start.1 = (bf16[128,768]{1,0:T(8,128)(2,1)S(1)}, bf16[128,768]{1,0:T(8,128)(2,1)S(1)}, u32[]{:S(2)}, u32[]{:S(2)}) collective-permute-start(bf16[128,768]{1,0:T(8,128)(2,1)S(1)} %get-tuple-element.27), channel_id=1, source_target_pairs={{16,0},{32,16},{48,32},{64,48},{80,64},{96,80},{112,96},{128,112},... | collective-permute-start | bytes 589832 | tf_op jit(solution)/shard_map/ppermute | solution.py:274
  20.0 0.0 collective-permute-done.2.other_ref
  20.0 0.0 collective-permute-start.3
  20.0 4.8 %collective-permute-start.4 = (bf16[128,768]{1,0:T(8,128)(2,1)S(1)}, bf16[128,768]{1,0:T(8,128)(2,1)S(1)}, u32[]{:S(2)}, u32[]{:S(2)}) collective-permute-start(bf16[128,768]{1,0:T(8,128)(2,1)S(1)} %collective-permute-done.2.other_ref), channel_id=1, source_target_pairs={{16,0},{32,16},{48,32},{64,48},{80,64},{96,80},{112,96},{128,112},... | collective-permute-start | bytes 589832 | tf_op jit(solution)/shard_map/ppermute | solution.py:274
  24.8 0.0 collective-permute-done.before_ref
  24.8 0.0 collective-permute-done.1.after_ref
  24.8 3.4 %early.1 = (bf16[6,512,128]{2,1,0:T(8,128)(2,1)S(1)}, f32[256,768]{1,0:T(8,128)S(1)}, f32[6,512,128]{2,1,0:T(8,128)S(1)}, f32[256,768]{1,0:T(8,128)S(1)}) custom-call(f32[2,512]{1,0:T(2,128)S(1)} %get-tuple-element.23.bias_ref, bf16[128,768]{1,0:T(8,128)(2,1)S(1)} %get-tuple-element.24.query_in, bf16[128,768]{1,0:T(8,128)(2,1)S(1)} %get-tuple-element.25.keys_in, ...), custom_call_target="tpu_custom_call" | custom-call | flops 4000000000 | bytes 4000000 | tf_op jit(solution)/shard_map/early/pallas_call | solution.py:300
  28.1 0.3 collective-permute-done.3.before_ref
  28.4 0.0 collective-permute-done.4.after_ref
  28.4 3.3 %late.1 = bf16[256,768]{1,0:T(8,128)(2,1)} custom-call(f32[2,256]{1,0:T(2,128)S(1)} %get-tuple-element.22.bias_ref, bf16[6,512,128]{2,1,0:T(8,128)(2,1)S(1)} %get-tuple-element.29.query_ref, f32[256,768]{1,0:T(8,128)S(1)} %get-tuple-element.30.sums_ref, f32[6,512,128]{2,1,0:T(8,128)S(1)} %get-tuple-element.31.tops_ref, ...), custom_call_target="tpu_custom_call" | custom-call | tf_op jit(solution)/shard_map/late/pallas_call | solution.py:313
  31.7 20.5 %all_to_all.23 = bf16[16,16,768]{2,1,0:T(8,128)(2,1)S(1)} all-to-all(bf16[16,16,768]{2,1,0:T(8,128)(2,1)} %bitcast.9), channel_id=1, replica_groups=mesh['pair'=16,'half'=2,'chip'=4,'core'=2] {'half','chip','core'}, dimensions={0} | all-to-all | bytes 786432 | tf_op jit(solution)/shard_map/all_to_all | solution.py:333
  52.2 4.8 %temporal.1 = bf16[256,768]{1,0:T(8,128)(2,1)} custom-call(bf16[256,768]{1,0:T(8,128)(2,1)S(1)} %bitcast.7, f32[16,128]{1,0:T(8,128)S(1)} %get-tuple-element.35.cos_ref, f32[16,128]{1,0:T(8,128)S(1)} %get-tuple-element.36.sin_ref, bf16[768,2304]{1,0:T(8,128)(2,1)S(1)} %get-tuple-element.37.qkv_ref, bf16[768,768]{1,0:T(8,128)(2,1)S(1)} %get-tuple-element.38.out_w_ref), custom_call_target="tpu_custom_call" | custom-call | tf_op jit(solution)/shard_map/temporal/pallas_call | solution.py:335
  56.9 14.4 %all_to_all.24 = bf16[16,16,768]{2,1,0:T(8,128)(2,1)S(1)} all-to-all(bf16[16,16,768]{2,1,0:T(8,128)(2,1)} %bitcast.10), channel_id=1, replica_groups=mesh['pair'=16,'half'=2,'chip'=4,'core'=2] {'chip','core'}, dimensions={0} | all-to-all | bytes 786432 | tf_op jit(solution)/shard_map/all_to_all | solution.py:351
  71.4 0.8 %copy.9 = bf16[8,2,16,768]{3,2,0,1:T(8,128)(2,1)} copy(bf16[8,2,16,768]{3,2,1,0:T(8,128)(2,1)S(1)} %bitcast.8) | data formatting | bytes 786432 | tf_op jit(solution)/shard_map/all_to_all | solution.py:351
Async XLA Ops:
  0.9 19.0 %collective-permute-start.2 = (bf16[128,768]{1,0:T(8,128)(2,1)S(1)}, bf16[128,768]{1,0:T(8,128)(2,1)S(1)}, u32[]{:S(2)}, u32[]{:S(2)}) collective-permute-start(bf16[128,768]{1,0:T(8,128)(2,1)S(1)} %give.1.given_ref), channel_id=1, source_target_pairs={{0,8},{8,0},{1,9},{9,1},{2,10},{10,2},{3,11},{11,3},{4,12},{12,4},... | collective-permute-start | bytes 589832 | tf_op jit(solution)/shard_map/ppermute | solution.py:270
  9.5 0.7 copy-start
  14.9 9.9 %collective-permute-start = (bf16[128,768]{1,0:T(8,128)(2,1)S(1)}, bf16[128,768]{1,0:T(8,128)(2,1)S(1)}, u32[]{:S(2)}, u32[]{:S(2)}) collective-permute-start(bf16[128,768]{1,0:T(8,128)(2,1)S(1)} %get-tuple-element.27), channel_id=1, source_target_pairs={{0,16},{16,32},{32,48},{48,64},{64,80},{80,96},{96,112},{112,128},... | collective-permute-start | bytes 589832 | tf_op jit(solution)/shard_map/ppermute | solution.py:273
  16.2 8.6 %collective-permute-start.1 = (bf16[128,768]{1,0:T(8,128)(2,1)S(1)}, bf16[128,768]{1,0:T(8,128)(2,1)S(1)}, u32[]{:S(2)}, u32[]{:S(2)}) collective-permute-start(bf16[128,768]{1,0:T(8,128)(2,1)S(1)} %get-tuple-element.27), channel_id=1, source_target_pairs={{16,0},{32,16},{48,32},{64,48},{80,64},{96,80},{112,96},{128,112},... | collective-permute-start | bytes 589832 | tf_op jit(solution)/shard_map/ppermute | solution.py:274
  20.0 8.4 %collective-permute-start.3 = (bf16[128,768]{1,0:T(8,128)(2,1)S(1)}, bf16[128,768]{1,0:T(8,128)(2,1)S(1)}, u32[]{:S(2)}, u32[]{:S(2)}) collective-permute-start(bf16[128,768]{1,0:T(8,128)(2,1)S(1)} %collective-permute-done.2.other_ref), channel_id=1, source_target_pairs={{0,16},{16,32},{32,48},{48,64},{64,80},{80,96},{96,112},{112,128},... | collective-permute-start | bytes 589832 | tf_op jit(solution)/shard_map/ppermute | solution.py:273
  20.0 8.4 %collective-permute-start.4 = (bf16[128,768]{1,0:T(8,128)(2,1)S(1)}, bf16[128,768]{1,0:T(8,128)(2,1)S(1)}, u32[]{:S(2)}, u32[]{:S(2)}) collective-permute-start(bf16[128,768]{1,0:T(8,128)(2,1)S(1)} %collective-permute-done.2.other_ref), channel_id=1, source_target_pairs={{16,0},{32,16},{48,32},{64,48},{80,64},{96,80},{112,96},{128,112},... | collective-permute-start | bytes 589832 | tf_op jit(solution)/shard_map/ppermute | solution.py:274

commit v5 on v4

--- a/solution.py
+++ b/solution.py
@@ -171,7 +171,7 @@
 
 def late_kernel(
     bias_ref, query_ref, sums_ref, tops_ref, totals_ref, before_ref, after_ref,
-    base_ref, other_ref, qkv_ref, out_ref, hidden_ref, keys, values, mix, hidden, semaphore,
+    base_ref, other_ref, qkv_ref, out_ref, hidden_ref, keys, values, mix,
 ):
     half = lax.axis_index("half")
     block, width = other_ref.shape
@@ -193,15 +193,12 @@
     added = dot(mix[...], out_ref[...])
     here = pl.ds(pl.multiple_of(half * block, block), block)
     there = pl.ds(pl.multiple_of((1 - half) * block, block), block)
-    hidden[here, :] = (base_ref[...].astype(jnp.float32) + added[:block]).astype(jnp.bfloat16)
-    hidden[there, :] = (other_ref[...].astype(jnp.float32) + added[block:]).astype(jnp.bfloat16)
-    store = pltpu.make_async_copy(hidden, hidden_ref, semaphore)
-    store.start()
-    store.wait()
+    hidden_ref[here, :] = (base_ref[...].astype(jnp.float32) + added[:block]).astype(jnp.bfloat16)
+    hidden_ref[there, :] = (other_ref[...].astype(jnp.float32) + added[block:]).astype(jnp.bfloat16)
 
 
 def time_kernel(
-    hidden_ref, cos_ref, sin_ref, qkv_ref, out_w_ref, layer_ref, query, keys, values, mix, layer, semaphore
+    hidden_ref, cos_ref, sin_ref, qkv_ref, out_w_ref, layer_ref, query, keys, values, mix
 ):
     rows, width = hidden_ref.shape
     frames = cos_ref.shape[0]
@@ -213,15 +210,13 @@
     sine = jnp.concatenate(
         [jnp.broadcast_to(sin_ref[f : f + 1, :], (group, PAIR)) for f in range(frames)], axis=0
     )
-    lane = lax.broadcasted_iota(jnp.int32, (rows, PAIR), 1)
-    first = (lane % HEAD) < HEAD // 2
+    source = lax.broadcasted_iota(jnp.int32, (PAIR, PAIR), 0)
+    target = lax.broadcasted_iota(jnp.int32, (PAIR, PAIR), 1)
+    exchange = jnp.where(source == target ^ (HEAD // 2), 1.0, 0.0).astype(jnp.bfloat16)
 
     def rotate(entries):
-        entries = entries.astype(jnp.bfloat16).astype(jnp.float32)
-        swapped = jnp.where(
-            first, pltpu.roll(entries, PAIR - HEAD // 2, 1), pltpu.roll(entries, HEAD // 2, 1)
-        )
-        return entries * cosine + swapped * sine
+        entries = entries.astype(jnp.bfloat16)
+        return entries.astype(jnp.float32) * cosine + dot(entries, exchange) * sine
 
     pairs = width // PAIR
     projected = dot(normed, qkv_ref[...])
@@ -244,10 +239,7 @@
     per_half = frames // 2
     for j in range(frames):
         frame = 2 * (j % per_half) + j // per_half
-        layer[frame * group : (frame + 1) * group, :] = added[j * group : (j + 1) * group, :]
-    store = pltpu.make_async_copy(layer, layer_ref, semaphore)
-    store.start()
-    store.wait()
+        layer_ref[frame * group : (frame + 1) * group, :] = added[j * group : (j + 1) * group, :]
 
 
 def shards(activations, contacts, frame_index, spatial_qkv, spatial_out, time_qkv, time_out):
@@ -312,15 +304,13 @@
     )(early_bias, query, keys, values, kept_before, kept_after, other, spatial_qkv)
     hidden = pl.pallas_call(
         late_kernel,
-        out_shape=pltpu.HBM((rows, width), bf16),
+        out_shape=pltpu.VMEM((rows, width), bf16),
         in_specs=[VMEM] * 11,
-        out_specs=HBM,
+        out_specs=VMEM,
         scratch_shapes=[
             pltpu.VMEM((rows, width), bf16),
             pltpu.VMEM((width // PAIR, rows, 2 * PAIR), bf16),
             pltpu.VMEM((rows, width), bf16),
-            pltpu.VMEM((rows, width), bf16),
-            pltpu.SemaphoreType.DMA,
         ],
         compiler_params=LIMIT,
         name="late",
@@ -334,16 +324,14 @@
 
     layer = pl.pallas_call(
         time_kernel,
-        out_shape=pltpu.HBM((rows, width), bf16),
+        out_shape=pltpu.VMEM((rows, width), bf16),
         in_specs=[VMEM] * 5,
-        out_specs=HBM,
+        out_specs=VMEM,
         scratch_shapes=[
             pltpu.VMEM((width // PAIR, 2 * rows, PAIR), bf16),
             pltpu.VMEM((rows, width), bf16),
             pltpu.VMEM((width // PAIR, rows, 2 * PAIR), bf16),
             pltpu.VMEM((rows, width), bf16),
-            pltpu.VMEM((rows, width), bf16),
-            pltpu.SemaphoreType.DMA,
         ],
         compiler_params=LIMIT,
         name="temporal",

time: 72.5 us -> 69.3 us (0.956)
  Pallas kernels: 17 us -> 14.3 us
    pallas_call x2, Pallas kernels: 8.06 us -> 5.39 us  [the longest x1 2.86 us: shards(): pl.pallas_call(time_kernel, out_shape=pltpu.VMEM((rows, width), bf16), in...]
  transfers between devices with their start and end apart: 5 -> 5, of which waited for: 1 -> 1; matrix products, arithmetic and copies ran while one was open for 1% -> 1% of each run, Pallas kernels for 11% -> 12%
where the time goes in v5:
time: 69.3 us; the launch traced here: 69.1 us
  blocking collectives  34.5 us (50%)
  starting transfers between devices  17.7 us (26%)
  Pallas kernels  14.3 us (21%)
  local copies, waits for them, and re-layouts  2.19 us (3%)
    all_to_all x1, blocking collectives, shards(): lax.all_to_all(hidden.reshape(members, group, width), COLUMN, 0, 0, tiled...  20.3 us
    all_to_all x1, blocking collectives, shards(): lax.all_to_all(layer.reshape(members, group, width), ('chip', 'core'), 0,...  14.2 us
    ppermute x2, starting transfers between devices, from_neighbours(): lax.ppermute(tile, 'pair', [((i + 1) % pairs, i) for i in range(pairs)])  8.59 us
    ppermute x1, starting transfers between devices, shards(): other = lax.ppermute(given, 'half', [(0, 1), (1, 0)])  7.83 us
    pallas_call x1, Pallas kernels, shards(): pl.pallas_call(first_kernel, out_shape=tuple((pltpu.VMEM(w.shape, bf16) f...  4.67 us
    pallas_call x1, Pallas kernels, shards(): pl.pallas_call(early_kernel, out_shape=(pltpu.VMEM((width // PAIR, 2 * ro...  3.36 us
    pallas_call x1, Pallas kernels, shards(): pl.pallas_call(time_kernel, out_shape=pltpu.VMEM((rows, width), bf16), in...  2.86 us
    pallas_call x1, Pallas kernels, shards(): pl.pallas_call(late_kernel, out_shape=pltpu.VMEM((rows, width), bf16), in...  2.53 us
  transfers between devices with their start and end apart: 5, of which 1 were waited for; matrix products, arithmetic and copies ran while one was open for 1% of the time, Pallas kernels for 12%

profile of v5, /device:TPU:1, one launch (start us, length us, event | category | flops | bytes accessed | tf_op | source)
XLA Modules:
  0.0 69.1 jit_solution(16413104924899670466)
XLA Ops:
  0.0 0.9 %give.1.given_ref = bf16[128,768]{1,0:T(8,128)(2,1)S(1)} custom-call(bf16[2,128,768]{2,1,0:T(8,128)(2,1)} %act_ref.3), custom_call_target="tpu_custom_call" | custom-call | tf_op jit(solution)/shard_map/give/pallas_call | solution.py:254
  0.9 7.8 %collective-permute-start.2 = (bf16[128,768]{1,0:T(8,128)(2,1)S(1)}, bf16[128,768]{1,0:T(8,128)(2,1)S(1)}, u32[]{:S(2)}, u32[]{:S(2)}) collective-permute-start(bf16[128,768]{1,0:T(8,128)(2,1)S(1)} %give.1.given_ref), channel_id=1, source_target_pairs={{0,8},{8,0},{1,9},{9,1},{2,10},{10,2},{3,11},{11,3},{4,12},{12,4},... | collective-permute-start | bytes 589832 | tf_op jit(solution)/shard_map/ppermute | solution.py:262
  8.8 0.8 %copy.8.contacts_ref = s32[32,5]{1,0:T(8,128)S(1)} copy(s32[32,5]{0,1:T(8,128)} %param.8) | data formatting | bytes 1280 | tf_op args[1]
  9.5 0.0 copy-start
  9.5 0.7 copy-done
  10.2 4.7 %first.1 = (bf16[768,2304]{1,0:T(8,128)(2,1)S(1)}, bf16[768,768]{1,0:T(8,128)(2,1)S(1)}, bf16[768,2304]{1,0:T(8,128)(2,1)S(1)}, bf16[768,768]{1,0:T(8,128)(2,1)S...) custom-call(s32[32,5]{1,0:T(8,128)S(1)} %copy.8.contacts_ref, ...), custom_call_target="tpu_custom_call" | custom-call | flops 452984832 | bytes 10000000 | tf_op jit(solution)/shard_map/first/pallas_call | solution.py:273
  14.9 1.3 %collective-permute-start = (bf16[128,768]{1,0:T(8,128)(2,1)S(1)}, bf16[128,768]{1,0:T(8,128)(2,1)S(1)}, u32[]{:S(2)}, u32[]{:S(2)}) collective-permute-start(bf16[128,768]{1,0:T(8,128)(2,1)S(1)} %get-tuple-element.27), channel_id=1, source_target_pairs={{0,16},{16,32},{32,48},{48,64},{64,80},{80,96},{96,112},{112,128},... | collective-permute-start | bytes 589832 | tf_op jit(solution)/shard_map/ppermute | solution.py:265
  16.2 3.8 %collective-permute-start.1 = (bf16[128,768]{1,0:T(8,128)(2,1)S(1)}, bf16[128,768]{1,0:T(8,128)(2,1)S(1)}, u32[]{:S(2)}, u32[]{:S(2)}) collective-permute-start(bf16[128,768]{1,0:T(8,128)(2,1)S(1)} %get-tuple-element.27), channel_id=1, source_target_pairs={{16,0},{32,16},{48,32},{64,48},{80,64},{96,80},{112,96},{128,112},... | collective-permute-start | bytes 589832 | tf_op jit(solution)/shard_map/ppermute | solution.py:266
  20.0 0.0 collective-permute-done.2.other_ref
  20.0 0.0 collective-permute-start.3
  20.0 4.8 %collective-permute-start.4 = (bf16[128,768]{1,0:T(8,128)(2,1)S(1)}, bf16[128,768]{1,0:T(8,128)(2,1)S(1)}, u32[]{:S(2)}, u32[]{:S(2)}) collective-permute-start(bf16[128,768]{1,0:T(8,128)(2,1)S(1)} %collective-permute-done.2.other_ref), channel_id=1, source_target_pairs={{16,0},{32,16},{48,32},{64,48},{80,64},{96,80},{112,96},{128,112},... | collective-permute-start | bytes 589832 | tf_op jit(solution)/shard_map/ppermute | solution.py:266
  24.8 0.0 collective-permute-done.before_ref
  24.8 0.0 collective-permute-done.1.after_ref
  24.8 3.4 %early.1 = (bf16[6,512,128]{2,1,0:T(8,128)(2,1)S(1)}, f32[256,768]{1,0:T(8,128)S(1)}, f32[6,512,128]{2,1,0:T(8,128)S(1)}, f32[256,768]{1,0:T(8,128)S(1)}) custom-call(f32[2,512]{1,0:T(2,128)S(1)} %get-tuple-element.23.bias_ref, bf16[128,768]{1,0:T(8,128)(2,1)S(1)} %get-tuple-element.24.query_in, bf16[128,768]{1,0:T(8,128)(2,1)S(1)} %get-tuple-element.25.keys_in, ...), custom_call_target="tpu_custom_call" | custom-call | flops 4000000000 | bytes 4000000 | tf_op jit(solution)/shard_map/early/pallas_call | solution.py:292
  28.1 0.3 collective-permute-done.3.before_ref
  28.4 0.0 collective-permute-done.4.after_ref
  28.4 2.5 %late.1 = bf16[256,768]{1,0:T(8,128)(2,1)S(1)} custom-call(f32[2,256]{1,0:T(2,128)S(1)} %get-tuple-element.22.bias_ref, bf16[6,512,128]{2,1,0:T(8,128)(2,1)S(1)} %get-tuple-element.29.query_ref, f32[256,768]{1,0:T(8,128)S(1)} %get-tuple-element.30.sums_ref, f32[6,512,128]{2,1,0:T(8,128)S(1)} %get-tuple-element.31.tops_ref, ...), custom_call_target="tpu_custom_call" | custom-call | tf_op jit(solution)/shard_map/late/pallas_call | solution.py:305
  30.9 20.3 %all_to_all.23 = bf16[16,16,768]{2,1,0:T(8,128)(2,1)S(1)} all-to-all(bf16[16,16,768]{2,1,0:T(8,128)(2,1)S(1)} %bitcast.7), channel_id=1, replica_groups=mesh['pair'=16,'half'=2,'chip'=4,'core'=2] {'half','chip','core'}, dimensions={0} | all-to-all | bytes 786432 | tf_op jit(solution)/shard_map/all_to_all | solution.py:323
  51.2 2.9 %temporal.1 = bf16[256,768]{1,0:T(8,128)(2,1)S(1)} custom-call(bf16[256,768]{1,0:T(8,128)(2,1)S(1)} %bitcast.8, f32[16,128]{1,0:T(8,128)S(1)} %get-tuple-element.35.cos_ref, f32[16,128]{1,0:T(8,128)S(1)} %get-tuple-element.36.sin_ref, bf16[768,2304]{1,0:T(8,128)(2,1)S(1)} %get-tuple-element.37.qkv_ref, bf16[768,768]{1,0:T(8,128)(2,1)S(1)} %get-tuple-element.38.out_w_ref), custom_call_target="tpu_custom_call" | custom-call | tf_op jit(solution)/shard_map/temporal/pallas_call | solution.py:325
  54.1 14.2 %all_to_all.24 = bf16[16,16,768]{2,1,0:T(8,128)(2,1)S(1)} all-to-all(bf16[16,16,768]{2,1,0:T(8,128)(2,1)S(1)} %bitcast.9), channel_id=1, replica_groups=mesh['pair'=16,'half'=2,'chip'=4,'core'=2] {'chip','core'}, dimensions={0} | all-to-all | bytes 786432 | tf_op jit(solution)/shard_map/all_to_all | solution.py:339
  68.3 0.8 %copy.9 = bf16[8,2,16,768]{3,2,0,1:T(8,128)(2,1)} copy(bf16[8,2,16,768]{3,2,1,0:T(8,128)(2,1)S(1)} %bitcast.10) | data formatting | bytes 786432 | tf_op jit(solution)/shard_map/all_to_all | solution.py:339
Async XLA Ops:
  0.9 19.0 %collective-permute-start.2 = (bf16[128,768]{1,0:T(8,128)(2,1)S(1)}, bf16[128,768]{1,0:T(8,128)(2,1)S(1)}, u32[]{:S(2)}, u32[]{:S(2)}) collective-permute-start(bf16[128,768]{1,0:T(8,128)(2,1)S(1)} %give.1.given_ref), channel_id=1, source_target_pairs={{0,8},{8,0},{1,9},{9,1},{2,10},{10,2},{3,11},{11,3},{4,12},{12,4},... | collective-permute-start | bytes 589832 | tf_op jit(solution)/shard_map/ppermute | solution.py:262
  9.5 0.7 copy-start
  14.9 9.9 %collective-permute-start = (bf16[128,768]{1,0:T(8,128)(2,1)S(1)}, bf16[128,768]{1,0:T(8,128)(2,1)S(1)}, u32[]{:S(2)}, u32[]{:S(2)}) collective-permute-start(bf16[128,768]{1,0:T(8,128)(2,1)S(1)} %get-tuple-element.27), channel_id=1, source_target_pairs={{0,16},{16,32},{32,48},{48,64},{64,80},{80,96},{96,112},{112,128},... | collective-permute-start | bytes 589832 | tf_op jit(solution)/shard_map/ppermute | solution.py:265
  16.2 8.6 %collective-permute-start.1 = (bf16[128,768]{1,0:T(8,128)(2,1)S(1)}, bf16[128,768]{1,0:T(8,128)(2,1)S(1)}, u32[]{:S(2)}, u32[]{:S(2)}) collective-permute-start(bf16[128,768]{1,0:T(8,128)(2,1)S(1)} %get-tuple-element.27), channel_id=1, source_target_pairs={{16,0},{32,16},{48,32},{64,48},{80,64},{96,80},{112,96},{128,112},... | collective-permute-start | bytes 589832 | tf_op jit(solution)/shard_map/ppermute | solution.py:266
  20.0 8.4 %collective-permute-start.3 = (bf16[128,768]{1,0:T(8,128)(2,1)S(1)}, bf16[128,768]{1,0:T(8,128)(2,1)S(1)}, u32[]{:S(2)}, u32[]{:S(2)}) collective-permute-start(bf16[128,768]{1,0:T(8,128)(2,1)S(1)} %collective-permute-done.2.other_ref), channel_id=1, source_target_pairs={{0,16},{16,32},{32,48},{48,64},{64,80},{80,96},{96,112},{112,128},... | collective-permute-start | bytes 589832 | tf_op jit(solution)/shard_map/ppermute | solution.py:265
  20.0 8.4 %collective-permute-start.4 = (bf16[128,768]{1,0:T(8,128)(2,1)S(1)}, bf16[128,768]{1,0:T(8,128)(2,1)S(1)}, u32[]{:S(2)}, u32[]{:S(2)}) collective-permute-start(bf16[128,768]{1,0:T(8,128)(2,1)S(1)} %collective-permute-done.2.other_ref), channel_id=1, source_target_pairs={{16,0},{32,16},{48,32},{64,48},{80,64},{96,80},{112,96},{128,112},... | collective-permute-start | bytes 589832 | tf_op jit(solution)/shard_map/ppermute | solution.py:266

commit v6 on v5

--- a/solution.py
+++ b/solution.py
@@ -82,15 +82,16 @@
     half, pair = lax.axis_index("half"), lax.axis_index("pair")
     block = early_ref.shape[1] // 4
     to_other = 1 - 2 * half
+    odd = 4 * (pair % 2) - 2
     for row, (parity, moves) in enumerate(
         (
-            (half, (0, -2, 2, to_other, to_other - 2, to_other + 2)),
-            (1 - half, (-to_other, -to_other - 2, -to_other + 2, 0, -2, 2)),
+            (half, (0, odd, -odd, to_other, to_other + odd, to_other - odd)),
+            (1 - half, (-to_other, odd - to_other, -odd - to_other, 0, odd, -odd)),
         )
     ):
         for tile, move in enumerate(moves):
             column = jnp.clip(move + 2, 0, 4)
-            flag = jnp.where(column == move + 2, contacts_ref[2 * pair + parity, column], 0)
+            flag = jnp.where(column == move + 2, contacts_ref[column, 2 * pair + parity], 0)
             ref, at = (early_ref, tile) if tile < 4 else (late_ref, tile - 4)
             ref[row : row + 1, at * block : (at + 1) * block] = jnp.full(
                 (1, block), jnp.where(flag > 0, 0.0, EXCLUDED), jnp.float32
@@ -114,20 +115,22 @@
 
 
 def first_kernel(
-    contacts_ref, frame_ref, given_ref, act_ref, qkv_hbm, out_hbm, time_qkv_hbm, time_out_hbm,
-    qkv_ref, out_ref, time_qkv_ref, time_out_ref, normed_ref, base_ref, query_ref, keys_ref, values_ref,
-    early_ref, late_ref, cos_ref, sin_ref, semaphores,
+    contacts_hbm, frame_hbm, given_ref, act_ref, qkv_hbm,
+    qkv_ref, normed_ref, base_ref, query_ref, keys_ref, values_ref, early_ref, late_ref, cos_ref, sin_ref,
+    contacts_ref, frame_ref, semaphores,
 ):
     half = lax.axis_index("half")
     width = base_ref.shape[1]
     own = pltpu.make_async_copy(act_ref.at[half], base_ref, semaphores.at[0])
     own.start()
-    loads = []
-    for at, (source, target) in enumerate(
-        ((qkv_hbm, qkv_ref), (out_hbm, out_ref), (time_qkv_hbm, time_qkv_ref), (time_out_hbm, time_out_ref))
-    ):
-        loads.append(pltpu.make_async_copy(source, target, semaphores.at[at + 1]))
-        loads[-1].start()
+    loads = [
+        pltpu.make_async_copy(source, target, semaphores.at[at + 1])
+        for at, (source, target) in enumerate(
+            ((qkv_hbm, qkv_ref), (contacts_hbm, contacts_ref), (frame_hbm, frame_ref))
+        )
+    ]
+    for load in loads:
+        load.start()
     own.wait()
     normed = unit_rows(base_ref[...])
     normed_ref[...] = normed
@@ -135,22 +138,31 @@
     query_ref[...] = (dot(normed, qkv_ref[:, :width]) * SCALE).astype(jnp.bfloat16)
     keys_ref[...] = dot(normed, qkv_ref[:, width : 2 * width]).astype(jnp.bfloat16)
     values_ref[...] = dot(normed, qkv_ref[:, 2 * width :]).astype(jnp.bfloat16)
+    for load in loads[1:]:
+        load.wait()
     contact_biases(contacts_ref, early_ref, late_ref)
     rotation_tables(frame_ref, cos_ref, sin_ref)
-    for load in loads[1:]:
-        load.wait()
 
 
 def early_kernel(
-    bias_ref, query_in, keys_in, values_in, before_ref, after_ref, other_ref, qkv_ref,
-    query_ref, sums_ref, tops_ref, totals_ref, keys, values,
+    bias_ref, query_in, keys_in, values_in, odd_ref, even_ref, other_ref, qkv_ref, out_hbm, time_qkv_hbm,
+    time_out_hbm, query_ref, sums_ref, tops_ref, totals_ref, out_ref, time_qkv_ref, time_out_ref,
+    keys, values, semaphores,
 ):
+    loads = [
+        pltpu.make_async_copy(source, target, semaphores.at[at])
+        for at, (source, target) in enumerate(
+            ((out_hbm, out_ref), (time_qkv_hbm, time_qkv_ref), (time_out_hbm, time_out_ref))
+        )
+    ]
+    for load in loads:
+        load.start()
     block, width = other_ref.shape
     pairs = width // PAIR
     normed = unit_rows(other_ref[...])
     query = (dot(normed, qkv_ref[:, :width]) * SCALE).astype(jnp.bfloat16)
     keys[:block, :] = keys_in[...]
-    tiles = jnp.concatenate([before_ref[...], after_ref[...], normed], axis=0)
+    tiles = jnp.concatenate([odd_ref[...], even_ref[...], normed], axis=0)
     keys[block:, :] = dot(tiles, qkv_ref[:, width : 2 * width]).astype(jnp.bfloat16)
     fresh = dot(tiles, qkv_ref[:, 2 * width :]).astype(jnp.bfloat16)
     for pair in range(pairs):
@@ -167,16 +179,18 @@
         totals_ref[:, at] = side_by_side(product[:, PAIR:])
 
     attend(query_ref, keys, values, pairs, two_rows(bias_ref, block), finish)
+    for load in loads:
+        load.wait()
 
 
 def late_kernel(
-    bias_ref, query_ref, sums_ref, tops_ref, totals_ref, before_ref, after_ref,
+    bias_ref, query_ref, sums_ref, tops_ref, totals_ref, odd_ref, even_ref,
     base_ref, other_ref, qkv_ref, out_ref, hidden_ref, keys, values, mix,
 ):
     half = lax.axis_index("half")
     block, width = other_ref.shape
     pairs = width // PAIR
-    tiles = unit_rows(jnp.concatenate([before_ref[...], after_ref[...]], axis=0))
+    tiles = unit_rows(jnp.concatenate([odd_ref[...], even_ref[...]], axis=0))
     keys[...] = dot(tiles, qkv_ref[:, width : 2 * width]).astype(jnp.bfloat16)
     fresh = dot(tiles, qkv_ref[:, 2 * width :]).astype(jnp.bfloat16)
     for pair in range(pairs):
@@ -261,47 +275,66 @@
     )(activations)
     other = lax.ppermute(given, "half", [(0, 1), (1, 0)])
 
+    column = lax.axis_size("half") * lax.axis_size("chip") * lax.axis_size("core")
+    even, odd = [], []
+    for i in range(pairs):
+        for place in range(column):
+            at = i * column + place
+            even.append((at, (i ^ 1) * column + place))
+            if i in (0, pairs - 1):
+                odd.append((at, at ^ 1))
+            else:
+                odd.append((at, (((i - 1) ^ 1) + 1) * column + place))
+
     def from_neighbours(tile):
-        before = lax.ppermute(tile, "pair", [(i, (i + 1) % pairs) for i in range(pairs)])
-        after = lax.ppermute(tile, "pair", [((i + 1) % pairs, i) for i in range(pairs)])
-        return before, after
+        axes = ("pair",) + COLUMN
+        return lax.ppermute(tile, axes, odd), lax.ppermute(tile, axes, even)
 
     tile_in_vmem = pltpu.VMEM((block, width), bf16)
-    weights = (spatial_qkv, spatial_out, time_qkv, time_out)
     members = 2 * lax.axis_size("chip") * lax.axis_size("core")
     table = pltpu.VMEM((members, PAIR), f32)
-    *weights, normed, base, query, keys, values, early_bias, late_bias, cosine, sine = pl.pallas_call(
+    by_offset = contacts.T
+    spatial_qkv, normed, base, query, keys, values, early_bias, late_bias, cosine, sine = pl.pallas_call(
         first_kernel,
-        out_shape=tuple(pltpu.VMEM(w.shape, bf16) for w in weights)
-        + (tile_in_vmem,)
-        + (tile_in_vmem,) * 4
+        out_shape=(pltpu.VMEM(spatial_qkv.shape, bf16),)
+        + (tile_in_vmem,) * 5
         + (pltpu.VMEM((2, 4 * block), f32), pltpu.VMEM((2, 2 * block), f32), table, table),
-        in_specs=[SMEM] * 2 + [VMEM] + [HBM] * 5,
-        out_specs=(VMEM,) * 13,
-        scratch_shapes=[pltpu.SemaphoreType.DMA((5,))],
+        in_specs=[HBM] * 2 + [VMEM] + [HBM] * 2,
+        out_specs=(VMEM,) * 10,
+        scratch_shapes=[
+            pltpu.SMEM(by_offset.shape, jnp.int32),
+            pltpu.SMEM(frame_index.shape, jnp.int32),
+            pltpu.SemaphoreType.DMA((4,)),
+        ],
         compiler_params=LIMIT,
-        cost_estimate=pl.CostEstimate(flops=2 * block * width * 3 * width, bytes_accessed=10_000_000, transcendentals=0),
+        cost_estimate=pl.CostEstimate(flops=2 * block * width * 3 * width, bytes_accessed=4_000_000, transcendentals=0),
         name="first",
-    )(contacts, frame_index, given, activations, *weights)
-    spatial_qkv, spatial_out, time_qkv, time_out = weights
-    kept_before, kept_after = from_neighbours(normed)
-    other_before, other_after = from_neighbours(other)
+    )(
+        pltpu.with_memory_space_constraint(by_offset, pltpu.HBM),
+        pltpu.with_memory_space_constraint(frame_index, pltpu.HBM),
+        given, activations, spatial_qkv,
+    )
+    kept_odd, kept_even = from_neighbours(normed)
+    other_odd, other_even = from_neighbours(other)
 
     wide = pltpu.VMEM((rows, width), f32)
     tops_shape = pltpu.VMEM((width // PAIR, 2 * rows, PAIR), f32)
-    query, sums, tops, totals = pl.pallas_call(
+    later = (spatial_out, time_qkv, time_out)
+    query, sums, tops, totals, spatial_out, time_qkv, time_out = pl.pallas_call(
         early_kernel,
-        out_shape=(pltpu.VMEM((width // PAIR, 2 * rows, PAIR), bf16), wide, tops_shape, wide),
-        in_specs=[VMEM] * 8,
-        out_specs=(VMEM,) * 4,
+        out_shape=(pltpu.VMEM((width // PAIR, 2 * rows, PAIR), bf16), wide, tops_shape, wide)
+        + tuple(pltpu.VMEM(weight.shape, bf16) for weight in later),
+        in_specs=[VMEM] * 8 + [HBM] * 3,
+        out_specs=(VMEM,) * 7,
         scratch_shapes=[
             pltpu.VMEM((4 * block, width), bf16),
             pltpu.VMEM((width // PAIR, 4 * block, 2 * PAIR), bf16),
+            pltpu.SemaphoreType.DMA((3,)),
         ],
         compiler_params=LIMIT,
         cost_estimate=pl.CostEstimate(flops=4_000_000_000, bytes_accessed=4_000_000, transcendentals=2_000_000),
         name="early",
-    )(early_bias, query, keys, values, kept_before, kept_after, other, spatial_qkv)
+    )(early_bias, query, keys, values, kept_odd, kept_even, other, spatial_qkv, *later)
     hidden = pl.pallas_call(
         late_kernel,
         out_shape=pltpu.VMEM((rows, width), bf16),
@@ -315,7 +348,7 @@
         compiler_params=LIMIT,
         name="late",
     )(
-        late_bias, query, sums, tops, totals, other_before, other_after,
+        late_bias, query, sums, tops, totals, other_odd, other_even,
         base, other, spatial_qkv, spatial_out,
     )
 

time: 69.3 us -> 68.2 us (0.984)
  starting transfers between devices: 17.7 us -> 12.5 us
  blocking collectives: 34.5 us -> 38.5 us
  waiting for transfers between devices: 0.29 us -> 2.96 us
  Pallas kernels: 14.3 us -> 12.6 us
  local copies, waits for them, and re-layouts: 2.19 us -> 0.77 us
    ppermute x4, starting transfers between devices: 9.88 us -> 4.64 us  [from_neighbours(): return (lax.ppermute(tile, axes, odd), lax.ppermute(tile, axes, even))]
    all_to_all x1, blocking collectives: 20.3 us -> 24.3 us  [shards(): lax.all_to_all(hidden.reshape(members, group, width), COLUMN, 0, 0, tiled...]
    ppermute x4, waiting for transfers between devices: 0.28 us -> 2.96 us  [from_neighbours(): return (lax.ppermute(tile, axes, odd), lax.ppermute(tile, axes, even))]
    pallas_call x1, Pallas kernels: 4.67 us -> 2.91 us  [shards(): pl.pallas_call(first_kernel, out_shape=(pltpu.VMEM(spatial_qkv.shape, bf1...]
    unnamed x3 -> x0, local copies, waits for them, and re-layouts: 1.42 us -> none
  transfers between devices with their start and end apart: 5 -> 5, of which waited for: 1 -> 2; matrix products, arithmetic and copies ran while one was open for 1% -> 0% of each run, Pallas kernels for 12% -> 9%
where the time goes in v6:
time: 68.2 us; the launch traced here: 67.4 us
  blocking collectives  38.5 us (56%)
  Pallas kernels  12.6 us (18%)
  starting transfers between devices  12.5 us (18%)
  waiting for transfers between devices  2.96 us (4%)
  local copies, waits for them, and re-layouts  0.77 us (1%)
    all_to_all x1, blocking collectives, shards(): lax.all_to_all(hidden.reshape(members, group, width), COLUMN, 0, 0, tiled...  24.3 us
    all_to_all x1, blocking collectives, shards(): lax.all_to_all(layer.reshape(members, group, width), ('chip', 'core'), 0,...  14.2 us
    ppermute x1, starting transfers between devices, shards(): other = lax.ppermute(given, 'half', [(0, 1), (1, 0)])  7.83 us
    ppermute x4, starting transfers between devices, from_neighbours(): return (lax.ppermute(tile, axes, odd), lax.ppermute(tile, axes, even))  4.64 us
    pallas_call x1, Pallas kernels, shards(): pl.pallas_call(early_kernel, out_shape=(pltpu.VMEM((width // PAIR, 2 * ro...  3.39 us
    ppermute x4, waiting for transfers between devices, from_neighbours(): return (lax.ppermute(tile, axes, odd), lax.ppermute(tile, axes, even))  2.96 us
    pallas_call x1, Pallas kernels, shards(): pl.pallas_call(first_kernel, out_shape=(pltpu.VMEM(spatial_qkv.shape, bf1...  2.91 us
    pallas_call x1, Pallas kernels, shards(): pl.pallas_call(time_kernel, out_shape=pltpu.VMEM((rows, width), bf16), in...  2.85 us
  transfers between devices with their start and end apart: 5, of which 2 were waited for; matrix products, arithmetic and copies ran while one was open for 0% of the time, Pallas kernels for 9%

profile of v6, /device:TPU:1, one launch (start us, length us, event | category | flops | bytes accessed | tf_op | source)
XLA Modules:
  0.0 67.4 jit_solution(17816426852555658661)
XLA Ops:
  0.0 0.9 %give.1.given_ref = bf16[128,768]{1,0:T(8,128)(2,1)S(1)} custom-call(bf16[2,128,768]{2,1,0:T(8,128)(2,1)} %act_ref.3), custom_call_target="tpu_custom_call" | custom-call | tf_op jit(solution)/shard_map/give/pallas_call | solution.py:268
  0.9 7.8 %collective-permute-start.2 = (bf16[128,768]{1,0:T(8,128)(2,1)S(1)}, bf16[128,768]{1,0:T(8,128)(2,1)S(1)}, u32[]{:S(2)}, u32[]{:S(2)}) collective-permute-start(bf16[128,768]{1,0:T(8,128)(2,1)S(1)} %give.1.given_ref), channel_id=1, source_target_pairs={{0,8},{8,0},{1,9},{9,1},{2,10},{10,2},{3,11},{11,3},{4,12},{12,4},... | collective-permute-start | bytes 589832 | tf_op jit(solution)/shard_map/ppermute | solution.py:276
  8.8 2.9 %first.1 = (bf16[768,2304]{1,0:T(8,128)(2,1)S(1)}, bf16[128,768]{1,0:T(8,128)(2,1)S(1)}, bf16[128,768]{1,0:T(8,128)(2,1)S(1)}, bf16[128,768]{1,0:T(8,128)(2,1)S(...) custom-call(s32[5,32]{1,0:T(8,128)} %bitcast.12, ...), custom_call_target="tpu_custom_call" | custom-call | flops 452984832 | bytes 4000000 | tf_op jit(solution)/shard_map/first/pallas_call | solution.py:297
  11.7 1.0 %collective-permute-start = (bf16[128,768]{1,0:T(8,128)(2,1)S(1)}, bf16[128,768]{1,0:T(8,128)(2,1)S(1)}, u32[]{:S(2)}, u32[]{:S(2)}) collective-permute-start(bf16[128,768]{1,0:T(8,128)(2,1)S(1)} %get-tuple-element.27), channel_id=1, source_target_pairs={{0,1},{1,0},{2,3},{3,2},{4,5},{5,4},{6,7},{7,6},{8,9},{9,8},{10,11... | collective-permute-start | bytes 589832 | tf_op jit(solution)/shard_map/ppermute | solution.py:291
  12.7 1.5 %collective-permute-start.1 = (bf16[128,768]{1,0:T(8,128)(2,1)S(1)}, bf16[128,768]{1,0:T(8,128)(2,1)S(1)}, u32[]{:S(2)}, u32[]{:S(2)}) collective-permute-start(bf16[128,768]{1,0:T(8,128)(2,1)S(1)} %get-tuple-element.27), channel_id=1, source_target_pairs={{0,16},{1,17},{2,18},{3,19},{4,20},{5,21},{6,22},{7,23},{8,24},{9,... | collective-permute-start | bytes 589832 | tf_op jit(solution)/shard_map/ppermute | solution.py:291
  14.2 0.0 collective-permute-done.2.other_ref
  14.2 1.5 %collective-permute-start.3 = (bf16[128,768]{1,0:T(8,128)(2,1)S(1)}, bf16[128,768]{1,0:T(8,128)(2,1)S(1)}, u32[]{:S(2)}, u32[]{:S(2)}) collective-permute-start(bf16[128,768]{1,0:T(8,128)(2,1)S(1)} %collective-permute-done.2.other_ref), channel_id=1, source_target_pairs={{0,1},{1,0},{2,3},{3,2},{4,5},{5,4},{6,7},{7,6},{8,9},{9,8},{10,11... | collective-permute-start | bytes 589832 | tf_op jit(solution)/shard_map/ppermute | solution.py:291
  15.7 0.6 collective-permute-start.4
  16.3 0.0 collective-permute-done.odd_ref
  16.3 1.9 %collective-permute-done.1.even_ref = bf16[128,768]{1,0:T(8,128)(2,1)S(1)} collective-permute-done((bf16[128,768]{1,0:T(8,128)(2,1)S(1)}, bf16[128,768]{1,0:T(8,128)(2,1)S(1)}, u32[]{:S(2)}, u32[]{:S(2)}) %collective-permute-start.1) | collective-permute-done | bytes 196640 | tf_op jit(solution)/shard_map/ppermute | solution.py:291
  18.2 3.4 %early.1 = (bf16[6,512,128]{2,1,0:T(8,128)(2,1)S(1)}, f32[256,768]{1,0:T(8,128)S(1)}, f32[6,512,128]{2,1,0:T(8,128)S(1)}, f32[256,768]{1,0:T(8,128)S(1)}, bf16[7...) custom-call(f32[2,512]{1,0:T(2,128)S(1)} %get-tuple-element.23.bias_ref, ...), custom_call_target="tpu_custom_call" | custom-call | flops 4000000000 | bytes 4000000 | tf_op jit(solution)/shard_map/early/pallas_call | solution.py:323
  21.6 0.0 collective-permute-done.3.odd_ref
  21.6 1.1 %collective-permute-done.4.even_ref = bf16[128,768]{1,0:T(8,128)(2,1)S(1)} collective-permute-done((bf16[128,768]{1,0:T(8,128)(2,1)S(1)}, bf16[128,768]{1,0:T(8,128)(2,1)S(1)}, u32[]{:S(2)}, u32[]{:S(2)}) %collective-permute-start.4) | collective-permute-done | bytes 196640 | tf_op jit(solution)/shard_map/ppermute | solution.py:291
  22.7 2.5 %late.1 = bf16[256,768]{1,0:T(8,128)(2,1)S(1)} custom-call(f32[2,256]{1,0:T(2,128)S(1)} %get-tuple-element.22.bias_ref, bf16[6,512,128]{2,1,0:T(8,128)(2,1)S(1)} %get-tuple-element.29.query_ref, f32[256,768]{1,0:T(8,128)S(1)} %get-tuple-element.30.sums_ref, f32[6,512,128]{2,1,0:T(8,128)S(1)} %get-tuple-element.31.tops_ref, ...), custom_call_target="tpu_custom_call" | custom-call | tf_op jit(solution)/shard_map/late/pallas_call | solution.py:338
  25.2 24.3 %all_to_all.23 = bf16[16,16,768]{2,1,0:T(8,128)(2,1)S(1)} all-to-all(bf16[16,16,768]{2,1,0:T(8,128)(2,1)S(1)} %bitcast.8), channel_id=1, replica_groups=mesh['pair'=16,'half'=2,'chip'=4,'core'=2] {'half','chip','core'}, dimensions={0} | all-to-all | bytes 786432 | tf_op jit(solution)/shard_map/all_to_all | solution.py:356
  49.5 2.9 %temporal.1 = bf16[256,768]{1,0:T(8,128)(2,1)S(1)} custom-call(bf16[256,768]{1,0:T(8,128)(2,1)S(1)} %bitcast.9, f32[16,128]{1,0:T(8,128)S(1)} %get-tuple-element.35.cos_ref, f32[16,128]{1,0:T(8,128)S(1)} %get-tuple-element.36.sin_ref, bf16[768,2304]{1,0:T(8,128)(2,1)S(1)} %get-tuple-element.37.qkv_ref, bf16[768,768]{1,0:T(8,128)(2,1)S(1)} %get-tuple-element.38.out_w_ref), custom_call_target="tpu_custom_call" | custom-call | tf_op jit(solution)/shard_map/temporal/pallas_call | solution.py:358
  52.4 14.2 %all_to_all.24 = bf16[16,16,768]{2,1,0:T(8,128)(2,1)S(1)} all-to-all(bf16[16,16,768]{2,1,0:T(8,128)(2,1)S(1)} %bitcast.10), channel_id=1, replica_groups=mesh['pair'=16,'half'=2,'chip'=4,'core'=2] {'chip','core'}, dimensions={0} | all-to-all | bytes 786432 | tf_op jit(solution)/shard_map/all_to_all | solution.py:372
  66.6 0.8 %copy.8 = bf16[8,2,16,768]{3,2,0,1:T(8,128)(2,1)} copy(bf16[8,2,16,768]{3,2,1,0:T(8,128)(2,1)S(1)} %bitcast.11) | data formatting | bytes 786432 | tf_op jit(solution)/shard_map/all_to_all | solution.py:372
Async XLA Ops:
  0.9 13.3 %collective-permute-start.2 = (bf16[128,768]{1,0:T(8,128)(2,1)S(1)}, bf16[128,768]{1,0:T(8,128)(2,1)S(1)}, u32[]{:S(2)}, u32[]{:S(2)}) collective-permute-start(bf16[128,768]{1,0:T(8,128)(2,1)S(1)} %give.1.given_ref), channel_id=1, source_target_pairs={{0,8},{8,0},{1,9},{9,1},{2,10},{10,2},{3,11},{11,3},{4,12},{12,4},... | collective-permute-start | bytes 589832 | tf_op jit(solution)/shard_map/ppermute | solution.py:276
  11.7 4.6 %collective-permute-start = (bf16[128,768]{1,0:T(8,128)(2,1)S(1)}, bf16[128,768]{1,0:T(8,128)(2,1)S(1)}, u32[]{:S(2)}, u32[]{:S(2)}) collective-permute-start(bf16[128,768]{1,0:T(8,128)(2,1)S(1)} %get-tuple-element.27), channel_id=1, source_target_pairs={{0,1},{1,0},{2,3},{3,2},{4,5},{5,4},{6,7},{7,6},{8,9},{9,8},{10,11... | collective-permute-start | bytes 589832 | tf_op jit(solution)/shard_map/ppermute | solution.py:291
  12.7 5.5 %collective-permute-start.1 = (bf16[128,768]{1,0:T(8,128)(2,1)S(1)}, bf16[128,768]{1,0:T(8,128)(2,1)S(1)}, u32[]{:S(2)}, u32[]{:S(2)}) collective-permute-start(bf16[128,768]{1,0:T(8,128)(2,1)S(1)} %get-tuple-element.27), channel_id=1, source_target_pairs={{0,16},{1,17},{2,18},{3,19},{4,20},{5,21},{6,22},{7,23},{8,24},{9,... | collective-permute-start | bytes 589832 | tf_op jit(solution)/shard_map/ppermute | solution.py:291
  14.2 7.4 %collective-permute-start.3 = (bf16[128,768]{1,0:T(8,128)(2,1)S(1)}, bf16[128,768]{1,0:T(8,128)(2,1)S(1)}, u32[]{:S(2)}, u32[]{:S(2)}) collective-permute-start(bf16[128,768]{1,0:T(8,128)(2,1)S(1)} %collective-permute-done.2.other_ref), channel_id=1, source_target_pairs={{0,1},{1,0},{2,3},{3,2},{4,5},{5,4},{6,7},{7,6},{8,9},{9,8},{10,11... | collective-permute-start | bytes 589832 | tf_op jit(solution)/shard_map/ppermute | solution.py:291
  15.7 7.0 %collective-permute-start.4 = (bf16[128,768]{1,0:T(8,128)(2,1)S(1)}, bf16[128,768]{1,0:T(8,128)(2,1)S(1)}, u32[]{:S(2)}, u32[]{:S(2)}) collective-permute-start(bf16[128,768]{1,0:T(8,128)(2,1)S(1)} %collective-permute-done.2.other_ref), channel_id=1, source_target_pairs={{0,16},{1,17},{2,18},{3,19},{4,20},{5,21},{6,22},{7,23},{8,24},{9,... | collective-permute-start | bytes 589832 | tf_op jit(solution)/shard_map/ppermute | solution.py:291

commit v7 on v6

--- a/solution.py
+++ b/solution.py
@@ -13,10 +13,12 @@
 EXCLUDED = -1e30
 LOG2E = 1.4426950408889634
 SCALE = LOG2E / 8.0
+EXCHANGES = (0, 2, 3, 1)
 COLUMN = ("half", "chip", "core")
 VMEM = pl.BlockSpec(memory_space=pltpu.VMEM)
 SMEM = pl.BlockSpec(memory_space=pltpu.SMEM)
 HBM = pl.BlockSpec(memory_space=pltpu.HBM)
+SMALL = pltpu.CompilerParams(vmem_limit_bytes=4 * 1024 * 1024)
 LIMIT = pltpu.CompilerParams(vmem_limit_bytes=24 * 1024 * 1024)
 
 
@@ -212,7 +214,7 @@
 
 
 def time_kernel(
-    hidden_ref, cos_ref, sin_ref, qkv_ref, out_w_ref, layer_ref, query, keys, values, mix
+    hidden_ref, cos_ref, sin_ref, qkv_ref, out_w_ref, own_ref, partner_ref, query, keys, values, mix, layer
 ):
     rows, width = hidden_ref.shape
     frames = cos_ref.shape[0]
@@ -252,8 +254,42 @@
     added = (hidden_ref[...].astype(jnp.float32) + dot(mix[...], out_w_ref[...])).astype(jnp.bfloat16)
     per_half = frames // 2
     for j in range(frames):
-        frame = 2 * (j % per_half) + j // per_half
-        layer_ref[frame * group : (frame + 1) * group, :] = added[j * group : (j + 1) * group, :]
+        target = (j % 2) * per_half + (j % per_half) // 2 * 2 + j // per_half
+        layer[target * group : (target + 1) * group, :] = added[j * group : (j + 1) * group, :]
+    core = lax.axis_index("core")
+    own_ref[...] = layer[pl.ds(pl.multiple_of(core * (rows // 2), rows // 2), rows // 2), :]
+    partner_ref[...] = layer[pl.ds(pl.multiple_of((1 - core) * (rows // 2), rows // 2), rows // 2), :]
+
+
+def join_kernel(own_ref, partner_ref, *chunk_refs):
+    chip, core = lax.axis_index("chip"), lax.axis_index("core")
+    rows = own_ref.shape[0] // len(chunk_refs)
+    group = rows // 2
+    for d, chunk_ref in zip(EXCHANGES, chunk_refs):
+        for frame in range(2):
+            at = pl.ds(pl.multiple_of((chip ^ d) * rows + frame * group, group), group)
+            here = pl.ds(pl.multiple_of(frame * rows + core * group, group), group)
+            there = pl.ds(pl.multiple_of(frame * rows + (1 - core) * group, group), group)
+            chunk_ref[here, :] = own_ref[at, :]
+            chunk_ref[there, :] = partner_ref[at, :]
+
+
+def assemble_kernel(*refs):
+    *chunk_refs, layer_ref, semaphores = refs
+    chip = lax.axis_index("chip")
+    rows = chunk_refs[0].shape[0] // 2
+    moves = []
+    for d, chunk_ref in zip(EXCHANGES, chunk_refs):
+        at = pl.ds(pl.multiple_of((chip ^ d) * rows, rows), rows)
+        for frame in range(2):
+            moves.append(
+                pltpu.make_async_copy(
+                    chunk_ref.at[pl.ds(frame * rows, rows), :], layer_ref.at[frame, at, :], semaphores.at[2 * d + frame]
+                )
+            )
+            moves[-1].start()
+    for move in moves:
+        move.wait()
 
 
 def shards(activations, contacts, frame_index, spatial_qkv, spatial_out, time_qkv, time_out):
@@ -355,23 +391,45 @@
     group = rows // members
     hidden = lax.all_to_all(hidden.reshape(members, group, width), COLUMN, 0, 0, tiled=True)
 
-    layer = pl.pallas_call(
+    chips = lax.axis_size("chip")
+    part_of_rows = pltpu.VMEM((rows // 2, width), bf16)
+    own, partner = pl.pallas_call(
         time_kernel,
-        out_shape=pltpu.VMEM((rows, width), bf16),
+        out_shape=(part_of_rows, part_of_rows),
         in_specs=[VMEM] * 5,
-        out_specs=VMEM,
+        out_specs=(VMEM, VMEM),
         scratch_shapes=[
             pltpu.VMEM((width // PAIR, 2 * rows, PAIR), bf16),
             pltpu.VMEM((rows, width), bf16),
             pltpu.VMEM((width // PAIR, rows, 2 * PAIR), bf16),
             pltpu.VMEM((rows, width), bf16),
+            pltpu.VMEM((rows, width), bf16),
         ],
         compiler_params=LIMIT,
         name="temporal",
     )(hidden.reshape(rows, width), cosine, sine, time_qkv, time_out)
-    return lax.all_to_all(
-        layer.reshape(members, group, width), ("chip", "core"), 0, 1, tiled=True
-    )
+    partner = lax.ppermute(partner, "core", [(0, 1), (1, 0)])
+    chunk = pltpu.VMEM((rows // chips, width), bf16)
+    chunks = pl.pallas_call(
+        join_kernel,
+        out_shape=(chunk,) * chips,
+        in_specs=[VMEM] * 2,
+        out_specs=(VMEM,) * chips,
+        compiler_params=SMALL,
+        name="join",
+    )(own, partner)
+    chunks = [chunks[0]] + [
+        lax.ppermute(piece, "chip", [(i, i ^ d) for i in range(chips)]) for d, piece in zip(EXCHANGES[1:], chunks[1:])
+    ]
+    return pl.pallas_call(
+        assemble_kernel,
+        out_shape=pltpu.HBM((frames_dev, block, width), bf16),
+        in_specs=[VMEM] * chips,
+        out_specs=HBM,
+        scratch_shapes=[pltpu.SemaphoreType.DMA((2 * chips,))],
+        compiler_params=SMALL,
+        name="assemble",
+    )(*chunks)
 
 
 def solution(mesh):

time: 68.2 us -> 65.4 us (0.959)
  blocking collectives: 38.5 us -> 24.3 us
  waiting for transfers between devices: 2.96 us -> 11.2 us
  starting transfers between devices: 12.5 us -> 15.3 us
  Pallas kernels: 12.6 us -> 13.5 us
  local copies, waits for them, and re-layouts: 0.77 us -> 0 us
    all_to_all x1 -> x0, blocking collectives: 14.2 us -> none  [shards(): lax.all_to_all(layer.reshape(members, group, width), ('chip', 'core'), 0,...]
    ppermute x0 -> x4, waiting for transfers between devices: none -> 8.21 us  [the longest x3 6.78 us: shards(): lax.ppermute(piece, 'chip', [(i, i ^ d) for i in range(chips)])]
    ppermute x0 -> x4, starting transfers between devices: none -> 2.83 us  [the longest x3 2.74 us: shards(): lax.ppermute(piece, 'chip', [(i, i ^ d) for i in range(chips)])]
    pallas_call x1 -> x3, Pallas kernels: 2.85 us -> 3.72 us  [the longest x1 2.9 us: shards(): pl.pallas_call(time_kernel, out_shape=(part_of_rows, part_of_rows), in_sp...]
    all_to_all x1 -> x0, local copies, waits for them, and re-layouts: 0.77 us -> none  [shards(): lax.all_to_all(layer.reshape(members, group, width), ('chip', 'core'), 0,...]
  transfers between devices with their start and end apart: 5 -> 9, of which waited for: 2 -> 5; matrix products, arithmetic and copies ran while one was open for 0% -> 0% of each run, Pallas kernels for 9% -> 10%
where the time goes in v7:
time: 65.4 us; the launch traced here: 64.3 us
  blocking collectives  24.3 us (37%)
  starting transfers between devices  15.3 us (23%)
  Pallas kernels  13.5 us (21%)
  waiting for transfers between devices  11.2 us (17%)
    all_to_all x1, blocking collectives, shards(): lax.all_to_all(hidden.reshape(members, group, width), COLUMN, 0, 0, tiled...  24.3 us
    ppermute x1, starting transfers between devices, shards(): other = lax.ppermute(given, 'half', [(0, 1), (1, 0)])  7.83 us
    ppermute x3, waiting for transfers between devices, shards(): lax.ppermute(piece, 'chip', [(i, i ^ d) for i in range(chips)])  6.78 us
    ppermute x4, starting transfers between devices, from_neighbours(): return (lax.ppermute(tile, axes, odd), lax.ppermute(tile, axes, even))  4.64 us
    pallas_call x1, Pallas kernels, shards(): pl.pallas_call(early_kernel, out_shape=(pltpu.VMEM((width // PAIR, 2 * ro...  3.39 us
    ppermute x4, waiting for transfers between devices, from_neighbours(): return (lax.ppermute(tile, axes, odd), lax.ppermute(tile, axes, even))  2.96 us
    pallas_call x1, Pallas kernels, shards(): pl.pallas_call(first_kernel, out_shape=(pltpu.VMEM(spatial_qkv.shape, bf1...  2.91 us
    pallas_call x1, Pallas kernels, shards(): pl.pallas_call(time_kernel, out_shape=(part_of_rows, part_of_rows), in_sp...  2.9 us
  transfers between devices with their start and end apart: 9, of which 5 were waited for; matrix products, arithmetic and copies ran while one was open for 0% of the time, Pallas kernels for 10%

profile of v7, /device:TPU:1, one launch (start us, length us, event | category | flops | bytes accessed | tf_op | source)
XLA Modules:
  0.0 64.3 jit_solution(11069702739941687749)
XLA Ops:
  0.0 0.9 %give.1.given_ref = bf16[128,768]{1,0:T(8,128)(2,1)S(1)} custom-call(bf16[2,128,768]{2,1,0:T(8,128)(2,1)} %act_ref.3), custom_call_target="tpu_custom_call" | custom-call | tf_op jit(solution)/shard_map/give/pallas_call | solution.py:304
  0.9 7.8 %collective-permute-start.2 = (bf16[128,768]{1,0:T(8,128)(2,1)S(1)}, bf16[128,768]{1,0:T(8,128)(2,1)S(1)}, u32[]{:S(2)}, u32[]{:S(2)}) collective-permute-start(bf16[128,768]{1,0:T(8,128)(2,1)S(1)} %give.1.given_ref), channel_id=1, source_target_pairs={{0,8},{8,0},{1,9},{9,1},{2,10},{10,2},{3,11},{11,3},{4,12},{12,4},... | collective-permute-start | bytes 589832 | tf_op jit(solution)/shard_map/ppermute | solution.py:312
  8.8 2.9 %first.1 = (bf16[768,2304]{1,0:T(8,128)(2,1)S(1)}, bf16[128,768]{1,0:T(8,128)(2,1)S(1)}, bf16[128,768]{1,0:T(8,128)(2,1)S(1)}, bf16[128,768]{1,0:T(8,128)(2,1)S(...) custom-call(s32[5,32]{1,0:T(8,128)} %bitcast.5, ...), custom_call_target="tpu_custom_call" | custom-call | flops 452984832 | bytes 4000000 | tf_op jit(solution)/shard_map/first/pallas_call | solution.py:333
  11.7 1.0 %collective-permute-start = (bf16[128,768]{1,0:T(8,128)(2,1)S(1)}, bf16[128,768]{1,0:T(8,128)(2,1)S(1)}, u32[]{:S(2)}, u32[]{:S(2)}) collective-permute-start(bf16[128,768]{1,0:T(8,128)(2,1)S(1)} %get-tuple-element.33), channel_id=1, source_target_pairs={{0,1},{1,0},{2,3},{3,2},{4,5},{5,4},{6,7},{7,6},{8,9},{9,8},{10,11... | collective-permute-start | bytes 589832 | tf_op jit(solution)/shard_map/ppermute | solution.py:327
  12.7 1.5 %collective-permute-start.1 = (bf16[128,768]{1,0:T(8,128)(2,1)S(1)}, bf16[128,768]{1,0:T(8,128)(2,1)S(1)}, u32[]{:S(2)}, u32[]{:S(2)}) collective-permute-start(bf16[128,768]{1,0:T(8,128)(2,1)S(1)} %get-tuple-element.33), channel_id=1, source_target_pairs={{0,16},{1,17},{2,18},{3,19},{4,20},{5,21},{6,22},{7,23},{8,24},{9,... | collective-permute-start | bytes 589832 | tf_op jit(solution)/shard_map/ppermute | solution.py:327
  14.2 0.0 collective-permute-done.2.other_ref
  14.2 1.5 %collective-permute-start.3 = (bf16[128,768]{1,0:T(8,128)(2,1)S(1)}, bf16[128,768]{1,0:T(8,128)(2,1)S(1)}, u32[]{:S(2)}, u32[]{:S(2)}) collective-permute-start(bf16[128,768]{1,0:T(8,128)(2,1)S(1)} %collective-permute-done.2.other_ref), channel_id=1, source_target_pairs={{0,1},{1,0},{2,3},{3,2},{4,5},{5,4},{6,7},{7,6},{8,9},{9,8},{10,11... | collective-permute-start | bytes 589832 | tf_op jit(solution)/shard_map/ppermute | solution.py:327
  15.7 0.6 collective-permute-start.4
  16.3 0.0 collective-permute-done.odd_ref
  16.3 1.9 %collective-permute-done.1.even_ref = bf16[128,768]{1,0:T(8,128)(2,1)S(1)} collective-permute-done((bf16[128,768]{1,0:T(8,128)(2,1)S(1)}, bf16[128,768]{1,0:T(8,128)(2,1)S(1)}, u32[]{:S(2)}, u32[]{:S(2)}) %collective-permute-start.1) | collective-permute-done | bytes 196640 | tf_op jit(solution)/shard_map/ppermute | solution.py:327
  18.2 3.4 %early.1 = (bf16[6,512,128]{2,1,0:T(8,128)(2,1)S(1)}, f32[256,768]{1,0:T(8,128)S(1)}, f32[6,512,128]{2,1,0:T(8,128)S(1)}, f32[256,768]{1,0:T(8,128)S(1)}, bf16[7...) custom-call(f32[2,512]{1,0:T(2,128)S(1)} %get-tuple-element.29.bias_ref, ...), custom_call_target="tpu_custom_call" | custom-call | flops 4000000000 | bytes 4000000 | tf_op jit(solution)/shard_map/early/pallas_call | solution.py:359
  21.6 0.0 collective-permute-done.3.odd_ref
  21.6 1.1 %collective-permute-done.4.even_ref = bf16[128,768]{1,0:T(8,128)(2,1)S(1)} collective-permute-done((bf16[128,768]{1,0:T(8,128)(2,1)S(1)}, bf16[128,768]{1,0:T(8,128)(2,1)S(1)}, u32[]{:S(2)}, u32[]{:S(2)}) %collective-permute-start.4) | collective-permute-done | bytes 196640 | tf_op jit(solution)/shard_map/ppermute | solution.py:327
  22.7 2.5 %late.1 = bf16[256,768]{1,0:T(8,128)(2,1)S(1)} custom-call(f32[2,256]{1,0:T(2,128)S(1)} %get-tuple-element.28.bias_ref, bf16[6,512,128]{2,1,0:T(8,128)(2,1)S(1)} %get-tuple-element.35.query_ref, f32[256,768]{1,0:T(8,128)S(1)} %get-tuple-element.36.sums_ref, f32[6,512,128]{2,1,0:T(8,128)S(1)} %get-tuple-element.37.tops_ref, ...), custom_call_target="tpu_custom_call" | custom-call | tf_op jit(solution)/shard_map/late/pallas_call | solution.py:374
  25.2 24.3 %all_to_all.5 = bf16[16,16,768]{2,1,0:T(8,128)(2,1)S(1)} all-to-all(bf16[16,16,768]{2,1,0:T(8,128)(2,1)S(1)} %bitcast.4), channel_id=1, replica_groups=mesh['pair'=16,'half'=2,'chip'=4,'core'=2] {'half','chip','core'}, dimensions={0} | all-to-all | bytes 786432 | tf_op jit(solution)/shard_map/all_to_all | solution.py:392
  49.5 2.9 %temporal.1 = (bf16[128,768]{1,0:T(8,128)(2,1)S(1)}, bf16[128,768]{1,0:T(8,128)(2,1)S(1)}) custom-call(bf16[256,768]{1,0:T(8,128)(2,1)S(1)} %bitcast.3, f32[16,128]{1,0:T(8,128)S(1)} %get-tuple-element.41.cos_ref, f32[16,128]{1,0:T(8,128)S(1)} %get-tuple-element.42.sin_ref, bf16[768,2304]{1,0:T(8,128)(2,1)S(1)} %get-tuple-element.43.qkv_ref, ...), custom_call_target="tpu_custom_call" | custom-call | tf_op jit(solution)/shard_map/temporal/pallas_call | solution.py:396
  52.4 0.1 collective-permute-start.5
  52.5 1.4 %collective-permute-done.5.partner_ref = bf16[128,768]{1,0:T(8,128)(2,1)S(1)} collective-permute-done((bf16[128,768]{1,0:T(8,128)(2,1)S(1)}, bf16[128,768]{1,0:T(8,128)(2,1)S(1)}, u32[]{:S(2)}, u32[]{:S(2)}) %collective-permute-start.5) | collective-permute-done | bytes 196640 | tf_op jit(solution)/shard_map/ppermute | solution.py:411
  54.0 0.2 collective-permute-start.6
  54.1 1.1 %collective-permute-start.7 = (bf16[64,768]{1,0:T(8,128)(2,1)S(1)}, bf16[64,768]{1,0:T(8,128)(2,1)S(1)}, u32[]{:S(2)}, u32[]{:S(2)}) collective-permute-start(bf16[64,768]{1,0:T(8,128)(2,1)S(1)} %get-tuple-element.49), channel_id=1, source_target_pairs={{0,6},{2,4},{4,2},{6,0},{1,7},{3,5},{5,3},{7,1},{8,14},{10,12},{12... | collective-permute-start | bytes 294920 | tf_op jit(solution)/shard_map/ppermute | solution.py:422
  55.2 1.5 %collective-permute-start.8 = (bf16[64,768]{1,0:T(8,128)(2,1)S(1)}, bf16[64,768]{1,0:T(8,128)(2,1)S(1)}, u32[]{:S(2)}, u32[]{:S(2)}) collective-permute-start(bf16[64,768]{1,0:T(8,128)(2,1)S(1)} %get-tuple-element.50), channel_id=1, source_target_pairs={{0,2},{2,0},{4,6},{6,4},{1,3},{3,1},{5,7},{7,5},{8,10},{10,8},{12,... | collective-permute-start | bytes 294920 | tf_op jit(solution)/shard_map/ppermute | solution.py:422
  56.7 6.1 %collective-permute-done.6.refs_1_ = bf16[64,768]{1,0:T(8,128)(2,1)S(1)} collective-permute-done((bf16[64,768]{1,0:T(8,128)(2,1)S(1)}, bf16[64,768]{1,0:T(8,128)(2,1)S(1)}, u32[]{:S(2)}, u32[]{:S(2)}) %collective-permute-start.6) | collective-permute-done | bytes 98336 | tf_op jit(solution)/shard_map/ppermute | solution.py:422
  62.8 0.0 collective-permute-done.7.refs_2_
  62.8 0.7 %collective-permute-done.8.refs_3_ = bf16[64,768]{1,0:T(8,128)(2,1)S(1)} collective-permute-done((bf16[64,768]{1,0:T(8,128)(2,1)S(1)}, bf16[64,768]{1,0:T(8,128)(2,1)S(1)}, u32[]{:S(2)}, u32[]{:S(2)}) %collective-permute-start.8) | collective-permute-done | bytes 98336 | tf_op jit(solution)/shard_map/ppermute | solution.py:422
  63.5 0.8 %assemble.1 = bf16[2,128,768]{2,1,0:T(8,128)(2,1)} custom-call(bf16[64,768]{1,0:T(8,128)(2,1)S(1)} %get-tuple-element.47.refs_0_, bf16[64,768]{1,0:T(8,128)(2,1)S(1)} %collective-permute-done.6.refs_1_, bf16[64,768]{1,0:T(8,128)(2,1)S(1)} %collective-permute-done.7.refs_2_, bf16[64,768]{1,0:T(8,128)(2,1)S(1)} %collective-permute-done.8.refs_3_), custom_call_target="tpu_custom_call" | custom-call | tf_op jit(solution)/shard_map/assemble/pallas_call | solution.py:424
  (1 shorter events, 0.0 us)
Async XLA Ops:
  0.9 13.3 %collective-permute-start.2 = (bf16[128,768]{1,0:T(8,128)(2,1)S(1)}, bf16[128,768]{1,0:T(8,128)(2,1)S(1)}, u32[]{:S(2)}, u32[]{:S(2)}) collective-permute-start(bf16[128,768]{1,0:T(8,128)(2,1)S(1)} %give.1.given_ref), channel_id=1, source_target_pairs={{0,8},{8,0},{1,9},{9,1},{2,10},{10,2},{3,11},{11,3},{4,12},{12,4},... | collective-permute-start | bytes 589832 | tf_op jit(solution)/shard_map/ppermute | solution.py:312
  11.7 4.6 %collective-permute-start = (bf16[128,768]{1,0:T(8,128)(2,1)S(1)}, bf16[128,768]{1,0:T(8,128)(2,1)S(1)}, u32[]{:S(2)}, u32[]{:S(2)}) collective-permute-start(bf16[128,768]{1,0:T(8,128)(2,1)S(1)} %get-tuple-element.33), channel_id=1, source_target_pairs={{0,1},{1,0},{2,3},{3,2},{4,5},{5,4},{6,7},{7,6},{8,9},{9,8},{10,11... | collective-permute-start | bytes 589832 | tf_op jit(solution)/shard_map/ppermute | solution.py:327
  12.7 5.5 %collective-permute-start.1 = (bf16[128,768]{1,0:T(8,128)(2,1)S(1)}, bf16[128,768]{1,0:T(8,128)(2,1)S(1)}, u32[]{:S(2)}, u32[]{:S(2)}) collective-permute-start(bf16[128,768]{1,0:T(8,128)(2,1)S(1)} %get-tuple-element.33), channel_id=1, source_target_pairs={{0,16},{1,17},{2,18},{3,19},{4,20},{5,21},{6,22},{7,23},{8,24},{9,... | collective-permute-start | bytes 589832 | tf_op jit(solution)/shard_map/ppermute | solution.py:327
  14.2 7.4 %collective-permute-start.3 = (bf16[128,768]{1,0:T(8,128)(2,1)S(1)}, bf16[128,768]{1,0:T(8,128)(2,1)S(1)}, u32[]{:S(2)}, u32[]{:S(2)}) collective-permute-start(bf16[128,768]{1,0:T(8,128)(2,1)S(1)} %collective-permute-done.2.other_ref), channel_id=1, source_target_pairs={{0,1},{1,0},{2,3},{3,2},{4,5},{5,4},{6,7},{7,6},{8,9},{9,8},{10,11... | collective-permute-start | bytes 589832 | tf_op jit(solution)/shard_map/ppermute | solution.py:327
  15.7 7.0 %collective-permute-start.4 = (bf16[128,768]{1,0:T(8,128)(2,1)S(1)}, bf16[128,768]{1,0:T(8,128)(2,1)S(1)}, u32[]{:S(2)}, u32[]{:S(2)}) collective-permute-start(bf16[128,768]{1,0:T(8,128)(2,1)S(1)} %collective-permute-done.2.other_ref), channel_id=1, source_target_pairs={{0,16},{1,17},{2,18},{3,19},{4,20},{5,21},{6,22},{7,23},{8,24},{9,... | collective-permute-start | bytes 589832 | tf_op jit(solution)/shard_map/ppermute | solution.py:327
  52.4 1.5 %collective-permute-start.5 = (bf16[128,768]{1,0:T(8,128)(2,1)S(1)}, bf16[128,768]{1,0:T(8,128)(2,1)S(1)}, u32[]{:S(2)}, u32[]{:S(2)}) collective-permute-start(bf16[128,768]{1,0:T(8,128)(2,1)S(1)} %get-tuple-element.46), channel_id=1, source_target_pairs={{0,1},{1,0},{2,3},{3,2},{4,5},{5,4},{6,7},{7,6},{8,9},{9,8},{10,11... | collective-permute-start | bytes 589832 | tf_op jit(solution)/shard_map/ppermute | solution.py:411
  54.0 8.8 %collective-permute-start.6 = (bf16[64,768]{1,0:T(8,128)(2,1)S(1)}, bf16[64,768]{1,0:T(8,128)(2,1)S(1)}, u32[]{:S(2)}, u32[]{:S(2)}) collective-permute-start(bf16[64,768]{1,0:T(8,128)(2,1)S(1)} %get-tuple-element.48), channel_id=1, source_target_pairs={{0,4},{2,6},{4,0},{6,2},{1,5},{3,7},{5,1},{7,3},{8,12},{10,14},{12... | collective-permute-start | bytes 294920 | tf_op jit(solution)/shard_map/ppermute | solution.py:422
  54.1 8.6 %collective-permute-start.7 = (bf16[64,768]{1,0:T(8,128)(2,1)S(1)}, bf16[64,768]{1,0:T(8,128)(2,1)S(1)}, u32[]{:S(2)}, u32[]{:S(2)}) collective-permute-start(bf16[64,768]{1,0:T(8,128)(2,1)S(1)} %get-tuple-element.49), channel_id=1, source_target_pairs={{0,6},{2,4},{4,2},{6,0},{1,7},{3,5},{5,3},{7,1},{8,14},{10,12},{12... | collective-permute-start | bytes 294920 | tf_op jit(solution)/shard_map/ppermute | solution.py:422
  55.2 8.3 %collective-permute-start.8 = (bf16[64,768]{1,0:T(8,128)(2,1)S(1)}, bf16[64,768]{1,0:T(8,128)(2,1)S(1)}, u32[]{:S(2)}, u32[]{:S(2)}) collective-permute-start(bf16[64,768]{1,0:T(8,128)(2,1)S(1)} %get-tuple-element.50), channel_id=1, source_target_pairs={{0,2},{2,0},{4,6},{6,4},{1,3},{3,1},{5,7},{7,5},{8,10},{10,8},{12,... | collective-permute-start | bytes 294920 | tf_op jit(solution)/shard_map/ppermute | solution.py:422

commit v8 on v7

--- a/solution.py
+++ b/solution.py
@@ -11,8 +11,7 @@
 HEAD = 64
 PAIR = 2 * HEAD
 EXCLUDED = -1e30
-LOG2E = 1.4426950408889634
-SCALE = LOG2E / 8.0
+SCALE = HEAD ** (-0.5)
 EXCHANGES = (0, 2, 3, 1)
 COLUMN = ("half", "chip", "core")
 VMEM = pl.BlockSpec(memory_space=pltpu.VMEM)
@@ -69,7 +68,7 @@
         top = jnp.broadcast_to(jnp.max(scores, axis=-1, keepdims=True), (scores.shape[0], PAIR))
         if floors is not None:
             top = jnp.maximum(top, floors[pair])
-        expo = jnp.exp2(scores - jnp.concatenate([top] * (width // PAIR), axis=1)).astype(jnp.bfloat16)
+        expo = jnp.exp(scores - jnp.concatenate([top] * (width // PAIR), axis=1)).astype(jnp.bfloat16)
         finish(pair, top, dot(expo, values[pair]))
         scores = ahead
 
@@ -201,7 +200,7 @@
 
     def finish(pair, top, product):
         at = slice(pair * PAIR, (pair + 1) * PAIR)
-        share = side_by_side(jnp.exp2(tops_ref[pair] - top))
+        share = side_by_side(jnp.exp(tops_ref[pair] - top))
         total = totals_ref[:, at] * share + side_by_side(product[:, PAIR:])
         mix[:, at] = ((sums_ref[:, at] * share + side_by_side(product)) / total).astype(jnp.bfloat16)
 

time: 65.4 us -> 65.5 us (level)
  no operation moved by 1% of the time
where the time goes in v8:
time: 65.5 us; the launch traced here: 64.4 us
  blocking collectives  24.3 us (37%)
  starting transfers between devices  15.3 us (23%)
  Pallas kernels  13.7 us (21%)
  waiting for transfers between devices  11 us (17%)
    all_to_all x1, blocking collectives, shards(): lax.all_to_all(hidden.reshape(members, group, width), COLUMN, 0, 0, tiled...  24.3 us
    ppermute x1, starting transfers between devices, shards(): other = lax.ppermute(given, 'half', [(0, 1), (1, 0)])  7.83 us
    ppermute x3, waiting for transfers between devices, shards(): lax.ppermute(piece, 'chip', [(i, i ^ d) for i in range(chips)])  6.78 us
    ppermute x4, starting transfers between devices, from_neighbours(): return (lax.ppermute(tile, axes, odd), lax.ppermute(tile, axes, even))  4.64 us
    pallas_call x1, Pallas kernels, shards(): pl.pallas_call(early_kernel, out_shape=(pltpu.VMEM((width // PAIR, 2 * ro...  3.57 us
    pallas_call x1, Pallas kernels, shards(): pl.pallas_call(time_kernel, out_shape=(part_of_rows, part_of_rows), in_sp...  2.91 us
    pallas_call x1, Pallas kernels, shards(): pl.pallas_call(first_kernel, out_shape=(pltpu.VMEM(spatial_qkv.shape, bf1...  2.91 us
    ppermute x4, waiting for transfers between devices, from_neighbours(): return (lax.ppermute(tile, axes, odd), lax.ppermute(tile, axes, even))  2.78 us
  transfers between devices with their start and end apart: 9, of which 5 were waited for; matrix products, arithmetic and copies ran while one was open for 0% of the time, Pallas kernels for 10%

profile of v8, /device:TPU:1, one launch (start us, length us, event | category | flops | bytes accessed | tf_op | source)
XLA Modules:
  0.0 64.4 jit_solution(14199346485212619675)
XLA Ops:
  0.0 0.9 %give.1.given_ref = bf16[128,768]{1,0:T(8,128)(2,1)S(1)} custom-call(bf16[2,128,768]{2,1,0:T(8,128)(2,1)} %act_ref.3), custom_call_target="tpu_custom_call" | custom-call | tf_op jit(solution)/shard_map/give/pallas_call | solution.py:303
  0.9 7.8 %collective-permute-start.2 = (bf16[128,768]{1,0:T(8,128)(2,1)S(1)}, bf16[128,768]{1,0:T(8,128)(2,1)S(1)}, u32[]{:S(2)}, u32[]{:S(2)}) collective-permute-start(bf16[128,768]{1,0:T(8,128)(2,1)S(1)} %give.1.given_ref), channel_id=1, source_target_pairs={{0,8},{8,0},{1,9},{9,1},{2,10},{10,2},{3,11},{11,3},{4,12},{12,4},... | collective-permute-start | bytes 589832 | tf_op jit(solution)/shard_map/ppermute | solution.py:311
  8.8 2.9 %first.1 = (bf16[768,2304]{1,0:T(8,128)(2,1)S(1)}, bf16[128,768]{1,0:T(8,128)(2,1)S(1)}, bf16[128,768]{1,0:T(8,128)(2,1)S(1)}, bf16[128,768]{1,0:T(8,128)(2,1)S(...) custom-call(s32[5,32]{1,0:T(8,128)} %bitcast.5, ...), custom_call_target="tpu_custom_call" | custom-call | flops 452984832 | bytes 4000000 | tf_op jit(solution)/shard_map/first/pallas_call | solution.py:332
  11.7 1.0 %collective-permute-start = (bf16[128,768]{1,0:T(8,128)(2,1)S(1)}, bf16[128,768]{1,0:T(8,128)(2,1)S(1)}, u32[]{:S(2)}, u32[]{:S(2)}) collective-permute-start(bf16[128,768]{1,0:T(8,128)(2,1)S(1)} %get-tuple-element.33), channel_id=1, source_target_pairs={{0,1},{1,0},{2,3},{3,2},{4,5},{5,4},{6,7},{7,6},{8,9},{9,8},{10,11... | collective-permute-start | bytes 589832 | tf_op jit(solution)/shard_map/ppermute | solution.py:326
  12.7 1.5 %collective-permute-start.1 = (bf16[128,768]{1,0:T(8,128)(2,1)S(1)}, bf16[128,768]{1,0:T(8,128)(2,1)S(1)}, u32[]{:S(2)}, u32[]{:S(2)}) collective-permute-start(bf16[128,768]{1,0:T(8,128)(2,1)S(1)} %get-tuple-element.33), channel_id=1, source_target_pairs={{0,16},{1,17},{2,18},{3,19},{4,20},{5,21},{6,22},{7,23},{8,24},{9,... | collective-permute-start | bytes 589832 | tf_op jit(solution)/shard_map/ppermute | solution.py:326
  14.2 0.0 collective-permute-done.2.other_ref
  14.2 1.5 %collective-permute-start.3 = (bf16[128,768]{1,0:T(8,128)(2,1)S(1)}, bf16[128,768]{1,0:T(8,128)(2,1)S(1)}, u32[]{:S(2)}, u32[]{:S(2)}) collective-permute-start(bf16[128,768]{1,0:T(8,128)(2,1)S(1)} %collective-permute-done.2.other_ref), channel_id=1, source_target_pairs={{0,1},{1,0},{2,3},{3,2},{4,5},{5,4},{6,7},{7,6},{8,9},{9,8},{10,11... | collective-permute-start | bytes 589832 | tf_op jit(solution)/shard_map/ppermute | solution.py:326
  15.7 0.6 collective-permute-start.4
  16.3 0.0 collective-permute-done.odd_ref
  16.3 1.9 %collective-permute-done.1.even_ref = bf16[128,768]{1,0:T(8,128)(2,1)S(1)} collective-permute-done((bf16[128,768]{1,0:T(8,128)(2,1)S(1)}, bf16[128,768]{1,0:T(8,128)(2,1)S(1)}, u32[]{:S(2)}, u32[]{:S(2)}) %collective-permute-start.1) | collective-permute-done | bytes 196640 | tf_op jit(solution)/shard_map/ppermute | solution.py:326
  18.2 3.6 %early.1 = (bf16[6,512,128]{2,1,0:T(8,128)(2,1)S(1)}, f32[256,768]{1,0:T(8,128)S(1)}, f32[6,512,128]{2,1,0:T(8,128)S(1)}, f32[256,768]{1,0:T(8,128)S(1)}, bf16[7...) custom-call(f32[2,512]{1,0:T(2,128)S(1)} %get-tuple-element.29.bias_ref, ...), custom_call_target="tpu_custom_call" | custom-call | flops 4000000000 | bytes 4000000 | tf_op jit(solution)/shard_map/early/pallas_call | solution.py:358
  21.8 0.0 collective-permute-done.3.odd_ref
  21.8 0.9 %collective-permute-done.4.even_ref = bf16[128,768]{1,0:T(8,128)(2,1)S(1)} collective-permute-done((bf16[128,768]{1,0:T(8,128)(2,1)S(1)}, bf16[128,768]{1,0:T(8,128)(2,1)S(1)}, u32[]{:S(2)}, u32[]{:S(2)}) %collective-permute-start.4) | collective-permute-done | bytes 196640 | tf_op jit(solution)/shard_map/ppermute | solution.py:326
  22.7 2.6 %late.1 = bf16[256,768]{1,0:T(8,128)(2,1)S(1)} custom-call(f32[2,256]{1,0:T(2,128)S(1)} %get-tuple-element.28.bias_ref, bf16[6,512,128]{2,1,0:T(8,128)(2,1)S(1)} %get-tuple-element.35.query_ref, f32[256,768]{1,0:T(8,128)S(1)} %get-tuple-element.36.sums_ref, f32[6,512,128]{2,1,0:T(8,128)S(1)} %get-tuple-element.37.tops_ref, ...), custom_call_target="tpu_custom_call" | custom-call | tf_op jit(solution)/shard_map/late/pallas_call | solution.py:373
  25.3 24.3 %all_to_all.5 = bf16[16,16,768]{2,1,0:T(8,128)(2,1)S(1)} all-to-all(bf16[16,16,768]{2,1,0:T(8,128)(2,1)S(1)} %bitcast.4), channel_id=1, replica_groups=mesh['pair'=16,'half'=2,'chip'=4,'core'=2] {'half','chip','core'}, dimensions={0} | all-to-all | bytes 786432 | tf_op jit(solution)/shard_map/all_to_all | solution.py:391
  49.6 2.9 %temporal.1 = (bf16[128,768]{1,0:T(8,128)(2,1)S(1)}, bf16[128,768]{1,0:T(8,128)(2,1)S(1)}) custom-call(bf16[256,768]{1,0:T(8,128)(2,1)S(1)} %bitcast.3, f32[16,128]{1,0:T(8,128)S(1)} %get-tuple-element.41.cos_ref, f32[16,128]{1,0:T(8,128)S(1)} %get-tuple-element.42.sin_ref, bf16[768,2304]{1,0:T(8,128)(2,1)S(1)} %get-tuple-element.43.qkv_ref, ...), custom_call_target="tpu_custom_call" | custom-call | tf_op jit(solution)/shard_map/temporal/pallas_call | solution.py:395
  52.5 0.1 collective-permute-start.5
  52.6 1.4 %collective-permute-done.5.partner_ref = bf16[128,768]{1,0:T(8,128)(2,1)S(1)} collective-permute-done((bf16[128,768]{1,0:T(8,128)(2,1)S(1)}, bf16[128,768]{1,0:T(8,128)(2,1)S(1)}, u32[]{:S(2)}, u32[]{:S(2)}) %collective-permute-start.5) | collective-permute-done | bytes 196640 | tf_op jit(solution)/shard_map/ppermute | solution.py:410
  54.1 0.2 collective-permute-start.6
  54.2 1.1 %collective-permute-start.7 = (bf16[64,768]{1,0:T(8,128)(2,1)S(1)}, bf16[64,768]{1,0:T(8,128)(2,1)S(1)}, u32[]{:S(2)}, u32[]{:S(2)}) collective-permute-start(bf16[64,768]{1,0:T(8,128)(2,1)S(1)} %get-tuple-element.49), channel_id=1, source_target_pairs={{0,6},{2,4},{4,2},{6,0},{1,7},{3,5},{5,3},{7,1},{8,14},{10,12},{12... | collective-permute-start | bytes 294920 | tf_op jit(solution)/shard_map/ppermute | solution.py:421
  55.3 1.5 %collective-permute-start.8 = (bf16[64,768]{1,0:T(8,128)(2,1)S(1)}, bf16[64,768]{1,0:T(8,128)(2,1)S(1)}, u32[]{:S(2)}, u32[]{:S(2)}) collective-permute-start(bf16[64,768]{1,0:T(8,128)(2,1)S(1)} %get-tuple-element.50), channel_id=1, source_target_pairs={{0,2},{2,0},{4,6},{6,4},{1,3},{3,1},{5,7},{7,5},{8,10},{10,8},{12,... | collective-permute-start | bytes 294920 | tf_op jit(solution)/shard_map/ppermute | solution.py:421
  56.8 6.1 %collective-permute-done.6.refs_1_ = bf16[64,768]{1,0:T(8,128)(2,1)S(1)} collective-permute-done((bf16[64,768]{1,0:T(8,128)(2,1)S(1)}, bf16[64,768]{1,0:T(8,128)(2,1)S(1)}, u32[]{:S(2)}, u32[]{:S(2)}) %collective-permute-start.6) | collective-permute-done | bytes 98336 | tf_op jit(solution)/shard_map/ppermute | solution.py:421
  62.9 0.0 collective-permute-done.7.refs_2_
  62.9 0.7 %collective-permute-done.8.refs_3_ = bf16[64,768]{1,0:T(8,128)(2,1)S(1)} collective-permute-done((bf16[64,768]{1,0:T(8,128)(2,1)S(1)}, bf16[64,768]{1,0:T(8,128)(2,1)S(1)}, u32[]{:S(2)}, u32[]{:S(2)}) %collective-permute-start.8) | collective-permute-done | bytes 98336 | tf_op jit(solution)/shard_map/ppermute | solution.py:421
  63.6 0.8 %assemble.1 = bf16[2,128,768]{2,1,0:T(8,128)(2,1)} custom-call(bf16[64,768]{1,0:T(8,128)(2,1)S(1)} %get-tuple-element.47.refs_0_, bf16[64,768]{1,0:T(8,128)(2,1)S(1)} %collective-permute-done.6.refs_1_, bf16[64,768]{1,0:T(8,128)(2,1)S(1)} %collective-permute-done.7.refs_2_, bf16[64,768]{1,0:T(8,128)(2,1)S(1)} %collective-permute-done.8.refs_3_), custom_call_target="tpu_custom_call" | custom-call | tf_op jit(solution)/shard_map/assemble/pallas_call | solution.py:423
  (1 shorter events, 0.0 us)
Async XLA Ops:
  0.9 13.3 %collective-permute-start.2 = (bf16[128,768]{1,0:T(8,128)(2,1)S(1)}, bf16[128,768]{1,0:T(8,128)(2,1)S(1)}, u32[]{:S(2)}, u32[]{:S(2)}) collective-permute-start(bf16[128,768]{1,0:T(8,128)(2,1)S(1)} %give.1.given_ref), channel_id=1, source_target_pairs={{0,8},{8,0},{1,9},{9,1},{2,10},{10,2},{3,11},{11,3},{4,12},{12,4},... | collective-permute-start | bytes 589832 | tf_op jit(solution)/shard_map/ppermute | solution.py:311
  11.7 4.6 %collective-permute-start = (bf16[128,768]{1,0:T(8,128)(2,1)S(1)}, bf16[128,768]{1,0:T(8,128)(2,1)S(1)}, u32[]{:S(2)}, u32[]{:S(2)}) collective-permute-start(bf16[128,768]{1,0:T(8,128)(2,1)S(1)} %get-tuple-element.33), channel_id=1, source_target_pairs={{0,1},{1,0},{2,3},{3,2},{4,5},{5,4},{6,7},{7,6},{8,9},{9,8},{10,11... | collective-permute-start | bytes 589832 | tf_op jit(solution)/shard_map/ppermute | solution.py:326
  12.7 5.5 %collective-permute-start.1 = (bf16[128,768]{1,0:T(8,128)(2,1)S(1)}, bf16[128,768]{1,0:T(8,128)(2,1)S(1)}, u32[]{:S(2)}, u32[]{:S(2)}) collective-permute-start(bf16[128,768]{1,0:T(8,128)(2,1)S(1)} %get-tuple-element.33), channel_id=1, source_target_pairs={{0,16},{1,17},{2,18},{3,19},{4,20},{5,21},{6,22},{7,23},{8,24},{9,... | collective-permute-start | bytes 589832 | tf_op jit(solution)/shard_map/ppermute | solution.py:326
  14.2 7.6 %collective-permute-start.3 = (bf16[128,768]{1,0:T(8,128)(2,1)S(1)}, bf16[128,768]{1,0:T(8,128)(2,1)S(1)}, u32[]{:S(2)}, u32[]{:S(2)}) collective-permute-start(bf16[128,768]{1,0:T(8,128)(2,1)S(1)} %collective-permute-done.2.other_ref), channel_id=1, source_target_pairs={{0,1},{1,0},{2,3},{3,2},{4,5},{5,4},{6,7},{7,6},{8,9},{9,8},{10,11... | collective-permute-start | bytes 589832 | tf_op jit(solution)/shard_map/ppermute | solution.py:326
  15.7 7.0 %collective-permute-start.4 = (bf16[128,768]{1,0:T(8,128)(2,1)S(1)}, bf16[128,768]{1,0:T(8,128)(2,1)S(1)}, u32[]{:S(2)}, u32[]{:S(2)}) collective-permute-start(bf16[128,768]{1,0:T(8,128)(2,1)S(1)} %collective-permute-done.2.other_ref), channel_id=1, source_target_pairs={{0,16},{1,17},{2,18},{3,19},{4,20},{5,21},{6,22},{7,23},{8,24},{9,... | collective-permute-start | bytes 589832 | tf_op jit(solution)/shard_map/ppermute | solution.py:326
  52.5 1.5 %collective-permute-start.5 = (bf16[128,768]{1,0:T(8,128)(2,1)S(1)}, bf16[128,768]{1,0:T(8,128)(2,1)S(1)}, u32[]{:S(2)}, u32[]{:S(2)}) collective-permute-start(bf16[128,768]{1,0:T(8,128)(2,1)S(1)} %get-tuple-element.46), channel_id=1, source_target_pairs={{0,1},{1,0},{2,3},{3,2},{4,5},{5,4},{6,7},{7,6},{8,9},{9,8},{10,11... | collective-permute-start | bytes 589832 | tf_op jit(solution)/shard_map/ppermute | solution.py:410
  54.1 8.8 %collective-permute-start.6 = (bf16[64,768]{1,0:T(8,128)(2,1)S(1)}, bf16[64,768]{1,0:T(8,128)(2,1)S(1)}, u32[]{:S(2)}, u32[]{:S(2)}) collective-permute-start(bf16[64,768]{1,0:T(8,128)(2,1)S(1)} %get-tuple-element.48), channel_id=1, source_target_pairs={{0,4},{2,6},{4,0},{6,2},{1,5},{3,7},{5,1},{7,3},{8,12},{10,14},{12... | collective-permute-start | bytes 294920 | tf_op jit(solution)/shard_map/ppermute | solution.py:421
  54.2 8.6 %collective-permute-start.7 = (bf16[64,768]{1,0:T(8,128)(2,1)S(1)}, bf16[64,768]{1,0:T(8,128)(2,1)S(1)}, u32[]{:S(2)}, u32[]{:S(2)}) collective-permute-start(bf16[64,768]{1,0:T(8,128)(2,1)S(1)} %get-tuple-element.49), channel_id=1, source_target_pairs={{0,6},{2,4},{4,2},{6,0},{1,7},{3,5},{5,3},{7,1},{8,14},{10,12},{12... | collective-permute-start | bytes 294920 | tf_op jit(solution)/shard_map/ppermute | solution.py:421
  55.3 8.3 %collective-permute-start.8 = (bf16[64,768]{1,0:T(8,128)(2,1)S(1)}, bf16[64,768]{1,0:T(8,128)(2,1)S(1)}, u32[]{:S(2)}, u32[]{:S(2)}) collective-permute-start(bf16[64,768]{1,0:T(8,128)(2,1)S(1)} %get-tuple-element.50), channel_id=1, source_target_pairs={{0,2},{2,0},{4,6},{6,4},{1,3},{3,1},{5,7},{7,5},{8,10},{10,8},{12,... | collective-permute-start | bytes 294920 | tf_op jit(solution)/shard_map/ppermute | solution.py:421

commit v9 on v8

--- a/solution.py
+++ b/solution.py
@@ -19,6 +19,11 @@
 HBM = pl.BlockSpec(memory_space=pltpu.HBM)
 SMALL = pltpu.CompilerParams(vmem_limit_bytes=4 * 1024 * 1024)
 LIMIT = pltpu.CompilerParams(vmem_limit_bytes=24 * 1024 * 1024)
+
+
+def row_scale(rows):
+    widened = rows.astype(jnp.float32)
+    return lax.rsqrt(jnp.mean(widened * widened, axis=-1, keepdims=True) + 1e-06)
 
 
 def unit_rows(rows):
@@ -191,9 +196,10 @@
     half = lax.axis_index("half")
     block, width = other_ref.shape
     pairs = width // PAIR
-    tiles = unit_rows(jnp.concatenate([odd_ref[...], even_ref[...]], axis=0))
-    keys[...] = dot(tiles, qkv_ref[:, width : 2 * width]).astype(jnp.bfloat16)
-    fresh = dot(tiles, qkv_ref[:, 2 * width :]).astype(jnp.bfloat16)
+    tiles = jnp.concatenate([odd_ref[...], even_ref[...]], axis=0)
+    scale = row_scale(tiles)
+    keys[...] = (dot(tiles, qkv_ref[:, width : 2 * width]) * scale).astype(jnp.bfloat16)
+    fresh = (dot(tiles, qkv_ref[:, 2 * width :]) * scale).astype(jnp.bfloat16)
     for pair in range(pairs):
         values[pair, :, :PAIR] = fresh[:, pair * PAIR : (pair + 1) * PAIR]
         values[pair, :, PAIR:] = jnp.ones((2 * block, PAIR), jnp.bfloat16)
@@ -218,7 +224,7 @@
     rows, width = hidden_ref.shape
     frames = cos_ref.shape[0]
     group = rows // frames
-    normed = unit_rows(hidden_ref[...])
+    hidden = hidden_ref[...]
     cosine = jnp.concatenate(
         [jnp.broadcast_to(cos_ref[f : f + 1, :], (group, PAIR)) for f in range(frames)], axis=0
     )
@@ -234,7 +240,7 @@
         return entries.astype(jnp.float32) * cosine + dot(entries, exchange) * sine
 
     pairs = width // PAIR
-    projected = dot(normed, qkv_ref[...])
+    projected = dot(hidden, qkv_ref[...]) * row_scale(hidden)
     for pair in range(pairs):
         at = slice(pair * PAIR, (pair + 1) * PAIR)
         query[pair] = by_head((rotate(projected[:, at]) * SCALE).astype(jnp.bfloat16))

time: 65.5 us -> 65.2 us (level)
  no operation moved by 1% of the time
where the time goes in v9:
time: 65.2 us; the launch traced here: 64.1 us
  blocking collectives  24.3 us (37%)
  starting transfers between devices  15.3 us (23%)
  Pallas kernels  13.4 us (21%)
  waiting for transfers between devices  11 us (17%)
    all_to_all x1, blocking collectives, shards(): lax.all_to_all(hidden.reshape(members, group, width), COLUMN, 0, 0, tiled...  24.3 us
    ppermute x1, starting transfers between devices, shards(): other = lax.ppermute(given, 'half', [(0, 1), (1, 0)])  7.83 us
    ppermute x3, waiting for transfers between devices, shards(): lax.ppermute(piece, 'chip', [(i, i ^ d) for i in range(chips)])  6.78 us
    ppermute x4, starting transfers between devices, from_neighbours(): return (lax.ppermute(tile, axes, odd), lax.ppermute(tile, axes, even))  4.64 us
    pallas_call x1, Pallas kernels, shards(): pl.pallas_call(early_kernel, out_shape=(pltpu.VMEM((width // PAIR, 2 * ro...  3.57 us
    pallas_call x1, Pallas kernels, shards(): pl.pallas_call(first_kernel, out_shape=(pltpu.VMEM(spatial_qkv.shape, bf1...  2.91 us
    pallas_call x1, Pallas kernels, shards(): pl.pallas_call(time_kernel, out_shape=(part_of_rows, part_of_rows), in_sp...  2.8 us
    ppermute x4, waiting for transfers between devices, from_neighbours(): return (lax.ppermute(tile, axes, odd), lax.ppermute(tile, axes, even))  2.78 us
  transfers between devices with their start and end apart: 9, of which 5 were waited for; matrix products, arithmetic and copies ran while one was open for 0% of the time, Pallas kernels for 10%

profile of v9, /device:TPU:1, one launch (start us, length us, event | category | flops | bytes accessed | tf_op | source)
XLA Modules:
  0.0 64.1 jit_solution(9213892909632484369)
XLA Ops:
  0.0 0.9 %give.1.given_ref = bf16[128,768]{1,0:T(8,128)(2,1)S(1)} custom-call(bf16[2,128,768]{2,1,0:T(8,128)(2,1)} %act_ref.3), custom_call_target="tpu_custom_call" | custom-call | tf_op jit(solution)/shard_map/give/pallas_call | solution.py:309
  0.9 7.8 %collective-permute-start.2 = (bf16[128,768]{1,0:T(8,128)(2,1)S(1)}, bf16[128,768]{1,0:T(8,128)(2,1)S(1)}, u32[]{:S(2)}, u32[]{:S(2)}) collective-permute-start(bf16[128,768]{1,0:T(8,128)(2,1)S(1)} %give.1.given_ref), channel_id=1, source_target_pairs={{0,8},{8,0},{1,9},{9,1},{2,10},{10,2},{3,11},{11,3},{4,12},{12,4},... | collective-permute-start | bytes 589832 | tf_op jit(solution)/shard_map/ppermute | solution.py:317
  8.8 2.9 %first.1 = (bf16[768,2304]{1,0:T(8,128)(2,1)S(1)}, bf16[128,768]{1,0:T(8,128)(2,1)S(1)}, bf16[128,768]{1,0:T(8,128)(2,1)S(1)}, bf16[128,768]{1,0:T(8,128)(2,1)S(...) custom-call(s32[5,32]{1,0:T(8,128)} %bitcast.5, ...), custom_call_target="tpu_custom_call" | custom-call | flops 452984832 | bytes 4000000 | tf_op jit(solution)/shard_map/first/pallas_call | solution.py:338
  11.7 1.0 %collective-permute-start = (bf16[128,768]{1,0:T(8,128)(2,1)S(1)}, bf16[128,768]{1,0:T(8,128)(2,1)S(1)}, u32[]{:S(2)}, u32[]{:S(2)}) collective-permute-start(bf16[128,768]{1,0:T(8,128)(2,1)S(1)} %get-tuple-element.33), channel_id=1, source_target_pairs={{0,1},{1,0},{2,3},{3,2},{4,5},{5,4},{6,7},{7,6},{8,9},{9,8},{10,11... | collective-permute-start | bytes 589832 | tf_op jit(solution)/shard_map/ppermute | solution.py:332
  12.7 1.5 %collective-permute-start.1 = (bf16[128,768]{1,0:T(8,128)(2,1)S(1)}, bf16[128,768]{1,0:T(8,128)(2,1)S(1)}, u32[]{:S(2)}, u32[]{:S(2)}) collective-permute-start(bf16[128,768]{1,0:T(8,128)(2,1)S(1)} %get-tuple-element.33), channel_id=1, source_target_pairs={{0,16},{1,17},{2,18},{3,19},{4,20},{5,21},{6,22},{7,23},{8,24},{9,... | collective-permute-start | bytes 589832 | tf_op jit(solution)/shard_map/ppermute | solution.py:332
  14.2 0.0 collective-permute-done.2.other_ref
  14.2 1.5 %collective-permute-start.3 = (bf16[128,768]{1,0:T(8,128)(2,1)S(1)}, bf16[128,768]{1,0:T(8,128)(2,1)S(1)}, u32[]{:S(2)}, u32[]{:S(2)}) collective-permute-start(bf16[128,768]{1,0:T(8,128)(2,1)S(1)} %collective-permute-done.2.other_ref), channel_id=1, source_target_pairs={{0,1},{1,0},{2,3},{3,2},{4,5},{5,4},{6,7},{7,6},{8,9},{9,8},{10,11... | collective-permute-start | bytes 589832 | tf_op jit(solution)/shard_map/ppermute | solution.py:332
  15.7 0.6 collective-permute-start.4
  16.3 0.0 collective-permute-done.odd_ref
  16.3 1.9 %collective-permute-done.1.even_ref = bf16[128,768]{1,0:T(8,128)(2,1)S(1)} collective-permute-done((bf16[128,768]{1,0:T(8,128)(2,1)S(1)}, bf16[128,768]{1,0:T(8,128)(2,1)S(1)}, u32[]{:S(2)}, u32[]{:S(2)}) %collective-permute-start.1) | collective-permute-done | bytes 196640 | tf_op jit(solution)/shard_map/ppermute | solution.py:332
  18.2 3.6 %early.1 = (bf16[6,512,128]{2,1,0:T(8,128)(2,1)S(1)}, f32[256,768]{1,0:T(8,128)S(1)}, f32[6,512,128]{2,1,0:T(8,128)S(1)}, f32[256,768]{1,0:T(8,128)S(1)}, bf16[7...) custom-call(f32[2,512]{1,0:T(2,128)S(1)} %get-tuple-element.29.bias_ref, ...), custom_call_target="tpu_custom_call" | custom-call | flops 4000000000 | bytes 4000000 | tf_op jit(solution)/shard_map/early/pallas_call | solution.py:364
  21.8 0.0 collective-permute-done.3.odd_ref
  21.8 0.9 %collective-permute-done.4.even_ref = bf16[128,768]{1,0:T(8,128)(2,1)S(1)} collective-permute-done((bf16[128,768]{1,0:T(8,128)(2,1)S(1)}, bf16[128,768]{1,0:T(8,128)(2,1)S(1)}, u32[]{:S(2)}, u32[]{:S(2)}) %collective-permute-start.4) | collective-permute-done | bytes 196640 | tf_op jit(solution)/shard_map/ppermute | solution.py:332
  22.7 2.4 %late.1 = bf16[256,768]{1,0:T(8,128)(2,1)S(1)} custom-call(f32[2,256]{1,0:T(2,128)S(1)} %get-tuple-element.28.bias_ref, bf16[6,512,128]{2,1,0:T(8,128)(2,1)S(1)} %get-tuple-element.35.query_ref, f32[256,768]{1,0:T(8,128)S(1)} %get-tuple-element.36.sums_ref, f32[6,512,128]{2,1,0:T(8,128)S(1)} %get-tuple-element.37.tops_ref, ...), custom_call_target="tpu_custom_call" | custom-call | tf_op jit(solution)/shard_map/late/pallas_call | solution.py:379
  25.1 24.3 %all_to_all.5 = bf16[16,16,768]{2,1,0:T(8,128)(2,1)S(1)} all-to-all(bf16[16,16,768]{2,1,0:T(8,128)(2,1)S(1)} %bitcast.4), channel_id=1, replica_groups=mesh['pair'=16,'half'=2,'chip'=4,'core'=2] {'half','chip','core'}, dimensions={0} | all-to-all | bytes 786432 | tf_op jit(solution)/shard_map/all_to_all | solution.py:397
  49.4 2.8 %temporal.1 = (bf16[128,768]{1,0:T(8,128)(2,1)S(1)}, bf16[128,768]{1,0:T(8,128)(2,1)S(1)}) custom-call(bf16[256,768]{1,0:T(8,128)(2,1)S(1)} %bitcast.3, f32[16,128]{1,0:T(8,128)S(1)} %get-tuple-element.41.cos_ref, f32[16,128]{1,0:T(8,128)S(1)} %get-tuple-element.42.sin_ref, bf16[768,2304]{1,0:T(8,128)(2,1)S(1)} %get-tuple-element.43.qkv_ref, ...), custom_call_target="tpu_custom_call" | custom-call | tf_op jit(solution)/shard_map/temporal/pallas_call | solution.py:401
  52.2 0.1 collective-permute-start.5
  52.3 1.4 %collective-permute-done.5.partner_ref = bf16[128,768]{1,0:T(8,128)(2,1)S(1)} collective-permute-done((bf16[128,768]{1,0:T(8,128)(2,1)S(1)}, bf16[128,768]{1,0:T(8,128)(2,1)S(1)}, u32[]{:S(2)}, u32[]{:S(2)}) %collective-permute-start.5) | collective-permute-done | bytes 196640 | tf_op jit(solution)/shard_map/ppermute | solution.py:416
  53.8 0.2 collective-permute-start.6
  53.9 1.1 %collective-permute-start.7 = (bf16[64,768]{1,0:T(8,128)(2,1)S(1)}, bf16[64,768]{1,0:T(8,128)(2,1)S(1)}, u32[]{:S(2)}, u32[]{:S(2)}) collective-permute-start(bf16[64,768]{1,0:T(8,128)(2,1)S(1)} %get-tuple-element.49), channel_id=1, source_target_pairs={{0,6},{2,4},{4,2},{6,0},{1,7},{3,5},{5,3},{7,1},{8,14},{10,12},{12... | collective-permute-start | bytes 294920 | tf_op jit(solution)/shard_map/ppermute | solution.py:427
  55.0 1.5 %collective-permute-start.8 = (bf16[64,768]{1,0:T(8,128)(2,1)S(1)}, bf16[64,768]{1,0:T(8,128)(2,1)S(1)}, u32[]{:S(2)}, u32[]{:S(2)}) collective-permute-start(bf16[64,768]{1,0:T(8,128)(2,1)S(1)} %get-tuple-element.50), channel_id=1, source_target_pairs={{0,2},{2,0},{4,6},{6,4},{1,3},{3,1},{5,7},{7,5},{8,10},{10,8},{12,... | collective-permute-start | bytes 294920 | tf_op jit(solution)/shard_map/ppermute | solution.py:427
  56.5 6.1 %collective-permute-done.6.refs_1_ = bf16[64,768]{1,0:T(8,128)(2,1)S(1)} collective-permute-done((bf16[64,768]{1,0:T(8,128)(2,1)S(1)}, bf16[64,768]{1,0:T(8,128)(2,1)S(1)}, u32[]{:S(2)}, u32[]{:S(2)}) %collective-permute-start.6) | collective-permute-done | bytes 98336 | tf_op jit(solution)/shard_map/ppermute | solution.py:427
  62.6 0.0 collective-permute-done.7.refs_2_
  62.6 0.7 %collective-permute-done.8.refs_3_ = bf16[64,768]{1,0:T(8,128)(2,1)S(1)} collective-permute-done((bf16[64,768]{1,0:T(8,128)(2,1)S(1)}, bf16[64,768]{1,0:T(8,128)(2,1)S(1)}, u32[]{:S(2)}, u32[]{:S(2)}) %collective-permute-start.8) | collective-permute-done | bytes 98336 | tf_op jit(solution)/shard_map/ppermute | solution.py:427
  63.3 0.8 %assemble.1 = bf16[2,128,768]{2,1,0:T(8,128)(2,1)} custom-call(bf16[64,768]{1,0:T(8,128)(2,1)S(1)} %get-tuple-element.47.refs_0_, bf16[64,768]{1,0:T(8,128)(2,1)S(1)} %collective-permute-done.6.refs_1_, bf16[64,768]{1,0:T(8,128)(2,1)S(1)} %collective-permute-done.7.refs_2_, bf16[64,768]{1,0:T(8,128)(2,1)S(1)} %collective-permute-done.8.refs_3_), custom_call_target="tpu_custom_call" | custom-call | tf_op jit(solution)/shard_map/assemble/pallas_call | solution.py:429
  (1 shorter events, 0.0 us)
Async XLA Ops:
  0.9 13.3 %collective-permute-start.2 = (bf16[128,768]{1,0:T(8,128)(2,1)S(1)}, bf16[128,768]{1,0:T(8,128)(2,1)S(1)}, u32[]{:S(2)}, u32[]{:S(2)}) collective-permute-start(bf16[128,768]{1,0:T(8,128)(2,1)S(1)} %give.1.given_ref), channel_id=1, source_target_pairs={{0,8},{8,0},{1,9},{9,1},{2,10},{10,2},{3,11},{11,3},{4,12},{12,4},... | collective-permute-start | bytes 589832 | tf_op jit(solution)/shard_map/ppermute | solution.py:317
  11.7 4.6 %collective-permute-start = (bf16[128,768]{1,0:T(8,128)(2,1)S(1)}, bf16[128,768]{1,0:T(8,128)(2,1)S(1)}, u32[]{:S(2)}, u32[]{:S(2)}) collective-permute-start(bf16[128,768]{1,0:T(8,128)(2,1)S(1)} %get-tuple-element.33), channel_id=1, source_target_pairs={{0,1},{1,0},{2,3},{3,2},{4,5},{5,4},{6,7},{7,6},{8,9},{9,8},{10,11... | collective-permute-start | bytes 589832 | tf_op jit(solution)/shard_map/ppermute | solution.py:332
  12.7 5.5 %collective-permute-start.1 = (bf16[128,768]{1,0:T(8,128)(2,1)S(1)}, bf16[128,768]{1,0:T(8,128)(2,1)S(1)}, u32[]{:S(2)}, u32[]{:S(2)}) collective-permute-start(bf16[128,768]{1,0:T(8,128)(2,1)S(1)} %get-tuple-element.33), channel_id=1, source_target_pairs={{0,16},{1,17},{2,18},{3,19},{4,20},{5,21},{6,22},{7,23},{8,24},{9,... | collective-permute-start | bytes 589832 | tf_op jit(solution)/shard_map/ppermute | solution.py:332
  14.2 7.6 %collective-permute-start.3 = (bf16[128,768]{1,0:T(8,128)(2,1)S(1)}, bf16[128,768]{1,0:T(8,128)(2,1)S(1)}, u32[]{:S(2)}, u32[]{:S(2)}) collective-permute-start(bf16[128,768]{1,0:T(8,128)(2,1)S(1)} %collective-permute-done.2.other_ref), channel_id=1, source_target_pairs={{0,1},{1,0},{2,3},{3,2},{4,5},{5,4},{6,7},{7,6},{8,9},{9,8},{10,11... | collective-permute-start | bytes 589832 | tf_op jit(solution)/shard_map/ppermute | solution.py:332
  15.7 7.0 %collective-permute-start.4 = (bf16[128,768]{1,0:T(8,128)(2,1)S(1)}, bf16[128,768]{1,0:T(8,128)(2,1)S(1)}, u32[]{:S(2)}, u32[]{:S(2)}) collective-permute-start(bf16[128,768]{1,0:T(8,128)(2,1)S(1)} %collective-permute-done.2.other_ref), channel_id=1, source_target_pairs={{0,16},{1,17},{2,18},{3,19},{4,20},{5,21},{6,22},{7,23},{8,24},{9,... | collective-permute-start | bytes 589832 | tf_op jit(solution)/shard_map/ppermute | solution.py:332
  52.2 1.5 %collective-permute-start.5 = (bf16[128,768]{1,0:T(8,128)(2,1)S(1)}, bf16[128,768]{1,0:T(8,128)(2,1)S(1)}, u32[]{:S(2)}, u32[]{:S(2)}) collective-permute-start(bf16[128,768]{1,0:T(8,128)(2,1)S(1)} %get-tuple-element.46), channel_id=1, source_target_pairs={{0,1},{1,0},{2,3},{3,2},{4,5},{5,4},{6,7},{7,6},{8,9},{9,8},{10,11... | collective-permute-start | bytes 589832 | tf_op jit(solution)/shard_map/ppermute | solution.py:416
  53.8 8.8 %collective-permute-start.6 = (bf16[64,768]{1,0:T(8,128)(2,1)S(1)}, bf16[64,768]{1,0:T(8,128)(2,1)S(1)}, u32[]{:S(2)}, u32[]{:S(2)}) collective-permute-start(bf16[64,768]{1,0:T(8,128)(2,1)S(1)} %get-tuple-element.48), channel_id=1, source_target_pairs={{0,4},{2,6},{4,0},{6,2},{1,5},{3,7},{5,1},{7,3},{8,12},{10,14},{12... | collective-permute-start | bytes 294920 | tf_op jit(solution)/shard_map/ppermute | solution.py:427
  53.9 8.6 %collective-permute-start.7 = (bf16[64,768]{1,0:T(8,128)(2,1)S(1)}, bf16[64,768]{1,0:T(8,128)(2,1)S(1)}, u32[]{:S(2)}, u32[]{:S(2)}) collective-permute-start(bf16[64,768]{1,0:T(8,128)(2,1)S(1)} %get-tuple-element.49), channel_id=1, source_target_pairs={{0,6},{2,4},{4,2},{6,0},{1,7},{3,5},{5,3},{7,1},{8,14},{10,12},{12... | collective-permute-start | bytes 294920 | tf_op jit(solution)/shard_map/ppermute | solution.py:427
  55.0 8.3 %collective-permute-start.8 = (bf16[64,768]{1,0:T(8,128)(2,1)S(1)}, bf16[64,768]{1,0:T(8,128)(2,1)S(1)}, u32[]{:S(2)}, u32[]{:S(2)}) collective-permute-start(bf16[64,768]{1,0:T(8,128)(2,1)S(1)} %get-tuple-element.50), channel_id=1, source_target_pairs={{0,2},{2,0},{4,6},{6,4},{1,3},{3,1},{5,7},{7,5},{8,10},{10,8},{12,... | collective-permute-start | bytes 294920 | tf_op jit(solution)/shard_map/ppermute | solution.py:427
